TPU v7x, 32 devices: a whole 2x2x4 slice. The times are simulated.
32 devices in a mesh: ctx: 32 (over z, y, x, core).
Axes of the slice: x: 2, y: 2, z: 4, core: 2. Of those that a mesh axis runs over, the one named last changes fastest.
Arguments:
- queries: bfloat16 [4096, 16, 128], P('ctx'), may hold values from -6 to 6
- keys: bfloat16 [4096, 8, 128], P('ctx'), may hold values from -5 to 5
- values: bfloat16 [4096, 8, 128], P('ctx'), may hold values from -6 to 6
- d_out: bfloat16 [4096, 16, 128], P('ctx'), may hold values from -48 to 48
Outputs:
- grad_queries: bfloat16 [4096, 16, 128], P('ctx')
- grad_keys: bfloat16 [4096, 8, 128], P('ctx')
- grad_values: bfloat16 [4096, 8, 128], P('ctx')
All inputs are finite; a program needn't handle non-finite values.
Results may differ from a plain program's by a relative error of at most 0.012.
The roundings to bfloat16 on the way count: a program that leaves them out, or rounds other values in their place, can miss the bound.
Values may be sent and summed in bfloat16 or wider, within the bound.
No kernel may reach another device: no remote copies, remote signals or barrier semaphores. Data moves between devices by JAX's collectives and lax.ppermute only.
A program may use at most 64 MiB of HBM per device.

v0:
```python
import jax
import jax.numpy as jnp
from jax import lax
from jax.sharding import PartitionSpec as P

HEADS = 16
KV_HEADS = 8
HEAD_WIDTH = 128
WINDOW = 512
TOK_DEV = 128


score_scale = 168.0 ** (-0.5)


def from_behind(shard, axis, by):
    peers = lax.axis_size(axis)
    pairs = [(i, i + by) for i in range(peers) if 0 <= i + by < peers]
    return lax.ppermute(shard, axis, pairs)


def window_grads(queries, keys_win, values_win, d_out, row_start):
    row_count = queries.shape[0]
    key_span = keys_win.shape[0]
    group_size = HEADS // KV_HEADS
    grouped = queries.reshape(row_count, KV_HEADS, group_size, HEAD_WIDTH)
    gradient_per_group = d_out.reshape(row_count, KV_HEADS, group_size, HEAD_WIDTH)
    scores = (
        jnp.einsum("tgre,jge->grtj", grouped, keys_win, preferred_element_type=jnp.float32)
        * score_scale
    )
    query_pos = row_start + jnp.arange(row_count, dtype=jnp.int32)
    key_pos = row_start - WINDOW + jnp.arange(key_span, dtype=jnp.int32)
    distance = query_pos[:, None] - key_pos[None, :]
    visible = (distance >= 0) & (distance < WINDOW) & (key_pos[None, :] >= 0)
    scores = jnp.where(visible, scores, -jnp.inf)
    row_max = jnp.max(scores, axis=-1, keepdims=True)
    row_sum = jnp.sum(jnp.exp(scores - row_max), axis=-1, keepdims=True)
    log_total = row_max + jnp.log(row_sum)
    probability = jnp.exp(scores - log_total)
    probs_low = probability.astype(jnp.bfloat16)
    attention_result_rows = jnp.einsum(
        "grtj,jge->tgre", probs_low, values_win, preferred_element_type=jnp.float32
    ).astype(jnp.bfloat16)
    row_dot_product = jnp.einsum(
        "cqzj,cqzj->qzc",
        gradient_per_group,
        attention_result_rows,
        preferred_element_type=jnp.float32,
    )
    grad_probs = jnp.einsum(
        "tgre,jge->grtj", gradient_per_group, values_win, preferred_element_type=jnp.float32
    )
    grad_scores = (probability * (grad_probs - row_dot_product[..., None])).astype(jnp.bfloat16)
    query_gradient = (
        jnp.einsum("grtj,jge->tgre", grad_scores, keys_win, preferred_element_type=jnp.float32)
        * score_scale
    )
    grad_key = (
        jnp.einsum("grtj,tgre->jge", grad_scores, grouped, preferred_element_type=jnp.float32)
        * score_scale
    )
    grad_value = jnp.einsum(
        "grtj,tgre->jge", probs_low, gradient_per_group, preferred_element_type=jnp.float32
    )
    query_gradient = query_gradient.astype(jnp.bfloat16).reshape(row_count, HEADS, HEAD_WIDTH)
    return (query_gradient, grad_key, grad_value)


def body(queries, keys, values, d_out):
    halo_depth = WINDOW // TOK_DEV
    row_count = queries.shape[0]
    own_pair = jnp.stack([keys, values])
    preceding_shard = [from_behind(own_pair, "ctx", offset) for offset in range(halo_depth, 0, -1)]
    window_pair = jnp.concatenate(preceding_shard + [own_pair], axis=1)
    row_start = lax.axis_index("ctx") * row_count
    query_gradient, grad_key, grad_value = window_grads(
        queries, window_pair[0], window_pair[1], d_out, row_start
    )
    partials = jnp.stack([grad_key, grad_value]).reshape(
        2, halo_depth + 1, row_count, KV_HEADS, HEAD_WIDTH
    )
    summed = partials[:, halo_depth]
    for offset in range(1, halo_depth + 1):
        summed = summed + from_behind(
            partials[:, halo_depth - offset].astype(jnp.bfloat16), "ctx", -offset
        ).astype(jnp.float32)
    return (query_gradient, summed[0].astype(jnp.bfloat16), summed[1].astype(jnp.bfloat16))


def solution(mesh):
    placed = (
        P("ctx", None, None),
        P("ctx", None, None),
        P("ctx", None, None),
        P("ctx", None, None),
    )
    return jax.shard_map(
        body,
        mesh=mesh,
        in_specs=placed,
        out_specs=(P("ctx", None, None), P("ctx", None, None), P("ctx", None, None)),
        check_vma=False,
    )
```

profile of v0, /device:TPU:6, one launch (start us, length us, event | category | flops | bytes accessed | tf_op | source)
XLA Modules:
  0.0 130.2 jit_solution(8383918754982688878)
XLA Ops:
  0.6 0.0 copy-start
  0.6 1.2 copy_bitcast_fusion.1
  1.8 0.1 pad_maximum_fusion
  1.9 1.9 %collective-permute-start.3 = (bf16[2,128,8,128]{3,1,2,0:T(8,128)(2,1)S(1)}, bf16[2,128,8,128]{3,1,2,0:T(8,128)(2,1)S(1)}, u32[]{:S(2)}, u32[]{:S(2)}) collective-permute-start(bf16[2,128,8,128]{3,1,2,0:T(8,128)(2,1)S(1)} %pad_maximum_fusion), channel_id=1, source_target_pairs={{0,1},{1,2},{2,3},{3,4},{4,5},{5,6},{6,7},{7,8},{8,9},{9,10},{10,1... | collective-permute-start | bytes 1572872 | tf_op jit(solution)/shard_map/ppermute | solution.py:19
  3.8 3.4 %collective-permute-start.2 = (bf16[2,128,8,128]{3,1,2,0:T(8,128)(2,1)S(1)}, bf16[2,128,8,128]{3,1,2,0:T(8,128)(2,1)S(1)}, u32[]{:S(2)}, u32[]{:S(2)}) collective-permute-start(bf16[2,128,8,128]{3,1,2,0:T(8,128)(2,1)S(1)} %pad_maximum_fusion), channel_id=1, source_target_pairs={{0,2},{1,3},{2,4},{3,5},{4,6},{5,7},{6,8},{7,9},{8,10},{9,11},{10,... | collective-permute-start | bytes 1572872 | tf_op jit(solution)/shard_map/ppermute | solution.py:19
  7.2 4.3 %collective-permute-start.1 = (bf16[2,128,8,128]{3,1,2,0:T(8,128)(2,1)S(1)}, bf16[2,128,8,128]{3,1,2,0:T(8,128)(2,1)S(1)}, u32[]{:S(2)}, u32[]{:S(2)}) collective-permute-start(bf16[2,128,8,128]{3,1,2,0:T(8,128)(2,1)S(1)} %pad_maximum_fusion), channel_id=1, source_target_pairs={{0,3},{1,4},{2,5},{3,6},{4,7},{5,8},{6,9},{7,10},{8,11},{9,12},{10... | collective-permute-start | bytes 1572872 | tf_op jit(solution)/shard_map/ppermute | solution.py:19
  11.6 3.4 %collective-permute-start = (bf16[2,128,8,128]{3,1,2,0:T(8,128)(2,1)S(1)}, bf16[2,128,8,128]{3,1,2,0:T(8,128)(2,1)}, u32[]{:S(2)}, u32[]{:S(2)}) collective-permute-start(bf16[2,128,8,128]{3,1,2,0:T(8,128)(2,1)S(1)} %pad_maximum_fusion), channel_id=1, source_target_pairs={{0,4},{1,5},{2,6},{3,7},{4,8},{5,9},{6,10},{7,11},{8,12},{9,13},{1... | collective-permute-start | bytes 1572872 | tf_op jit(solution)/shard_map/ppermute | solution.py:19
  15.0 0.2 fusion.18
  15.3 37.8 %collective-permute-done = bf16[2,128,8,128]{3,1,2,0:T(8,128)(2,1)} collective-permute-done((bf16[2,128,8,128]{3,1,2,0:T(8,128)(2,1)S(1)}, bf16[2,128,8,128]{3,1,2,0:T(8,128)(2,1)}, u32[]{:S(2)}, u32[]{:S(2)}) %collective-permute-start) | collective-permute-done | bytes 524320 | tf_op jit(solution)/shard_map/ppermute | solution.py:19
  53.0 1.1 constant_dynamic-update-slice_fusion.4
  54.1 0.0 collective-permute-done.1
  54.1 0.1 constant_dynamic-update-slice_fusion.3
  54.2 0.0 collective-permute-done.2
  54.2 0.1 constant_dynamic-update-slice_fusion.2
  54.3 0.0 collective-permute-done.3
  54.3 0.1 constant_dynamic-update-slice_fusion.1
  54.4 0.1 constant_dynamic-update-slice_fusion
  54.5 0.9 fusion.3
  55.4 1.1 exponential_reduce_fusion
  56.5 1.2 copy-done.2
  57.7 1.4 %convolution_convert_fusion = bf16[8,128,2,128]{3,1,2,0:T(8,128)(2,1)S(1)} fusion(bf16[2,640,8,128]{3,1,2,0:T(8,128)(2,1)S(1)} %constant_dynamic-update-slice_fusion, f32[8,640,128,2]{2,1,3,0:T(8,128)S(1)} %get-tuple-element.13, f32[8,2,128]{2,1,0:T(2,128)S(1)} %bitcast.108, pred[128,640]{0,1:T(8,128)(4,1)S(1)} %fusion.18), kind=kOutput, calls=%fused_computation.15 | convolution fusion | flops 341049344 | bytes 7168000 | tf_op jit(solution)/shard_map/grtj,jge->tgre/dot_general | solution.py:42
  59.1 0.0 copy-start.5
  59.1 0.5 fusion.11
  59.7 1.6 %copy.26 = f32[8,2,128,128]{3,1,0,2:T(2,128)S(1)} copy(f32[8,2,128,128]{2,1,3,0:T(2,128)S(1)} %fusion.11) | data formatting | bytes 2097152
  61.3 1.2 multiply_reduce_fusion
  62.5 0.0 slice-start
  62.5 0.2 copy.27
  62.7 3.9 %fusion.12 = f32[8,640,128,1]{2,1,3,0:T(8,128)S(1)} fusion(bf16[128,8,2,128]{3,2,1,0:T(2,128)(2,1)S(1)} %bitcast.104, f32[8,640,128,2]{2,1,3,0:T(8,128)} %copy-done.2, f32[8,2,128]{2,1,0:T(2,128)S(1)} %bitcast.109, pred[128,640]{0,1:T(8,128)(4,1)S(1)} %fusion.18), kind=kOutput, calls=%fused_computation.33 | convolution fusion | flops 340787200 | bytes 8478720 | tf_op jit(solution)/shard_map/grtj,tgre->jge/dot_general | solution.py:63
  66.6 0.8 copy-done.4
  67.4 1.7 %fusion.1 = bf16[8,2,128,640]{2,3,1,0:T(8,128)(2,1)S(1)} fusion(f32[8,640,128,2]{2,1,3,0:T(8,128)S(1)} %bitcast.100, f32[8,2,128]{2,1,0:T(2,128)S(1)} %copy.27, f32[8,2,128]{2,1,0:T(2,128)S(1)} %bitcast.110, pred[128,640]{0,1:T(8,128)(4,1)S(1)} %fusion.18, bf16[2,640,8,128]{3,1,2,0:T(8,128)(2,1)S(1)} %copy-done.4, bf16[128,8,2,128]{3,2,1,0:T(2,128)(2,1)S(1)} %bitcast.105), kind=kOutput, calls=%fused_computation.2 | convolution fusion | flops 343408640 | bytes 9797632 | tf_op jit(solution)/shard_map/tgre,jge->grtj/dot_general | solution.py:51
  69.1 0.9 bitcast_multiply_fusion
  70.0 1.5 %copy_dynamic-update-slice_fusion.1 = f32[2,5,128,8,128]{4,3,2,0,1:T(8,128)S(1)} fusion(f32[1,5,128,8,128]{4,2,1,3,0:T(8,128)S(1)} %bitcast.98), kind=kLoop, calls=%fused_computation.10 | loop fusion | bytes 5242880
  71.5 1.5 %copy_dynamic-update-slice_fusion = f32[2,5,128,8,128]{4,3,2,0,1:T(8,128)S(1)} fusion(f32[2,5,128,8,128]{4,3,2,0,1:T(8,128)S(1)} %copy_dynamic-update-slice_fusion.1, f32[1,5,128,8,128]{4,2,1,3,0:T(8,128)S(1)} %bitcast.101), kind=kLoop, calls=%fused_computation.9 | loop fusion | bytes 5242880 | tf_op jit(solution)/shard_map/stack | solution.py:80
  73.0 0.5 convert.10
  73.5 1.8 %copy-done.1 = f32[2,5,128,8,128]{4,3,2,0,1:T(8,128)} copy-done((f32[2,5,128,8,128]{4,3,2,0,1:T(8,128)}, f32[2,5,128,8,128]{4,3,2,0,1:T(8,128)S(1)}, u32[]{:S(2)}) %copy-start.1) | copy-done | bytes 5242904
  75.3 1.4 %slice_bitcast_fusion.10 = (bf16[2,128,8,128]{3,2,1,0:T(8,128)(2,1)}, bf16[2,128,8,128]{3,2,1,0:T(8,128)(2,1)}, bf16[2,128,8,128]{3,2,1,0:T(8,128)(2,1)}, bf16[2,128,8,128]{3,2,1,0:T(8,128)(2,1)}) fusion(bf16[2,5,128,8,128]{4,3,2,0,1:T(8,128)(2,1)S(1)} %convert.10), kind=kLoop, calls=%fused_computation.29 | loop fusion | bytes 4194304 | tf_op jit(solution)/shard_map/convert_element_type | solution.py:86
  76.7 1.9 %collective-permute-start.4 = (bf16[2,128,8,128]{3,2,1,0:T(8,128)(2,1)}, bf16[2,128,8,128]{3,2,1,0:T(8,128)(2,1)S(1)}, u32[]{:S(2)}, u32[]{:S(2)}) collective-permute-start(bf16[2,128,8,128]{3,2,1,0:T(8,128)(2,1)} %get-tuple-element.6), channel_id=1, source_target_pairs={{1,0},{2,1},{3,2},{4,3},{5,4},{6,5},{7,6},{8,7},{9,8},{10,9},{11,1... | collective-permute-start | bytes 1572872 | tf_op jit(solution)/shard_map/ppermute | solution.py:19
  78.6 1.9 %collective-permute-start.7 = (bf16[2,128,8,128]{3,2,1,0:T(8,128)(2,1)}, bf16[2,128,8,128]{3,2,1,0:T(8,128)(2,1)S(1)}, u32[]{:S(2)}, u32[]{:S(2)}) collective-permute-start(bf16[2,128,8,128]{3,2,1,0:T(8,128)(2,1)} %get-tuple-element.7), channel_id=1, source_target_pairs={{4,0},{5,1},{6,2},{7,3},{8,4},{9,5},{10,6},{11,7},{12,8},{13,9},{1... | collective-permute-start | bytes 1572872 | tf_op jit(solution)/shard_map/ppermute | solution.py:19
  80.5 1.9 %collective-permute-start.6 = (bf16[2,128,8,128]{3,2,1,0:T(8,128)(2,1)}, bf16[2,128,8,128]{3,2,1,0:T(8,128)(2,1)S(1)}, u32[]{:S(2)}, u32[]{:S(2)}) collective-permute-start(bf16[2,128,8,128]{3,2,1,0:T(8,128)(2,1)} %get-tuple-element.8), channel_id=1, source_target_pairs={{3,0},{4,1},{5,2},{6,3},{7,4},{8,5},{9,6},{10,7},{11,8},{12,9},{13... | collective-permute-start | bytes 1572872 | tf_op jit(solution)/shard_map/ppermute | solution.py:19
  82.4 1.9 %collective-permute-start.5 = (bf16[2,128,8,128]{3,2,1,0:T(8,128)(2,1)}, bf16[2,128,8,128]{3,2,1,0:T(8,128)(2,1)S(1)}, u32[]{:S(2)}, u32[]{:S(2)}) collective-permute-start(bf16[2,128,8,128]{3,2,1,0:T(8,128)(2,1)} %get-tuple-element.9), channel_id=1, source_target_pairs={{2,0},{3,1},{4,2},{5,3},{6,4},{7,5},{8,6},{9,7},{10,8},{11,9},{12,... | collective-permute-start | bytes 1572872 | tf_op jit(solution)/shard_map/ppermute | solution.py:19
  84.4 0.7 fusion.4
  85.0 1.2 copy.17
  86.2 0.0 collective-permute-done.4
  86.2 19.0 %collective-permute-done.7 = bf16[2,128,8,128]{3,2,1,0:T(8,128)(2,1)S(1)} collective-permute-done((bf16[2,128,8,128]{3,2,1,0:T(8,128)(2,1)}, bf16[2,128,8,128]{3,2,1,0:T(8,128)(2,1)S(1)}, u32[]{:S(2)}, u32[]{:S(2)}) %collective-permute-start.7) | collective-permute-done | bytes 524320 | tf_op jit(solution)/shard_map/ppermute | solution.py:19
  105.3 5.7 %collective-permute-done.6 = bf16[2,128,8,128]{3,2,1,0:T(8,128)(2,1)S(1)} collective-permute-done((bf16[2,128,8,128]{3,2,1,0:T(8,128)(2,1)}, bf16[2,128,8,128]{3,2,1,0:T(8,128)(2,1)S(1)}, u32[]{:S(2)}, u32[]{:S(2)}) %collective-permute-start.6) | collective-permute-done | bytes 524320 | tf_op jit(solution)/shard_map/ppermute | solution.py:19
  111.0 16.9 %collective-permute-done.5 = bf16[2,128,8,128]{3,2,1,0:T(8,128)(2,1)S(1)} collective-permute-done((bf16[2,128,8,128]{3,2,1,0:T(8,128)(2,1)}, bf16[2,128,8,128]{3,2,1,0:T(8,128)(2,1)S(1)}, u32[]{:S(2)}, u32[]{:S(2)}) %collective-permute-start.5) | collective-permute-done | bytes 524320 | tf_op jit(solution)/shard_map/ppermute | solution.py:19
  127.8 1.5 %fusion.10 = bf16[2,128,8,128]{3,2,1,0:T(8,128)(2,1)S(1)} fusion(f32[2,5,128,8,128]{4,3,2,0,1:T(8,128)} %copy-done.1, bf16[2,128,8,128]{3,2,1,0:T(8,128)(2,1)S(1)} %collective-permute-done.7, bf16[2,128,8,128]{3,2,1,0:T(8,128)(2,1)S(1)} %collective-permute-done.6, bf16[2,128,8,128]{3,2,1,0:T(8,128)(2,1)S(1)} %collective-permute-done.5, ...), kind=kLoop, calls=%fused_computation.22 | loop fusion | flops 2359296 | bytes 3670016 | tf_op jit(solution)/shard_map/convert.1
  129.4 0.8 slice_bitcast_fusion.11
  (15 shorter events, 0.0 us)
Async XLA Ops:
  0.6 53.8 %copy-start = (bf16[128,16,128]{2,1,0:T(8,128)(2,1)S(1)}, bf16[128,16,128]{2,1,0:T(8,128)(2,1)}, u32[]{:S(2)}) copy-start(bf16[128,16,128]{2,1,0:T(8,128)(2,1)} %param.4) | copy-start | bytes 1572868
  1.9 52.4 %collective-permute-start.3 = (bf16[2,128,8,128]{3,1,2,0:T(8,128)(2,1)S(1)}, bf16[2,128,8,128]{3,1,2,0:T(8,128)(2,1)S(1)}, u32[]{:S(2)}, u32[]{:S(2)}) collective-permute-start(bf16[2,128,8,128]{3,1,2,0:T(8,128)(2,1)S(1)} %pad_maximum_fusion), channel_id=1, source_target_pairs={{0,1},{1,2},{2,3},{3,4},{4,5},{5,6},{6,7},{7,8},{8,9},{9,10},{10,1... | collective-permute-start | bytes 1572872 | tf_op jit(solution)/shard_map/ppermute | solution.py:19
  3.8 50.4 %collective-permute-start.2 = (bf16[2,128,8,128]{3,1,2,0:T(8,128)(2,1)S(1)}, bf16[2,128,8,128]{3,1,2,0:T(8,128)(2,1)S(1)}, u32[]{:S(2)}, u32[]{:S(2)}) collective-permute-start(bf16[2,128,8,128]{3,1,2,0:T(8,128)(2,1)S(1)} %pad_maximum_fusion), channel_id=1, source_target_pairs={{0,2},{1,3},{2,4},{3,5},{4,6},{5,7},{6,8},{7,9},{8,10},{9,11},{10,... | collective-permute-start | bytes 1572872 | tf_op jit(solution)/shard_map/ppermute | solution.py:19
  7.2 46.9 %collective-permute-start.1 = (bf16[2,128,8,128]{3,1,2,0:T(8,128)(2,1)S(1)}, bf16[2,128,8,128]{3,1,2,0:T(8,128)(2,1)S(1)}, u32[]{:S(2)}, u32[]{:S(2)}) collective-permute-start(bf16[2,128,8,128]{3,1,2,0:T(8,128)(2,1)S(1)} %pad_maximum_fusion), channel_id=1, source_target_pairs={{0,3},{1,4},{2,5},{3,6},{4,7},{5,8},{6,9},{7,10},{8,11},{9,12},{10... | collective-permute-start | bytes 1572872 | tf_op jit(solution)/shard_map/ppermute | solution.py:19
  11.6 41.5 %collective-permute-start = (bf16[2,128,8,128]{3,1,2,0:T(8,128)(2,1)S(1)}, bf16[2,128,8,128]{3,1,2,0:T(8,128)(2,1)}, u32[]{:S(2)}, u32[]{:S(2)}) collective-permute-start(bf16[2,128,8,128]{3,1,2,0:T(8,128)(2,1)S(1)} %pad_maximum_fusion), channel_id=1, source_target_pairs={{0,4},{1,5},{2,6},{3,7},{4,8},{5,9},{6,10},{7,11},{8,12},{9,13},{1... | collective-permute-start | bytes 1572872 | tf_op jit(solution)/shard_map/ppermute | solution.py:19
  54.5 2.0 %copy-start.3 = (bf16[2,640,8,128]{3,1,2,0:T(8,128)(2,1)}, bf16[2,640,8,128]{3,1,2,0:T(8,128)(2,1)S(1)}, u32[]{:S(2)}) copy-start(bf16[2,640,8,128]{3,1,2,0:T(8,128)(2,1)S(1)} %constant_dynamic-update-slice_fusion) | copy-start | bytes 7864324
  55.4 2.3 %copy-start.2 = (f32[8,640,128,2]{2,1,3,0:T(8,128)}, f32[8,640,128,2]{2,1,3,0:T(8,128)S(1)}, u32[]{:S(2)}) copy-start(f32[8,640,128,2]{2,1,3,0:T(8,128)S(1)} %get-tuple-element.13) | copy-start | bytes 15728644
  59.1 2.2 %copy-start.5 = (bf16[128,16,128]{2,1,0:T(8,128)(2,1)S(1)}, bf16[128,16,128]{2,1,0:T(8,128)(2,1)}, u32[]{:S(2)}) copy-start(bf16[128,16,128]{2,1,0:T(8,128)(2,1)} %param.7) | copy-start | bytes 1572868
  62.5 4.1 %slice-start = ((s8[5242880]{0:T(1024)(128)(4,1)}), s8[1048576]{0:T(1024)(128)(4,1)S(1)}, s32[]{:S(2)}) async-start(s8[5242880]{0:T(1024)(128)(4,1)} %bitcast.99), calls=%async_computation | async-start | bytes 2097152
  62.7 3.9 %slice-start.1 = ((s8[5242880]{0:T(1024)(128)(4,1)}), s8[4194304]{0:T(1024)(128)(4,1)S(1)}, s32[]{:S(2)}) async-start(s8[5242880]{0:T(1024)(128)(4,1)} %bitcast.99), calls=%async_computation.1 | async-start | bytes 8388608
  62.7 4.7 %copy-start.4 = (bf16[2,640,8,128]{3,1,2,0:T(8,128)(2,1)S(1)}, bf16[2,640,8,128]{3,1,2,0:T(8,128)(2,1)}, u32[]{:S(2)}) copy-start(bf16[2,640,8,128]{3,1,2,0:T(8,128)(2,1)} %copy-done.3) | copy-start | bytes 7864324
  73.0 2.3 %copy-start.1 = (f32[2,5,128,8,128]{4,3,2,0,1:T(8,128)}, f32[2,5,128,8,128]{4,3,2,0,1:T(8,128)S(1)}, u32[]{:S(2)}) copy-start(f32[2,5,128,8,128]{4,3,2,0,1:T(8,128)S(1)} %copy_dynamic-update-slice_fusion) | copy-start | bytes 15728644
  76.7 9.6 %collective-permute-start.4 = (bf16[2,128,8,128]{3,2,1,0:T(8,128)(2,1)}, bf16[2,128,8,128]{3,2,1,0:T(8,128)(2,1)S(1)}, u32[]{:S(2)}, u32[]{:S(2)}) collective-permute-start(bf16[2,128,8,128]{3,2,1,0:T(8,128)(2,1)} %get-tuple-element.6), channel_id=1, source_target_pairs={{1,0},{2,1},{3,2},{4,3},{5,4},{6,5},{7,6},{8,7},{9,8},{10,9},{11,1... | collective-permute-start | bytes 1572872 | tf_op jit(solution)/shard_map/ppermute | solution.py:19
  78.6 26.7 %collective-permute-start.7 = (bf16[2,128,8,128]{3,2,1,0:T(8,128)(2,1)}, bf16[2,128,8,128]{3,2,1,0:T(8,128)(2,1)S(1)}, u32[]{:S(2)}, u32[]{:S(2)}) collective-permute-start(bf16[2,128,8,128]{3,2,1,0:T(8,128)(2,1)} %get-tuple-element.7), channel_id=1, source_target_pairs={{4,0},{5,1},{6,2},{7,3},{8,4},{9,5},{10,6},{11,7},{12,8},{13,9},{1... | collective-permute-start | bytes 1572872 | tf_op jit(solution)/shard_map/ppermute | solution.py:19
  80.5 30.5 %collective-permute-start.6 = (bf16[2,128,8,128]{3,2,1,0:T(8,128)(2,1)}, bf16[2,128,8,128]{3,2,1,0:T(8,128)(2,1)S(1)}, u32[]{:S(2)}, u32[]{:S(2)}) collective-permute-start(bf16[2,128,8,128]{3,2,1,0:T(8,128)(2,1)} %get-tuple-element.8), channel_id=1, source_target_pairs={{3,0},{4,1},{5,2},{6,3},{7,4},{8,5},{9,6},{10,7},{11,8},{12,9},{13... | collective-permute-start | bytes 1572872 | tf_op jit(solution)/shard_map/ppermute | solution.py:19
  82.4 45.4 %collective-permute-start.5 = (bf16[2,128,8,128]{3,2,1,0:T(8,128)(2,1)}, bf16[2,128,8,128]{3,2,1,0:T(8,128)(2,1)S(1)}, u32[]{:S(2)}, u32[]{:S(2)}) collective-permute-start(bf16[2,128,8,128]{3,2,1,0:T(8,128)(2,1)} %get-tuple-element.9), channel_id=1, source_target_pairs={{2,0},{3,1},{4,2},{5,3},{6,4},{7,5},{8,6},{9,7},{10,8},{11,9},{12,... | collective-permute-start | bytes 1572872 | tf_op jit(solution)/shard_map/ppermute | solution.py:19
where the time goes:
time: 131 us; the launch traced here: 130 us
  waiting for transfers between devices  79.4 us (61%)
  starting transfers between devices  20.7 us (16%)
  local copies, waits for them, and re-layouts  14.5 us (11%)
  matrix products  9.44 us (7%)
  other arithmetic  5.16 us (4%)
    ppermute x8, waiting for transfers between devices, from_behind(): return lax.ppermute(shard, axis, pairs)  79.4 us
    ppermute x8, starting transfers between devices, from_behind(): return lax.ppermute(shard, axis, pairs)  20.7 us
    unnamed x23, local copies, waits for them, and re-layouts  9.41 us
    dot_general x1, matrix products, window_grads(): jnp.einsum('grtj,tgre->jge', probs_low, gradient_per_group, preferred_ele...  3.89 us
  transfers between devices with their start and end apart: 8, of which 4 were waited for; matrix products, arithmetic and copies ran while one was open for 3% of the time, Pallas kernels for 0%

commit v1 on v0

v1 whole, which is shorter than its diff:
```python
import functools
import math

import jax
import jax.numpy as jnp
from jax import lax
from jax.experimental import pallas as pl
from jax.experimental.pallas import tpu as pltpu
from jax.sharding import PartitionSpec as P

WINDOW = 512
SCORE_SCALE = 168.0 ** -0.5
LOG2E = math.log2(math.e)
NEG = -1e30
VMEM_LIMIT = 48 * 1024 * 1024

NT = (((1,), (1,)), ((), ()))
NN = (((1,), (0,)), ((), ()))
TN = (((0,), (0,)), ((), ()))


def dot(a, b, dims):
    return lax.dot_general(a, b, dims, preferred_element_type=jnp.float32)


def swap(a, by):
    n = lax.axis_size("ctx")
    return lax.ppermute(a, "ctx", [(i, i ^ by) for i in range(n)])


def shift(a, by):
    n = lax.axis_size("ctx")
    return lax.ppermute(a, "ctx", [(i, i + by) for i in range(n) if 0 <= i + by < n])


def split_heads_kernel(place, a_ref, b_ref, keep_ref, send_ref, wide):
    tok, heads, width = a_ref.shape
    half = heads // 2
    x = place[0]
    for s, ref in enumerate((a_ref, b_ref)):
        wide[s] = ref[...].astype(jnp.float32).reshape(tok * heads, width)
        for j in range(half):
            low = wide[s, pl.ds(j, tok, stride=heads), :]
            high = wide[s, pl.ds(half + j, tok, stride=heads), :]
            keep_ref[s, j] = jnp.where(x == 0, low, high).astype(jnp.bfloat16)
            send_ref[s, j] = jnp.where(x == 0, high, low).astype(jnp.bfloat16)


def split_heads(place, a, b):
    tok, heads, width = a.shape
    out = jax.ShapeDtypeStruct((2, heads // 2, tok, width), jnp.bfloat16)
    return pl.pallas_call(
        split_heads_kernel,
        out_shape=(out, out),
        in_specs=[pl.BlockSpec(memory_space=pltpu.SMEM)] + [pl.BlockSpec(memory_space=pltpu.VMEM)] * 2,
        out_specs=(pl.BlockSpec(memory_space=pltpu.VMEM),) * 2,
        scratch_shapes=[pltpu.VMEM((2, tok * heads, width), jnp.float32)],
        compiler_params=pltpu.CompilerParams(vmem_limit_bytes=VMEM_LIMIT),
        name="split_heads",
    )(place, a, b)


def grads_kernel(
    place, keep_q, sent_q, ko, xo, mko, mxo, k1, k2, mk1, mk2,
    dq_keep, dq_send, prev_here, prev_mate, own_here, own_mate,
    kv, dkv,
):
    _, _, tok, width = ko.shape
    x, c, first = place[0], place[1], place[2]
    heads = keep_q.shape[1]
    mine, other = 2 * x + c, 2 * (1 - x) + c
    mate_mine, mate_other = 2 * x + 1 - c, 2 * (1 - x) + 1 - c
    blocks = WINDOW // tok

    def rows(slot):
        return pl.ds(pl.multiple_of(slot * tok, tok), tok)

    for ref, slot in (
        (k1, mine), (k2, other), (mk1, mate_mine), (mk2, mate_other),
        (ko, blocks + mine), (xo, blocks + other), (mko, blocks + mate_mine), (mxo, blocks + mate_other),
    ):
        for s in range(2):
            kv[s, rows(slot), :] = ref[s, 0]
    dkv[...] = jnp.zeros_like(dkv)

    query = lax.broadcasted_iota(jnp.int32, (heads * tok, tok), 0) % tok
    key = lax.broadcasted_iota(jnp.int32, (heads * tok, tok), 1)
    before, upto = key > query, key <= query

    for q_ref, block, dq_ref in ((keep_q, mine, dq_keep), (sent_q, other, dq_send)):
        window = pl.ds(pl.multiple_of(block * tok, tok), WINDOW + tok)
        q = q_ref[0].reshape(heads * tok, width)
        do = q_ref[1].reshape(heads * tok, width)
        k = kv[0, window, :]
        v = kv[1, window, :]
        scores = dot(q, k, NT) * (SCORE_SCALE * LOG2E)
        parts = []
        for t in range(blocks + 1):
            part = scores[:, t * tok : (t + 1) * tok]
            if t < blocks:
                hidden = jnp.logical_and(first == 1, block + t < blocks)
                part = part + jnp.where(hidden, NEG, 0.0)
            if t == 0:
                part = jnp.where(before, part, NEG)
            if t == blocks:
                part = jnp.where(upto, part, NEG)
            parts.append(part)
        top = jnp.max(functools.reduce(jnp.maximum, parts), axis=1, keepdims=True)
        parts = [jnp.exp2(part - top) for part in parts]
        total = jnp.sum(sum(parts[1:], parts[0]), axis=1, keepdims=True)
        inverse = 1.0 / total
        prob = jnp.concatenate([part * inverse for part in parts], axis=1)
        low = prob.astype(jnp.bfloat16)
        attended = dot(low, v, NN).astype(jnp.bfloat16)
        row_dot = jnp.sum(do.astype(jnp.float32) * attended.astype(jnp.float32), axis=1, keepdims=True)
        ds = (prob * (dot(do, v, NT) - row_dot)).astype(jnp.bfloat16)
        dq = dot(ds, k, NN) * SCORE_SCALE
        dq_ref[...] = dq.astype(jnp.bfloat16).reshape(heads, tok, width)
        dkv[0, window, :] += dot(ds, q, TN)
        dkv[1, window, :] += dot(low, do, TN)

    for s, scale in enumerate((SCORE_SCALE, 1.0)):
        for ref, base, pair in (
            (prev_here, 0, (mine, other)),
            (prev_mate, 0, (mate_mine, mate_other)),
            (own_here, blocks, (mine, other)),
            (own_mate, blocks, (mate_mine, mate_other)),
        ):
            for k_, slot in enumerate(pair):
                ref[k_, s, 0] = (dkv[s, rows(base + slot), :] * scale).astype(ref.dtype)


def grads(place, keep_q, sent_q, *kvs):
    _, groups, tok, width = kvs[0].shape
    q_heads = keep_q.shape[1]
    per = q_heads // groups
    bf, f32 = jnp.bfloat16, jnp.float32
    q_spec = pl.BlockSpec((2, per, tok, width), lambda g: (0, g, 0, 0))
    kv_spec = pl.BlockSpec((2, 1, tok, width), lambda g: (0, g, 0, 0))
    dq_spec = pl.BlockSpec((per, tok, width), lambda g: (g, 0, 0))
    dkv_spec = pl.BlockSpec((2, 2, 1, tok, width), lambda g: (0, 0, g, 0, 0))
    dq_shape = jax.ShapeDtypeStruct((q_heads, tok, width), bf)
    dkv_shape = functools.partial(jax.ShapeDtypeStruct, (2, 2, groups, tok, width))
    return pl.pallas_call(
        grads_kernel,
        grid=(groups,),
        out_shape=(dq_shape, dq_shape, dkv_shape(f32), dkv_shape(bf), dkv_shape(f32), dkv_shape(bf)),
        in_specs=[pl.BlockSpec(memory_space=pltpu.SMEM)] + [q_spec] * 2 + [kv_spec] * 8,
        out_specs=(dq_spec, dq_spec) + (dkv_spec,) * 4,
        scratch_shapes=[
            pltpu.VMEM((2, 2 * WINDOW, width), bf),
            pltpu.VMEM((2, 2 * WINDOW, width), f32),
        ],
        compiler_params=pltpu.CompilerParams(vmem_limit_bytes=VMEM_LIMIT),
        name="window_grads",
    )(place, keep_q, sent_q, *kvs)


def join_heads_kernel(place, keep_ref, sent_ref, out_ref, wide):
    tok, heads, width = out_ref.shape
    half = heads // 2
    x = place[0]
    for j in range(half):
        keep = keep_ref[j].astype(jnp.float32)
        sent = sent_ref[j].astype(jnp.float32)
        wide[pl.ds(j, tok, stride=heads), :] = jnp.where(x == 0, keep, sent)
        wide[pl.ds(half + j, tok, stride=heads), :] = jnp.where(x == 0, sent, keep)
    out_ref[...] = wide[...].reshape(tok, heads, width).astype(out_ref.dtype)


def join_heads(place, keep, sent):
    half, tok, width = keep.shape
    return pl.pallas_call(
        join_heads_kernel,
        out_shape=jax.ShapeDtypeStruct((tok, 2 * half, width), jnp.bfloat16),
        in_specs=[pl.BlockSpec(memory_space=pltpu.SMEM)] + [pl.BlockSpec(memory_space=pltpu.VMEM)] * 2,
        out_specs=pl.BlockSpec(memory_space=pltpu.VMEM),
        scratch_shapes=[pltpu.VMEM((tok * 2 * half, width), jnp.float32)],
        compiler_params=pltpu.CompilerParams(vmem_limit_bytes=VMEM_LIMIT),
        name="join_heads",
    )(place, keep, sent)


def body(queries, keys, values, d_out):
    tok = queries.shape[0]
    quad = WINDOW // tok
    assert quad == 4 and lax.axis_size("ctx") % quad == 0
    me = lax.axis_index("ctx")
    x, c, first = (me // 2) % 2, me % 2, (me < quad).astype(jnp.int32)
    place = jnp.stack([x, c, first]).astype(jnp.int32)
    bf, f32 = jnp.bfloat16, jnp.float32

    kv_keep, kv_send = split_heads(place, keys, values)
    kv_x = swap(kv_send, 2)
    kv_1 = shift(kv_keep, quad)
    q_keep, q_send = split_heads(place, queries, d_out)
    q_x = swap(q_send, 2)
    kv_2 = shift(kv_x, quad)
    mates = [swap(a, 1) for a in (kv_keep, kv_x, kv_1, kv_2)]

    dq_keep, dq_send, prev_here, prev_mate, own_here, own_mate = grads(
        place, q_keep, q_x, kv_keep, kv_x, mates[0], mates[1], kv_1, kv_2, mates[2], mates[3]
    )
    prev_sum = (prev_here + swap(prev_mate, 1).astype(f32)).astype(bf)
    back_2 = shift(prev_sum[1], -quad)
    back_1 = shift(prev_sum[0], -quad)
    own_sum = own_here + swap(own_mate, 1).astype(f32)
    other = (own_sum[1] + back_2.astype(f32)).astype(bf)
    dkv_x = swap(other, 2)
    dq_x = swap(dq_send, 2)
    mine = (own_sum[0] + back_1.astype(f32)).astype(bf)
    return (
        join_heads(place, dq_keep, dq_x),
        join_heads(place, mine[0], dkv_x[0]),
        join_heads(place, mine[1], dkv_x[1]),
    )


def solution(mesh):
    spec = P("ctx", None, None)
    return jax.shard_map(
        body,
        mesh=mesh,
        in_specs=(spec,) * 4,
        out_specs=(spec,) * 3,
        check_vma=False,
    )
```

time: 131 us -> 65.5 us (0.50)
  the two profiles are of different devices: /device:TPU:6 before, /device:TPU:0 now
where the time goes in v1:
time: 65.5 us; the launch traced here: 65.2 us
  waiting for transfers between devices  27.3 us (42%)
  Pallas kernels  18 us (27%)
  starting transfers between devices  15.7 us (24%)
  local copies, waits for them, and re-layouts  3.06 us (5%)
  between operations  0.82 us (1%)
    ppermute x4, waiting for transfers between devices, shift(): lax.ppermute(a, 'ctx', [(i, i + by) for i in range(n) if 0 <= i + by < n])  17.1 us
    pallas_call x1, Pallas kernels, grads(): pl.pallas_call(grads_kernel, grid=(groups,), out_shape=(dq_shape, dq_shap...  11.2 us
    ppermute x10, waiting for transfers between devices, swap(): return lax.ppermute(a, 'ctx', [(i, i ^ by) for i in range(n)])  10.2 us
    ppermute x4, starting transfers between devices, shift(): lax.ppermute(a, 'ctx', [(i, i + by) for i in range(n) if 0 <= i + by < n])  9.77 us
    ppermute x10, starting transfers between devices, swap(): return lax.ppermute(a, 'ctx', [(i, i ^ by) for i in range(n)])  5.9 us
    pallas_call x3, Pallas kernels, join_heads(): pl.pallas_call(join_heads_kernel, out_shape=jax.ShapeDtypeStruct((tok, 2...  4.73 us
    unnamed x10, local copies, waits for them, and re-layouts  2.98 us
    pallas_call x2, Pallas kernels, split_heads(): pl.pallas_call(split_heads_kernel, out_shape=(out, out), in_specs=[pl.Blo...  2.01 us
  transfers between devices with their start and end apart: 14, of which 6 were waited for; matrix products, arithmetic and copies ran while one was open for 1% of the time, Pallas kernels for 5%

profile of v1, /device:TPU:0, one launch (start us, length us, event | category | flops | bytes accessed | tf_op | source)
XLA Modules:
  0.0 65.2 jit_solution(9191003490205332592)
XLA Ops:
  0.6 0.0 copy-start
  0.7 0.1 pad_add_fusion.place
  0.8 0.0 copy-start.2
  0.8 1.0 %copy-done.2 = bf16[128,8,128]{2,1,0:T(8,128)(2,1)S(1)} copy-done((bf16[128,8,128]{2,1,0:T(8,128)(2,1)S(1)}, bf16[128,8,128]{2,1,0:T(8,128)(2,1)}, u32[]{:S(2)}) %copy-start.2) | copy-done | bytes 262168
  1.7 0.0 copy-start.3
  1.7 0.9 %copy-done.3 = bf16[128,8,128]{2,1,0:T(8,128)(2,1)S(1)} copy-done((bf16[128,8,128]{2,1,0:T(8,128)(2,1)S(1)}, bf16[128,8,128]{2,1,0:T(8,128)(2,1)}, u32[]{:S(2)}) %copy-start.3) | copy-done | bytes 262168
  2.7 0.8 %split_heads.3 = (bf16[2,4,128,128]{3,2,1,0:T(8,128)(2,1)S(1)}, bf16[2,4,128,128]{3,2,1,0:T(8,128)(2,1)S(1)}) custom-call(s32[3]{0:T(128)S(1)} %pad_add_fusion.place, bf16[128,8,128]{2,1,0:T(8,128)(2,1)S(1)} %copy-done.2, bf16[128,8,128]{2,1,0:T(8,128)(2,1)S(1)} %copy-done.3), custom_call_target="tpu_custom_call" | custom-call | tf_op jit(solution)/shard_map/split_heads/pallas_call | solution.py:52
  3.5 3.0 %collective-permute-start.1 = (bf16[2,4,128,128]{3,2,1,0:T(8,128)(2,1)S(1)}, bf16[2,4,128,128]{3,2,1,0:T(8,128)(2,1)S(1)}, u32[]{:S(2)}, u32[]{:S(2)}) collective-permute-start(bf16[2,4,128,128]{3,2,1,0:T(8,128)(2,1)S(1)} %get-tuple-element.16), channel_id=1, source_target_pairs={{0,2},{1,3},{2,0},{3,1},{4,6},{5,7},{6,4},{7,5},{8,10},{9,11},{10,... | collective-permute-start | bytes 786440 | tf_op jit(solution)/shard_map/ppermute | solution.py:28
  6.5 3.4 %collective-permute-start.4 = (bf16[2,4,128,128]{3,2,1,0:T(8,128)(2,1)S(1)}, bf16[2,4,128,128]{3,2,1,0:T(8,128)(2,1)S(1)}, u32[]{:S(2)}, u32[]{:S(2)}) collective-permute-start(bf16[2,4,128,128]{3,2,1,0:T(8,128)(2,1)S(1)} %get-tuple-element.15.ko), channel_id=1, source_target_pairs={{0,4},{1,5},{2,6},{3,7},{4,8},{5,9},{6,10},{7,11},{8,12},{9,13},{1... | collective-permute-start | bytes 786440 | tf_op jit(solution)/shard_map/ppermute | solution.py:33
  9.9 0.0 copy-done
  9.9 0.0 copy-start.1
  9.9 1.0 %copy-done.1 = bf16[128,16,128]{2,1,0:T(8,128)(2,1)S(1)} copy-done((bf16[128,16,128]{2,1,0:T(8,128)(2,1)S(1)}, bf16[128,16,128]{2,1,0:T(8,128)(2,1)}, u32[]{:S(2)}) %copy-start.1) | copy-done | bytes 524312
  10.9 1.3 %split_heads.2 = (bf16[2,8,128,128]{3,2,1,0:T(8,128)(2,1)S(1)}, bf16[2,8,128,128]{3,2,1,0:T(8,128)(2,1)S(1)}) custom-call(s32[3]{0:T(128)S(1)} %pad_add_fusion.place, bf16[128,16,128]{2,1,0:T(8,128)(2,1)S(1)} %copy-done, bf16[128,16,128]{2,1,0:T(8,128)(2,1)S(1)} %copy-done.1), custom_call_target="tpu_custom_call" | custom-call | tf_op jit(solution)/shard_map/split_heads/pallas_call | solution.py:52
  12.2 0.6 collective-permute-start
  12.8 0.0 collective-permute-done.1.xo
  12.8 3.6 %collective-permute-start.5 = (bf16[2,4,128,128]{3,2,1,0:T(8,128)(2,1)S(1)}, bf16[2,4,128,128]{3,2,1,0:T(8,128)(2,1)S(1)}, u32[]{:S(2)}, u32[]{:S(2)}) collective-permute-start(bf16[2,4,128,128]{3,2,1,0:T(8,128)(2,1)S(1)} %collective-permute-done.1.xo), channel_id=1, source_target_pairs={{0,4},{1,5},{2,6},{3,7},{4,8},{5,9},{6,10},{7,11},{8,12},{9,13},{1... | collective-permute-start | bytes 786440 | tf_op jit(solution)/shard_map/ppermute | solution.py:33
  16.4 0.1 collective-permute-start.2
  16.5 0.5 collective-permute-start.3
  17.0 0.0 collective-permute-done.4.k1
  17.0 0.1 collective-permute-start.6
  17.1 4.0 %collective-permute-done.5.k2 = bf16[2,4,128,128]{3,2,1,0:T(8,128)(2,1)S(1)} collective-permute-done((bf16[2,4,128,128]{3,2,1,0:T(8,128)(2,1)S(1)}, bf16[2,4,128,128]{3,2,1,0:T(8,128)(2,1)S(1)}, u32[]{:S(2)}, u32[]{:S(2)}) %collective-permute-start.5) | collective-permute-done | bytes 262176 | tf_op jit(solution)/shard_map/ppermute | solution.py:33
  21.1 0.0 collective-permute-start.7
  21.1 0.0 collective-permute-done.2.mko
  21.1 0.0 collective-permute-done.3.mxo
  21.1 0.0 collective-permute-done.6.mk1
  21.1 4.2 %collective-permute-done.sent_q = bf16[2,8,128,128]{3,2,1,0:T(8,128)(2,1)S(1)} collective-permute-done((bf16[2,8,128,128]{3,2,1,0:T(8,128)(2,1)S(1)}, bf16[2,8,128,128]{3,2,1,0:T(8,128)(2,1)S(1)}, u32[]{:S(2)}, u32[]{:S(2)}) %collective-permute-start) | collective-permute-done | bytes 524320 | tf_op jit(solution)/shard_map/ppermute | solution.py:28
  25.4 0.0 collective-permute-done.7.mk2
  25.4 11.2 %window_grads.1 = (bf16[8,128,128]{2,1,0:T(8,128)(2,1)S(1)}, bf16[8,128,128]{2,1,0:T(8,128)(2,1)S(1)}, f32[2,2,4,128,128]{4,3,2,1,0:T(8,128)S(1)}, bf16[2,2,4,12...) custom-call(s32[3]{0:T(128)S(1)} %pad_add_fusion.place, ...), custom_call_target="tpu_custom_call" | custom-call | tf_op jit(solution)/shard_map/window_grads/pallas_call | solution.py:144
  36.6 0.0 collective-permute-start.10
  36.6 0.5 collective-permute-start.9
  37.1 0.5 collective-permute-start.8
  37.6 0.9 %collective-permute-done.10 = bf16[2,2,4,128,128]{4,3,2,1,0:T(8,128)(2,1)S(1)} collective-permute-done((bf16[2,2,4,128,128]{4,3,2,1,0:T(8,128)(2,1)S(1)}, bf16[2,2,4,128,128]{4,3,2,1,0:T(8,128)(2,1)S(1)}, u32[]{:S(2)}, u32[]{:S(2)}) %collective-permute-start.10) | collective-permute-done | bytes 524320 | tf_op jit(solution)/shard_map/ppermute | solution.py:28
  38.5 0.1 add_convert_fusion
  38.6 0.0 copy-start.4
  38.7 1.4 %collective-permute-start.12 = (bf16[2,4,128,128]{3,2,1,0:T(8,128)(2,1)S(1)}, bf16[2,4,128,128]{3,2,1,0:T(8,128)(2,1)S(1)}, u32[]{:S(2)}, u32[]{:S(2)}) collective-permute-start(bf16[2,4,128,128]{3,2,1,0:T(8,128)(2,1)S(1)} %get-tuple-element.25), channel_id=1, source_target_pairs={{4,0},{5,1},{6,2},{7,3},{8,4},{9,5},{10,6},{11,7},{12,8},{13,9},{1... | collective-permute-start | bytes 786440 | tf_op jit(solution)/shard_map/ppermute | solution.py:33
  40.1 1.3 %collective-permute-start.11 = (bf16[2,4,128,128]{3,2,1,0:T(8,128)(2,1)S(1)}, bf16[2,4,128,128]{3,2,1,0:T(8,128)(2,1)S(1)}, u32[]{:S(2)}, u32[]{:S(2)}) collective-permute-start(bf16[2,4,128,128]{3,2,1,0:T(8,128)(2,1)S(1)} %get-tuple-element.26), channel_id=1, source_target_pairs={{4,0},{5,1},{6,2},{7,3},{8,4},{9,5},{10,6},{11,7},{12,8},{13,9},{1... | collective-permute-start | bytes 786440 | tf_op jit(solution)/shard_map/ppermute | solution.py:33
  41.4 0.0 collective-permute-done.9
  41.4 0.0 copy-done.4
  41.5 0.1 convert_add_fusion
  41.6 8.3 %collective-permute-done.12 = bf16[2,4,128,128]{3,2,1,0:T(8,128)(2,1)S(1)} collective-permute-done((bf16[2,4,128,128]{3,2,1,0:T(8,128)(2,1)S(1)}, bf16[2,4,128,128]{3,2,1,0:T(8,128)(2,1)S(1)}, u32[]{:S(2)}, u32[]{:S(2)}) %collective-permute-start.12) | collective-permute-done | bytes 262176 | tf_op jit(solution)/shard_map/ppermute | solution.py:33
  49.9 4.8 %collective-permute-done.11 = bf16[2,4,128,128]{3,2,1,0:T(8,128)(2,1)S(1)} collective-permute-done((bf16[2,4,128,128]{3,2,1,0:T(8,128)(2,1)S(1)}, bf16[2,4,128,128]{3,2,1,0:T(8,128)(2,1)S(1)}, u32[]{:S(2)}, u32[]{:S(2)}) %collective-permute-start.11) | collective-permute-done | bytes 262176 | tf_op jit(solution)/shard_map/ppermute | solution.py:33
  54.7 0.1 fusion.1
  54.8 0.6 collective-permute-start.13
  55.4 0.0 collective-permute-done.8.sent_ref
  55.4 1.9 %join_heads.3 = bf16[128,16,128]{2,1,0:T(8,128)(2,1)} custom-call(s32[3]{0:T(128)S(1)} %pad_add_fusion.place, bf16[8,128,128]{2,1,0:T(8,128)(2,1)S(1)} %get-tuple-element.17.keep_ref, bf16[8,128,128]{2,1,0:T(8,128)(2,1)S(1)} %collective-permute-done.8.sent_ref), custom_call_target="tpu_custom_call" | custom-call | tf_op jit(solution)/shard_map/join_heads/pallas_call | solution.py:173
  57.4 5.0 %collective-permute-done.13 = bf16[2,4,128,128]{3,2,1,0:T(8,128)(2,1)S(1)} collective-permute-done((bf16[2,4,128,128]{3,2,1,0:T(8,128)(2,1)S(1)}, bf16[2,4,128,128]{3,2,1,0:T(8,128)(2,1)S(1)}, u32[]{:S(2)}, u32[]{:S(2)}) %collective-permute-start.13) | collective-permute-done | bytes 262176 | tf_op jit(solution)/shard_map/ppermute | solution.py:28
  62.4 1.4 %join_heads.5 = bf16[128,8,128]{2,1,0:T(8,128)(2,1)} custom-call(s32[3]{0:T(128)S(1)} %pad_add_fusion.place, bf16[4,128,128]{2,1,0:T(8,128)(2,1)S(1)} %get-tuple-element.29.keep_ref, bf16[4,128,128]{2,1,0:T(8,128)(2,1)S(1)} %get-tuple-element.27.sent_ref), custom_call_target="tpu_custom_call" | custom-call | tf_op jit(solution)/shard_map/join_heads/pallas_call | solution.py:173
  63.8 1.4 %join_heads.4 = bf16[128,8,128]{2,1,0:T(8,128)(2,1)} custom-call(s32[3]{0:T(128)S(1)} %pad_add_fusion.place, bf16[4,128,128]{2,1,0:T(8,128)(2,1)S(1)} %get-tuple-element.30.keep_ref, bf16[4,128,128]{2,1,0:T(8,128)(2,1)S(1)} %get-tuple-element.28.sent_ref), custom_call_target="tpu_custom_call" | custom-call | tf_op jit(solution)/shard_map/join_heads/pallas_call | solution.py:173
  (3 shorter events, 0.1 us)
Async XLA Ops:
  0.6 9.3 %copy-start = (bf16[128,16,128]{2,1,0:T(8,128)(2,1)S(1)}, bf16[128,16,128]{2,1,0:T(8,128)(2,1)}, u32[]{:S(2)}) copy-start(bf16[128,16,128]{2,1,0:T(8,128)(2,1)} %a_ref.2) | copy-start | bytes 1572868
  0.8 1.0 %copy-start.2 = (bf16[128,8,128]{2,1,0:T(8,128)(2,1)S(1)}, bf16[128,8,128]{2,1,0:T(8,128)(2,1)}, u32[]{:S(2)}) copy-start(bf16[128,8,128]{2,1,0:T(8,128)(2,1)} %a_ref.3) | copy-start | bytes 786436
  1.7 0.9 %copy-start.3 = (bf16[128,8,128]{2,1,0:T(8,128)(2,1)S(1)}, bf16[128,8,128]{2,1,0:T(8,128)(2,1)}, u32[]{:S(2)}) copy-start(bf16[128,8,128]{2,1,0:T(8,128)(2,1)} %b_ref.3) | copy-start | bytes 786436
  3.5 9.4 %collective-permute-start.1 = (bf16[2,4,128,128]{3,2,1,0:T(8,128)(2,1)S(1)}, bf16[2,4,128,128]{3,2,1,0:T(8,128)(2,1)S(1)}, u32[]{:S(2)}, u32[]{:S(2)}) collective-permute-start(bf16[2,4,128,128]{3,2,1,0:T(8,128)(2,1)S(1)} %get-tuple-element.16), channel_id=1, source_target_pairs={{0,2},{1,3},{2,0},{3,1},{4,6},{5,7},{6,4},{7,5},{8,10},{9,11},{10,... | collective-permute-start | bytes 786440 | tf_op jit(solution)/shard_map/ppermute | solution.py:28
  6.5 10.6 %collective-permute-start.4 = (bf16[2,4,128,128]{3,2,1,0:T(8,128)(2,1)S(1)}, bf16[2,4,128,128]{3,2,1,0:T(8,128)(2,1)S(1)}, u32[]{:S(2)}, u32[]{:S(2)}) collective-permute-start(bf16[2,4,128,128]{3,2,1,0:T(8,128)(2,1)S(1)} %get-tuple-element.15.ko), channel_id=1, source_target_pairs={{0,4},{1,5},{2,6},{3,7},{4,8},{5,9},{6,10},{7,11},{8,12},{9,13},{1... | collective-permute-start | bytes 786440 | tf_op jit(solution)/shard_map/ppermute | solution.py:33
  9.9 1.0 %copy-start.1 = (bf16[128,16,128]{2,1,0:T(8,128)(2,1)S(1)}, bf16[128,16,128]{2,1,0:T(8,128)(2,1)}, u32[]{:S(2)}) copy-start(bf16[128,16,128]{2,1,0:T(8,128)(2,1)} %b_ref.2) | copy-start | bytes 1572868
  12.2 13.2 %collective-permute-start = (bf16[2,8,128,128]{3,2,1,0:T(8,128)(2,1)S(1)}, bf16[2,8,128,128]{3,2,1,0:T(8,128)(2,1)S(1)}, u32[]{:S(2)}, u32[]{:S(2)}) collective-permute-start(bf16[2,8,128,128]{3,2,1,0:T(8,128)(2,1)S(1)} %get-tuple-element.14), channel_id=1, source_target_pairs={{0,2},{1,3},{2,0},{3,1},{4,6},{5,7},{6,4},{7,5},{8,10},{9,11},{10,... | collective-permute-start | bytes 1572872 | tf_op jit(solution)/shard_map/ppermute | solution.py:28
  12.8 8.3 %collective-permute-start.5 = (bf16[2,4,128,128]{3,2,1,0:T(8,128)(2,1)S(1)}, bf16[2,4,128,128]{3,2,1,0:T(8,128)(2,1)S(1)}, u32[]{:S(2)}, u32[]{:S(2)}) collective-permute-start(bf16[2,4,128,128]{3,2,1,0:T(8,128)(2,1)S(1)} %collective-permute-done.1.xo), channel_id=1, source_target_pairs={{0,4},{1,5},{2,6},{3,7},{4,8},{5,9},{6,10},{7,11},{8,12},{9,13},{1... | collective-permute-start | bytes 786440 | tf_op jit(solution)/shard_map/ppermute | solution.py:33
  16.4 4.7 %collective-permute-start.2 = (bf16[2,4,128,128]{3,2,1,0:T(8,128)(2,1)S(1)}, bf16[2,4,128,128]{3,2,1,0:T(8,128)(2,1)S(1)}, u32[]{:S(2)}, u32[]{:S(2)}) collective-permute-start(bf16[2,4,128,128]{3,2,1,0:T(8,128)(2,1)S(1)} %get-tuple-element.15.ko), channel_id=1, source_target_pairs={{0,1},{1,0},{2,3},{3,2},{4,5},{5,4},{6,7},{7,6},{8,9},{9,8},{10,11... | collective-permute-start | bytes 786440 | tf_op jit(solution)/shard_map/ppermute | solution.py:28
  16.5 4.6 %collective-permute-start.3 = (bf16[2,4,128,128]{3,2,1,0:T(8,128)(2,1)S(1)}, bf16[2,4,128,128]{3,2,1,0:T(8,128)(2,1)S(1)}, u32[]{:S(2)}, u32[]{:S(2)}) collective-permute-start(bf16[2,4,128,128]{3,2,1,0:T(8,128)(2,1)S(1)} %collective-permute-done.1.xo), channel_id=1, source_target_pairs={{0,1},{1,0},{2,3},{3,2},{4,5},{5,4},{6,7},{7,6},{8,9},{9,8},{10,11... | collective-permute-start | bytes 786440 | tf_op jit(solution)/shard_map/ppermute | solution.py:28
  17.0 4.1 %collective-permute-start.6 = (bf16[2,4,128,128]{3,2,1,0:T(8,128)(2,1)S(1)}, bf16[2,4,128,128]{3,2,1,0:T(8,128)(2,1)S(1)}, u32[]{:S(2)}, u32[]{:S(2)}) collective-permute-start(bf16[2,4,128,128]{3,2,1,0:T(8,128)(2,1)S(1)} %collective-permute-done.4.k1), channel_id=1, source_target_pairs={{0,1},{1,0},{2,3},{3,2},{4,5},{5,4},{6,7},{7,6},{8,9},{9,8},{10,11... | collective-permute-start | bytes 786440 | tf_op jit(solution)/shard_map/ppermute | solution.py:28
  21.1 4.3 %collective-permute-start.7 = (bf16[2,4,128,128]{3,2,1,0:T(8,128)(2,1)S(1)}, bf16[2,4,128,128]{3,2,1,0:T(8,128)(2,1)S(1)}, u32[]{:S(2)}, u32[]{:S(2)}) collective-permute-start(bf16[2,4,128,128]{3,2,1,0:T(8,128)(2,1)S(1)} %collective-permute-done.5.k2), channel_id=1, source_target_pairs={{0,1},{1,0},{2,3},{3,2},{4,5},{5,4},{6,7},{7,6},{8,9},{9,8},{10,11... | collective-permute-start | bytes 786440 | tf_op jit(solution)/shard_map/ppermute | solution.py:28
  36.6 1.9 %collective-permute-start.10 = (bf16[2,2,4,128,128]{4,3,2,1,0:T(8,128)(2,1)S(1)}, bf16[2,2,4,128,128]{4,3,2,1,0:T(8,128)(2,1)S(1)}, u32[]{:S(2)}, u32[]{:S(2)}) collective-permute-start(bf16[2,2,4,128,128]{4,3,2,1,0:T(8,128)(2,1)S(1)} %get-tuple-element.22), channel_id=1, source_target_pairs={{0,1},{1,0},{2,3},{3,2},{4,5},{5,4},{6,7},{7,6},{8,9},{9,8},{10,11... | collective-permute-start | bytes 1572872 | tf_op jit(solution)/shard_map/ppermute | solution.py:28
  36.6 4.8 %collective-permute-start.9 = (bf16[2,2,4,128,128]{4,3,2,1,0:T(8,128)(2,1)S(1)}, bf16[2,2,4,128,128]{4,3,2,1,0:T(8,128)(2,1)S(1)}, u32[]{:S(2)}, u32[]{:S(2)}) collective-permute-start(bf16[2,2,4,128,128]{4,3,2,1,0:T(8,128)(2,1)S(1)} %get-tuple-element.20), channel_id=1, source_target_pairs={{0,1},{1,0},{2,3},{3,2},{4,5},{5,4},{6,7},{7,6},{8,9},{9,8},{10,11... | collective-permute-start | bytes 1572872 | tf_op jit(solution)/shard_map/ppermute | solution.py:28
  37.1 18.3 %collective-permute-start.8 = (bf16[8,128,128]{2,1,0:T(8,128)(2,1)S(1)}, bf16[8,128,128]{2,1,0:T(8,128)(2,1)S(1)}, u32[]{:S(2)}, u32[]{:S(2)}) collective-permute-start(bf16[8,128,128]{2,1,0:T(8,128)(2,1)S(1)} %get-tuple-element.18), channel_id=1, source_target_pairs={{0,2},{1,3},{2,0},{3,1},{4,6},{5,7},{6,4},{7,5},{8,10},{9,11},{10,... | collective-permute-start | bytes 786440 | tf_op jit(solution)/shard_map/ppermute | solution.py:28
  38.6 2.8 %copy-start.4 = (f32[2,2,4,128,128]{4,3,2,1,0:T(8,128)S(1)}, f32[2,2,4,128,128]{4,3,2,1,0:T(8,128)}, u32[]{:S(2)}) copy-start(f32[2,2,4,128,128]{4,3,2,1,0:T(8,128)} %get-tuple-element.19) | copy-start | bytes 3145732
  38.7 11.2 %collective-permute-start.12 = (bf16[2,4,128,128]{3,2,1,0:T(8,128)(2,1)S(1)}, bf16[2,4,128,128]{3,2,1,0:T(8,128)(2,1)S(1)}, u32[]{:S(2)}, u32[]{:S(2)}) collective-permute-start(bf16[2,4,128,128]{3,2,1,0:T(8,128)(2,1)S(1)} %get-tuple-element.25), channel_id=1, source_target_pairs={{4,0},{5,1},{6,2},{7,3},{8,4},{9,5},{10,6},{11,7},{12,8},{13,9},{1... | collective-permute-start | bytes 786440 | tf_op jit(solution)/shard_map/ppermute | solution.py:33
  40.1 14.6 %collective-permute-start.11 = (bf16[2,4,128,128]{3,2,1,0:T(8,128)(2,1)S(1)}, bf16[2,4,128,128]{3,2,1,0:T(8,128)(2,1)S(1)}, u32[]{:S(2)}, u32[]{:S(2)}) collective-permute-start(bf16[2,4,128,128]{3,2,1,0:T(8,128)(2,1)S(1)} %get-tuple-element.26), channel_id=1, source_target_pairs={{4,0},{5,1},{6,2},{7,3},{8,4},{9,5},{10,6},{11,7},{12,8},{13,9},{1... | collective-permute-start | bytes 786440 | tf_op jit(solution)/shard_map/ppermute | solution.py:33
  54.8 7.6 %collective-permute-start.13 = (bf16[2,4,128,128]{3,2,1,0:T(8,128)(2,1)S(1)}, bf16[2,4,128,128]{3,2,1,0:T(8,128)(2,1)S(1)}, u32[]{:S(2)}, u32[]{:S(2)}) collective-permute-start(bf16[2,4,128,128]{3,2,1,0:T(8,128)(2,1)S(1)} %get-tuple-element.23), channel_id=1, source_target_pairs={{0,2},{1,3},{2,0},{3,1},{4,6},{5,7},{6,4},{7,5},{8,10},{9,11},{10,... | collective-permute-start | bytes 786440 | tf_op jit(solution)/shard_map/ppermute | solution.py:28

commit v2 on v1

v2 whole, which is shorter than its diff:
```python
import functools
import math

import jax
import jax.numpy as jnp
from jax import lax
from jax.experimental import pallas as pl
from jax.experimental.pallas import tpu as pltpu
from jax.sharding import PartitionSpec as P

WINDOW = 512
SCORE_SCALE = 168.0 ** -0.5
LOG2E = math.log2(math.e)
NEG = -1e30
VMEM_LIMIT = 48 * 1024 * 1024

NT = (((1,), (1,)), ((), ()))
NN = (((1,), (0,)), ((), ()))


def dot(a, b, dims):
    return lax.dot_general(a, b, dims, preferred_element_type=jnp.float32)


def swap(a, by):
    n = lax.axis_size("ctx")
    return lax.ppermute(a, "ctx", [(i, i ^ by) for i in range(n)])


def shift(a, by, wrap=False):
    n = lax.axis_size("ctx")
    pairs = [(i, (i + by) % n) for i in range(n) if wrap or 0 <= i + by < n]
    return lax.ppermute(a, "ctx", pairs)


def after(a, *others):
    return lax.optimization_barrier((a, *others))[0]


def split_heads_kernel(place, *refs):
    wide = refs[-1]
    ins = [refs[0].at[0], refs[0].at[1]] if len(refs[0].shape) == 4 else refs[:2]
    keep_ref, *sends = refs[1:-1] if len(refs[0].shape) == 4 else refs[2:-1]
    tok, heads, width = ins[0].shape
    half = heads // 2
    part = half // len(sends)
    x = place[0]
    for s, ref in enumerate(ins):
        wide[s] = ref[...].astype(jnp.float32).reshape(tok * heads, width)
        for j in range(half):
            low = wide[s, pl.ds(j, tok, stride=heads), :]
            high = wide[s, pl.ds(half + j, tok, stride=heads), :]
            keep_ref[s, j] = jnp.where(x == 0, low, high).astype(jnp.bfloat16)
            sends[j // part][s, j % part] = jnp.where(x == 0, high, low).astype(jnp.bfloat16)


def split_heads(place, chunks, *arrays):
    tok, heads, width = arrays[0].shape[-3:]
    shapes = [jax.ShapeDtypeStruct((2, heads // 2 // k, tok, width), jnp.bfloat16) for k in [1] + [chunks] * chunks]
    vmem = pl.BlockSpec(memory_space=pltpu.VMEM)
    return pl.pallas_call(
        split_heads_kernel,
        out_shape=tuple(shapes),
        in_specs=[pl.BlockSpec(memory_space=pltpu.SMEM)] + [vmem] * len(arrays),
        out_specs=(vmem,) * len(shapes),
        scratch_shapes=[pltpu.VMEM((2, tok * heads, width), jnp.float32)],
        compiler_params=pltpu.CompilerParams(vmem_limit_bytes=VMEM_LIMIT),
        name="split_heads",
    )(place, *arrays)


def grads_kernel(
    start, groups, place, keep_q, sent_q, ko, xo, mko, mxo, k1, k2, mk1, mk2,
    dq_keep, dq_send, prev_here, prev_mate, own_here, own_mate,
    kv,
):
    _, all_groups, tok, width = ko.shape
    heads = keep_q.shape[1] // all_groups
    x, c, first = place[0], place[1], place[2]
    blocks = WINDOW // tok
    span = WINDOW + tok
    reach = (2 * blocks - 1) * tok
    mine, other = 2 * x + c, 2 * (1 - x) + c
    mate_mine, mate_other = 2 * x + 1 - c, 2 * (1 - x) + 1 - c
    for ref, slot in (
        (k1, mine), (k2, other), (mk1, mate_mine), (mk2, mate_other),
        (ko, blocks + mine), (xo, blocks + other), (mko, blocks + mate_mine), (mxo, blocks + mate_other),
    ):
        kv[:, :, pl.ds(pl.multiple_of(slot * tok, tok), tok), :] = ref[:, start : start + groups]
    rows = pl.ds(pl.multiple_of(c * tok, tok), reach)
    key = lax.broadcasted_iota(jnp.int32, (tok, heads * tok), 0)
    query = lax.broadcasted_iota(jnp.int32, (tok, heads * tok), 1) % tok
    before, upto = key > query, key <= query

    def load(g):
        k, v = kv[0, g, rows, :], kv[1, g, rows, :]
        qs = []
        for xx in range(2):
            pair = []
            for s in range(2):
                mine_of = pl.ds((start + g) * heads, heads)
                keep, sent = keep_q[s, mine_of], sent_q[s, mine_of]
                pair.append(jnp.where(x == xx, keep, sent).reshape(heads * tok, width))
            qs.append(pair)
        return k, v, k.T, qs

    def products(state, xx):
        k, v, kt, qs = state
        q, do = qs[xx]
        win = slice(xx * 2 * tok, xx * 2 * tok + span)
        return dot(k[win], q, NT), dot(v[win], do, NT)

    def weights(state, xx, scores, gp):
        parts = []
        for t in range(blocks + 1):
            part = scores[t * tok : (t + 1) * tok] * (SCORE_SCALE * LOG2E)
            if t < blocks:
                hidden = jnp.logical_and(first == 1, 2 * xx + c + t < blocks)
                part = part + jnp.where(hidden, NEG, 0.0)
            if t == 0:
                part = jnp.where(before, part, NEG)
            if t == blocks:
                part = jnp.where(upto, part, NEG)
            parts.append(part)
        top = jnp.max(functools.reduce(jnp.maximum, parts), axis=0, keepdims=True)
        parts = [jnp.exp2(part - top) for part in parts]
        gps = [gp[t * tok : (t + 1) * tok] for t in range(blocks + 1)]
        total = jnp.sum(sum(parts[1:], parts[0]), axis=0, keepdims=True)
        mixed = [p * g for p, g in zip(parts, gps)]
        inverse = 1.0 / total
        row_dot = jnp.sum(sum(mixed[1:], mixed[0]), axis=0, keepdims=True) * inverse
        parts = [part * inverse for part in parts]
        low = jnp.concatenate([p.astype(jnp.bfloat16) for p in parts], axis=0)
        ds = jnp.concatenate([(p * (g - row_dot)).astype(jnp.bfloat16) for p, g in zip(parts, gps)], axis=0)
        return low, ds

    def outputs(g, state, sides):
        k, v, kt, qs = state
        dqs = []
        for xx in range(2):
            win = slice(xx * 2 * tok, xx * 2 * tok + span)
            dqs.append((dot(kt[:, win], sides[xx][1], NN) * SCORE_SCALE).T.astype(jnp.bfloat16).reshape(heads, tok, width))
        hs = pl.ds(g * heads, heads)
        dq_keep[hs] = jnp.where(x == 0, dqs[0], dqs[1])
        dq_send[hs] = jnp.where(x == 0, dqs[1], dqs[0])
        cut = span - 2 * tok
        for s, scale in enumerate((SCORE_SCALE, 1.0)):
            w0, w1 = sides[0][1 - s], sides[1][1 - s]
            r0, r1 = qs[0][s], qs[1][s]
            early = dot(w0[: 2 * tok], r0, NN)
            both = dot(w0[2 * tok :], r0, NN) + dot(w1[:cut], r1, NN)
            late = dot(w1[cut:], r1, NN)
            got = jnp.concatenate([early, both, late], axis=0) * scale
            for t in range(0, 2 * blocks - 1, 2):
                ref, xx = (prev_here, t // 2) if t < blocks else (own_here, (t - blocks) // 2)
                ref[xx ^ x, s, g] = got[t * tok : (t + 1) * tok].astype(ref.dtype)
            odd = [got[t * tok : (t + 1) * tok].astype(jnp.bfloat16) for t in (1, 3, 5)]
            zero = jnp.zeros_like(odd[0])
            low_core = c == 0
            four = [
                jnp.where(low_core, odd[0], zero),
                jnp.where(low_core, odd[1], odd[0]),
                jnp.where(low_core, odd[2], odd[1]),
                jnp.where(low_core, zero, odd[2]),
            ]
            for xx in range(2):
                prev_mate[xx ^ x, s, g] = four[xx]
                own_mate[xx ^ x, s, g] = four[2 + xx]

    flow = [(g, xx) for g in range(groups) for xx in range(2)]
    states = {0: load(0)}
    ready = products(states[0], 0)
    sides = {}
    for i, (g, xx) in enumerate(flow):
        now = ready
        if i + 1 < len(flow):
            ng, nx = flow[i + 1]
            if ng not in states:
                states[ng] = load(ng)
            ready = products(states[ng], nx)
        if xx == 0 and g > 0:
            outputs(g - 1, states.pop(g - 1), sides.pop(g - 1))
        sides.setdefault(g, []).append(weights(states[g], xx, *now))
    outputs(groups - 1, states[groups - 1], sides[groups - 1])

def grads(start, groups, place, keep_q, sent_q, *kvs):
    _, all_groups, tok, width = kvs[0].shape
    heads = keep_q.shape[1] // all_groups
    bf, f32 = jnp.bfloat16, jnp.float32
    dq_shape = jax.ShapeDtypeStruct((groups * heads, tok, width), bf)
    dkv_shape = functools.partial(jax.ShapeDtypeStruct, (2, 2, groups, tok, width))
    vmem = pl.BlockSpec(memory_space=pltpu.VMEM)
    return pl.pallas_call(
        functools.partial(grads_kernel, start, groups),
        out_shape=(dq_shape, dq_shape, dkv_shape(f32), dkv_shape(bf), dkv_shape(f32), dkv_shape(bf)),
        in_specs=[pl.BlockSpec(memory_space=pltpu.SMEM)] + [vmem] * 10,
        out_specs=(vmem,) * 6,
        scratch_shapes=[pltpu.VMEM((2, groups, 2 * WINDOW, width), bf)],
        compiler_params=pltpu.CompilerParams(vmem_limit_bytes=VMEM_LIMIT),
        cost_estimate=pl.CostEstimate(flops=1, bytes_accessed=1, transcendentals=0),
        name="window_grads",
    )(place, keep_q, sent_q, *kvs)


def join_heads_kernel(count, place, *refs):
    outs, wide = refs[-1 - count : -1], refs[-1]
    ins = refs[: -1 - count]
    tok, heads, width = outs[0].shape
    half = heads // 2
    chunks = len(ins) // 2
    part = half // chunks
    x = place[0]
    for s, out in enumerate(outs):
        for j in range(half):
            keep = ins[j // part][s, j % part].astype(jnp.float32)
            sent = ins[chunks + j // part][s, j % part].astype(jnp.float32)
            wide[s, pl.ds(j, tok, stride=heads), :] = jnp.where(x == 0, keep, sent)
            wide[s, pl.ds(half + j, tok, stride=heads), :] = jnp.where(x == 0, sent, keep)
        out[...] = wide[s].reshape(tok, heads, width).astype(out.dtype)


def join_heads(place, keeps, sents):
    count, part, tok, width = keeps[0].shape
    heads = 2 * part * len(keeps)
    vmem = pl.BlockSpec(memory_space=pltpu.VMEM)
    return pl.pallas_call(
        functools.partial(join_heads_kernel, count),
        out_shape=(jax.ShapeDtypeStruct((tok, heads, width), jnp.bfloat16),) * count,
        in_specs=[pl.BlockSpec(memory_space=pltpu.SMEM)] + [vmem] * (2 * len(keeps)),
        out_specs=(vmem,) * count,
        scratch_shapes=[pltpu.VMEM((count, tok * heads, width), jnp.float32)],
        compiler_params=pltpu.CompilerParams(vmem_limit_bytes=VMEM_LIMIT),
        name="join_heads",
    )(place, *keeps, *sents)


def body(queries, keys, values, d_out):
    tok = queries.shape[0]
    quad = WINDOW // tok
    assert quad == 4 and lax.axis_size("ctx") % quad == 0
    me = lax.axis_index("ctx")
    x, c, first = (me // 2) % 2, me % 2, (me < quad).astype(jnp.int32)
    place = jnp.stack([x, c, first]).astype(jnp.int32)
    bf, f32 = jnp.bfloat16, jnp.float32
    chunks = 2

    kv_keep, kv_send = split_heads(place, 1, jnp.stack([keys, values]))
    q_keep, q_send = split_heads(place, 1, queries, d_out)
    kv_x = swap(kv_send, 2)
    kv_1 = shift(kv_keep, quad, wrap=True)
    q_x = swap(q_send, 2)
    kv_2 = shift(kv_x, quad)
    mates = [swap(after(a, kv_1), 1) for a in (kv_keep, kv_x)]
    mates += [swap(kv_1, 1), swap(kv_2, 1)]
    per = kv_keep.shape[1] // chunks

    dq_keep, dq_x, mine, dkv_x = [], [], [], []
    for i in range(chunks):
        keep, send, prev_here, prev_mate, own_here, own_mate = grads(
            i * per, per, place, q_keep, q_x,
            kv_keep, kv_x, mates[0], mates[1], kv_1, kv_2, mates[2], mates[3],
        )
        if i:
            own_mate = after(own_mate, back)
        prev_sum = (prev_here + swap(prev_mate, 1).astype(f32)).astype(bf)
        back = shift(prev_sum, -quad, wrap=i + 1 < chunks)
        own_sum = own_here + swap(own_mate, 1).astype(f32) + back.astype(f32)
        dkv_x.append(swap(own_sum[1].astype(bf), 2))
        mine.append(own_sum[0].astype(bf))
        dq_keep.append(keep[None])
        dq_x.append(swap(after(send, prev_sum), 2)[None])
    (dq,) = join_heads(place, dq_keep, dq_x)
    dk, dv = join_heads(place, mine, dkv_x)
    return dq, dk, dv


def solution(mesh):
    spec = P("ctx", None, None)
    return jax.shard_map(
        body,
        mesh=mesh,
        in_specs=(spec,) * 4,
        out_specs=(spec,) * 3,
        check_vma=False,
    )
```

time: 65.5 us -> 52.5 us (0.80)
  waiting for transfers between devices: 27.3 us -> 16.7 us
  Pallas kernels: 18 us -> 11.4 us
  starting transfers between devices: 15.7 us -> 21.8 us
  local copies, waits for them, and re-layouts: 3.06 us -> 0.05 us
  other arithmetic: 0.42 us -> 1.51 us
    ppermute x4, waiting for transfers between devices: 17.1 us -> 8.72 us  [shift(): return lax.ppermute(a, 'ctx', pairs)]
    pallas_call x6, Pallas kernels: 18 us -> 11.4 us  [the longest x2 5.92 us: grads(): pl.pallas_call(functools.partial(grads_kernel, start, groups), out_shape=...]
    ppermute x10 -> x14, starting transfers between devices: 5.9 us -> 10.1 us  [swap(): return lax.ppermute(a, 'ctx', [(i, i ^ by) for i in range(n)])]
    unnamed x10 -> x4, local copies, waits for them, and re-layouts: 2.98 us -> 0.01 us
    ppermute x10 -> x14, waiting for transfers between devices: 10.2 us -> 8 us  [swap(): return lax.ppermute(a, 'ctx', [(i, i ^ by) for i in range(n)])]
    ppermute x4, starting transfers between devices: 9.77 us -> 11.7 us  [shift(): return lax.ppermute(a, 'ctx', pairs)]
    another operation x0 -> x3, other arithmetic: none -> 1.32 us  [the longest x1 1.14 us: body(): kv_keep, kv_send = split_heads(place, 1, jnp.stack([keys, values]))]
  transfers between devices with their start and end apart: 14 -> 18, of which waited for: 6 -> 6; matrix products, arithmetic and copies ran while one was open for 1% -> 1% of each run, Pallas kernels for 5% -> 12%
where the time goes in v2:
time: 52.5 us; the launch traced here: 52.3 us
  starting transfers between devices  21.8 us (42%)
  waiting for transfers between devices  16.7 us (32%)
  Pallas kernels  11.4 us (22%)
  other arithmetic  1.51 us (3%)
  between operations  0.81 us (2%)
    ppermute x4, starting transfers between devices, shift(): return lax.ppermute(a, 'ctx', pairs)  11.7 us
    ppermute x14, starting transfers between devices, swap(): return lax.ppermute(a, 'ctx', [(i, i ^ by) for i in range(n)])  10.1 us
    ppermute x4, waiting for transfers between devices, shift(): return lax.ppermute(a, 'ctx', pairs)  8.72 us
    ppermute x14, waiting for transfers between devices, swap(): return lax.ppermute(a, 'ctx', [(i, i ^ by) for i in range(n)])  8 us
    pallas_call x2, Pallas kernels, grads(): pl.pallas_call(functools.partial(grads_kernel, start, groups), out_shape=...  5.92 us
    pallas_call x2, Pallas kernels, join_heads(): pl.pallas_call(functools.partial(join_heads_kernel, count), out_shape=(ja...  3.49 us
    pallas_call x2, Pallas kernels, split_heads(): pl.pallas_call(split_heads_kernel, out_shape=tuple(shapes), in_specs=[pl....  2.02 us
    another operation x1, other arithmetic, body(): kv_keep, kv_send = split_heads(place, 1, jnp.stack([keys, values]))  1.14 us
  transfers between devices with their start and end apart: 18, of which 6 were waited for; matrix products, arithmetic and copies ran while one was open for 1% of the time, Pallas kernels for 12%

profile of v2, /device:TPU:0, one launch (start us, length us, event | category | flops | bytes accessed | tf_op | source)
XLA Modules:
  0.0 52.3 jit_solution(15307596991474284266)
XLA Ops:
  0.7 1.1 %pad_maximum_fusion.refs_0_ = bf16[2,128,8,128]{3,2,1,0:T(8,128)(2,1)S(1)} fusion(bf16[1,128,8,128]{3,2,1,0:T(8,128)(2,1)} %bitcast.21, bf16[1,128,8,128]{3,2,1,0:T(8,128)(2,1)} %bitcast.22), kind=kLoop, calls=%fused_computation | loop fusion | flops 262144 | bytes 1048576 | tf_op jit(solution)/shard_map/stack | solution.py:247
  1.8 0.0 copy-start
  1.8 0.1 pad_add_fusion.place
  1.9 0.8 %split_heads.3 = (bf16[2,4,128,128]{3,2,1,0:T(8,128)(2,1)S(1)}, bf16[2,4,128,128]{3,2,1,0:T(8,128)(2,1)S(1)}) custom-call(s32[3]{0:T(128)S(1)} %pad_add_fusion.place, bf16[2,128,8,128]{3,2,1,0:T(8,128)(2,1)S(1)} %pad_maximum_fusion.refs_0_), custom_call_target="tpu_custom_call" | custom-call | tf_op jit(solution)/shard_map/split_heads/pallas_call | solution.py:61
  2.7 3.0 %collective-permute-start.1 = (bf16[2,4,128,128]{3,2,1,0:T(8,128)(2,1)S(1)}, bf16[2,4,128,128]{3,2,1,0:T(8,128)(2,1)S(1)}, u32[]{:S(2)}, u32[]{:S(2)}) collective-permute-start(bf16[2,4,128,128]{3,2,1,0:T(8,128)(2,1)S(1)} %get-tuple-element.29), channel_id=1, source_target_pairs={{0,2},{1,3},{2,0},{3,1},{4,6},{5,7},{6,4},{7,5},{8,10},{9,11},{10,... | collective-permute-start | bytes 786440 | tf_op jit(solution)/shard_map/ppermute | solution.py:27
  5.7 1.5 %collective-permute-start.2 = (bf16[2,4,128,128]{3,2,1,0:T(8,128)(2,1)S(1)}, bf16[2,4,128,128]{3,2,1,0:T(8,128)(2,1)S(1)}, u32[]{:S(2)}, u32[]{:S(2)}) collective-permute-start(bf16[2,4,128,128]{3,2,1,0:T(8,128)(2,1)S(1)} %get-tuple-element.30.ko), channel_id=1, source_target_pairs={{0,4},{1,5},{2,6},{3,7},{4,8},{5,9},{6,10},{7,11},{8,12},{9,13},{1... | collective-permute-start | bytes 786440 | tf_op jit(solution)/shard_map/ppermute | solution.py:33
  7.2 1.3 %split_heads.2 = (bf16[2,8,128,128]{3,2,1,0:T(8,128)(2,1)S(1)}, bf16[2,8,128,128]{3,2,1,0:T(8,128)(2,1)S(1)}) custom-call(s32[3]{0:T(128)S(1)} %pad_add_fusion.place, bf16[128,16,128]{2,1,0:T(8,128)(2,1)S(1)} %copy-done, bf16[128,16,128]{2,1,0:T(8,128)(2,1)S(1)} %copy-done.1), custom_call_target="tpu_custom_call" | custom-call | tf_op jit(solution)/shard_map/split_heads/pallas_call | solution.py:61
  8.5 0.6 %collective-permute-start = (bf16[2,8,128,128]{3,2,1,0:T(8,128)(2,1)S(1)}, bf16[2,8,128,128]{3,2,1,0:T(8,128)(2,1)S(1)}, u32[]{:S(2)}, u32[]{:S(2)}) collective-permute-start(bf16[2,8,128,128]{3,2,1,0:T(8,128)(2,1)S(1)} %get-tuple-element.27), channel_id=1, source_target_pairs={{0,2},{1,3},{2,0},{3,1},{4,6},{5,7},{6,4},{7,5},{8,10},{9,11},{10,... | collective-permute-start | bytes 1572872 | tf_op jit(solution)/shard_map/ppermute | solution.py:27
  9.1 3.7 %collective-permute-done.1.xo = bf16[2,4,128,128]{3,2,1,0:T(8,128)(2,1)S(1)} collective-permute-done((bf16[2,4,128,128]{3,2,1,0:T(8,128)(2,1)S(1)}, bf16[2,4,128,128]{3,2,1,0:T(8,128)(2,1)S(1)}, u32[]{:S(2)}, u32[]{:S(2)}) %collective-permute-start.1) | collective-permute-done | bytes 262176 | tf_op jit(solution)/shard_map/ppermute | solution.py:27
  12.8 4.0 %collective-permute-start.5 = (bf16[2,4,128,128]{3,2,1,0:T(8,128)(2,1)S(1)}, bf16[2,4,128,128]{3,2,1,0:T(8,128)(2,1)S(1)}, u32[]{:S(2)}, u32[]{:S(2)}) collective-permute-start(bf16[2,4,128,128]{3,2,1,0:T(8,128)(2,1)S(1)} %collective-permute-done.1.xo), channel_id=1, source_target_pairs={{0,4},{1,5},{2,6},{3,7},{4,8},{5,9},{6,10},{7,11},{8,12},{9,13},{1... | collective-permute-start | bytes 786440 | tf_op jit(solution)/shard_map/ppermute | solution.py:33
  16.8 0.0 collective-permute-done.2.k1
  16.8 0.1 collective-permute-start.4
  16.9 0.5 collective-permute-start.3
  17.4 0.1 collective-permute-start.6
  17.5 3.2 %collective-permute-done.5.k2 = bf16[2,4,128,128]{3,2,1,0:T(8,128)(2,1)S(1)} collective-permute-done((bf16[2,4,128,128]{3,2,1,0:T(8,128)(2,1)S(1)}, bf16[2,4,128,128]{3,2,1,0:T(8,128)(2,1)S(1)}, u32[]{:S(2)}, u32[]{:S(2)}) %collective-permute-start.5) | collective-permute-done | bytes 262176 | tf_op jit(solution)/shard_map/ppermute | solution.py:33
  20.7 0.0 collective-permute-start.7
  20.7 0.0 collective-permute-done.4.mxo
  20.7 0.0 collective-permute-done.3.mko
  20.7 0.0 collective-permute-done.6.mk1
  20.7 2.5 %collective-permute-done.sent_q = bf16[2,8,128,128]{3,2,1,0:T(8,128)(2,1)S(1)} collective-permute-done((bf16[2,8,128,128]{3,2,1,0:T(8,128)(2,1)S(1)}, bf16[2,8,128,128]{3,2,1,0:T(8,128)(2,1)S(1)}, u32[]{:S(2)}, u32[]{:S(2)}) %collective-permute-start) | collective-permute-done | bytes 524320 | tf_op jit(solution)/shard_map/ppermute | solution.py:27
  23.2 0.0 collective-permute-done.7.mk2
  23.2 2.9 %window_grads.2 = (bf16[4,128,128]{2,1,0:T(8,128)(2,1)S(1)}, bf16[4,128,128]{2,1,0:T(8,128)(2,1)S(1)}, f32[2,2,2,128,128]{4,3,2,1,0:T(8,128)S(1)}, bf16[2,2,2,12...) custom-call(s32[3]{0:T(128)S(1)} %pad_add_fusion.place, ...), custom_call_target="tpu_custom_call" | custom-call | flops 1 | bytes 1 | tf_op jit(solution)/shard_map/window_grads/pallas_call | solution.py:193
  26.2 0.1 collective-permute-start.8
  26.3 3.0 %window_grads.3 = (bf16[4,128,128]{2,1,0:T(8,128)(2,1)S(1)}, bf16[4,128,128]{2,1,0:T(8,128)(2,1)S(1)}, f32[2,2,2,128,128]{4,3,2,1,0:T(8,128)S(1)}, bf16[2,2,2,12...) custom-call(s32[3]{0:T(128)S(1)} %pad_add_fusion.place, ...), custom_call_target="tpu_custom_call" | custom-call | flops 1 | bytes 1 | tf_op jit(solution)/shard_map/window_grads/pallas_call | solution.py:193
  29.2 0.6 %collective-permute-start.10 = (bf16[2,2,2,128,128]{4,3,2,1,0:T(8,128)(2,1)S(1)}, bf16[2,2,2,128,128]{4,3,2,1,0:T(8,128)(2,1)S(1)}, u32[]{:S(2)}, u32[]{:S(2)}) collective-permute-start(bf16[2,2,2,128,128]{4,3,2,1,0:T(8,128)(2,1)S(1)} %get-tuple-element.40), channel_id=1, source_target_pairs={{0,1},{1,0},{2,3},{3,2},{4,5},{5,4},{6,7},{7,6},{8,9},{9,8},{10,11... | collective-permute-start | bytes 786440 | tf_op jit(solution)/shard_map/ppermute | solution.py:27
  29.8 0.0 collective-permute-done.8
  29.8 0.1 add_convert_fusion.3
  29.8 4.9 %collective-permute-start.13 = (bf16[2,2,2,128,128]{4,3,2,1,0:T(8,128)(2,1)S(1)}, bf16[2,2,2,128,128]{4,3,2,1,0:T(8,128)(2,1)S(1)}, u32[]{:S(2)}, u32[]{:S(2)}) collective-permute-start(bf16[2,2,2,128,128]{4,3,2,1,0:T(8,128)(2,1)S(1)} %add_convert_fusion.3), channel_id=1, source_target_pairs={{0,28},{1,29},{2,30},{3,31},{4,0},{5,1},{6,2},{7,3},{8,4},{9,5},{1... | collective-permute-start | bytes 786440 | tf_op jit(solution)/shard_map/ppermute | solution.py:33
  34.7 0.0 collective-permute-start.12
  34.7 0.0 collective-permute-done.10
  34.7 0.1 add_convert_fusion.2
  34.8 1.3 %collective-permute-start.15 = (bf16[2,2,2,128,128]{4,3,2,1,0:T(8,128)(2,1)S(1)}, bf16[2,2,2,128,128]{4,3,2,1,0:T(8,128)(2,1)S(1)}, u32[]{:S(2)}, u32[]{:S(2)}) collective-permute-start(bf16[2,2,2,128,128]{4,3,2,1,0:T(8,128)(2,1)S(1)} %add_convert_fusion.2), channel_id=1, source_target_pairs={{4,0},{5,1},{6,2},{7,3},{8,4},{9,5},{10,6},{11,7},{12,8},{13,9},{1... | collective-permute-start | bytes 786440 | tf_op jit(solution)/shard_map/ppermute | solution.py:33
  36.1 1.6 %collective-permute-start.11 = (bf16[4,128,128]{2,1,0:T(8,128)(2,1)S(1)}, bf16[4,128,128]{2,1,0:T(8,128)(2,1)S(1)}, u32[]{:S(2)}, u32[]{:S(2)}) collective-permute-start(bf16[4,128,128]{2,1,0:T(8,128)(2,1)S(1)} %get-tuple-element.41), channel_id=1, source_target_pairs={{0,2},{1,3},{2,0},{3,1},{4,6},{5,7},{6,4},{7,5},{8,10},{9,11},{10,... | collective-permute-start | bytes 393224 | tf_op jit(solution)/shard_map/ppermute | solution.py:27
  37.6 0.5 %collective-permute-start.9 = (bf16[4,128,128]{2,1,0:T(8,128)(2,1)S(1)}, bf16[4,128,128]{2,1,0:T(8,128)(2,1)S(1)}, u32[]{:S(2)}, u32[]{:S(2)}) collective-permute-start(bf16[4,128,128]{2,1,0:T(8,128)(2,1)S(1)} %get-tuple-element.37), channel_id=1, source_target_pairs={{0,2},{1,3},{2,0},{3,1},{4,6},{5,7},{6,4},{7,5},{8,10},{9,11},{10,... | collective-permute-start | bytes 393224 | tf_op jit(solution)/shard_map/ppermute | solution.py:27
  38.2 2.3 %collective-permute-done.13 = bf16[2,2,2,128,128]{4,3,2,1,0:T(8,128)(2,1)S(1)} collective-permute-done((bf16[2,2,2,128,128]{4,3,2,1,0:T(8,128)(2,1)S(1)}, bf16[2,2,2,128,128]{4,3,2,1,0:T(8,128)(2,1)S(1)}, u32[]{:S(2)}, u32[]{:S(2)}) %collective-permute-start.13) | collective-permute-done | bytes 262176 | tf_op jit(solution)/shard_map/ppermute | solution.py:33
  40.5 0.0 collective-permute-start.14
  40.5 0.0 collective-permute-done.12
  40.5 0.1 add_convert_fusion.1
  40.6 1.6 %collective-permute-start.16 = (bf16[2,2,128,128]{3,2,1,0:T(8,128)(2,1)S(1)}, bf16[2,2,128,128]{3,2,1,0:T(8,128)(2,1)S(1)}, u32[]{:S(2)}, u32[]{:S(2)}) collective-permute-start(bf16[2,2,128,128]{3,2,1,0:T(8,128)(2,1)S(1)} %get-tuple-element.51), channel_id=1, source_target_pairs={{0,2},{1,3},{2,0},{3,1},{4,6},{5,7},{6,4},{7,5},{8,10},{9,11},{10,... | collective-permute-start | bytes 393224 | tf_op jit(solution)/shard_map/ppermute | solution.py:27
  42.2 3.2 %collective-permute-done.15 = bf16[2,2,2,128,128]{4,3,2,1,0:T(8,128)(2,1)S(1)} collective-permute-done((bf16[2,2,2,128,128]{4,3,2,1,0:T(8,128)(2,1)S(1)}, bf16[2,2,2,128,128]{4,3,2,1,0:T(8,128)(2,1)S(1)}, u32[]{:S(2)}, u32[]{:S(2)}) %collective-permute-start.15) | collective-permute-done | bytes 262176 | tf_op jit(solution)/shard_map/ppermute | solution.py:33
  45.4 0.0 collective-permute-done.14
  45.4 0.1 add_convert_fusion
  45.5 1.6 %collective-permute-start.17 = (bf16[2,2,128,128]{3,2,1,0:T(8,128)(2,1)S(1)}, bf16[2,2,128,128]{3,2,1,0:T(8,128)(2,1)S(1)}, u32[]{:S(2)}, u32[]{:S(2)}) collective-permute-start(bf16[2,2,128,128]{3,2,1,0:T(8,128)(2,1)S(1)} %get-tuple-element.49), channel_id=1, source_target_pairs={{0,2},{1,3},{2,0},{3,1},{4,6},{5,7},{6,4},{7,5},{8,10},{9,11},{10,... | collective-permute-start | bytes 393224 | tf_op jit(solution)/shard_map/ppermute | solution.py:27
  47.1 0.0 collective-permute-done.11
  47.1 0.0 collective-permute-done.9
  47.1 1.9 %join_heads.2 = bf16[128,16,128]{2,1,0:T(8,128)(2,1)} custom-call(s32[3]{0:T(128)S(1)} %pad_add_fusion.place, bf16[1,4,128,128]{3,2,1,0:T(8,128)(2,1)S(1)} %bitcast.17, bf16[1,4,128,128]{3,2,1,0:T(8,128)(2,1)S(1)} %bitcast.18, bf16[1,4,128,128]{3,2,1,0:T(8,128)(2,1)S(1)} %bitcast.20, bf16[1,4,128,128]{3,2,1,0:T(8,128)(2,1)S(1)} %bitcast.19), custom_call_target="tpu_custom_call" | custom-call | tf_op jit(solution)/shard_map/join_heads/pallas_call | solution.py:226
  49.0 1.7 %collective-permute-done.17.refs_3_ = bf16[2,2,128,128]{3,2,1,0:T(8,128)(2,1)S(1)} collective-permute-done((bf16[2,2,128,128]{3,2,1,0:T(8,128)(2,1)S(1)}, bf16[2,2,128,128]{3,2,1,0:T(8,128)(2,1)S(1)}, u32[]{:S(2)}, u32[]{:S(2)}) %collective-permute-start.17) | collective-permute-done | bytes 131104 | tf_op jit(solution)/shard_map/ppermute | solution.py:27
  50.7 1.6 %join_heads.3 = (bf16[128,8,128]{2,1,0:T(8,128)(2,1)}, bf16[128,8,128]{2,1,0:T(8,128)(2,1)}) custom-call(s32[3]{0:T(128)S(1)} %pad_add_fusion.place, bf16[2,2,128,128]{3,2,1,0:T(8,128)(2,1)S(1)} %get-tuple-element.52.refs_0_, bf16[2,2,128,128]{3,2,1,0:T(8,128)(2,1)S(1)} %get-tuple-element.50.refs_1_, ...), custom_call_target="tpu_custom_call" | custom-call | tf_op jit(solution)/shard_map/join_heads/pallas_call | solution.py:226
  (6 shorter events, 0.0 us)
Async XLA Ops:
  0.7 6.5 %copy-start.1 = (bf16[128,16,128]{2,1,0:T(8,128)(2,1)S(1)}, bf16[128,16,128]{2,1,0:T(8,128)(2,1)}, u32[]{:S(2)}) copy-start(bf16[128,16,128]{2,1,0:T(8,128)(2,1)} %refs_1_.1) | copy-start | bytes 1572868
  1.8 5.4 %copy-start = (bf16[128,16,128]{2,1,0:T(8,128)(2,1)S(1)}, bf16[128,16,128]{2,1,0:T(8,128)(2,1)}, u32[]{:S(2)}) copy-start(bf16[128,16,128]{2,1,0:T(8,128)(2,1)} %refs_0_.1) | copy-start | bytes 1572868
  2.7 10.1 %collective-permute-start.1 = (bf16[2,4,128,128]{3,2,1,0:T(8,128)(2,1)S(1)}, bf16[2,4,128,128]{3,2,1,0:T(8,128)(2,1)S(1)}, u32[]{:S(2)}, u32[]{:S(2)}) collective-permute-start(bf16[2,4,128,128]{3,2,1,0:T(8,128)(2,1)S(1)} %get-tuple-element.29), channel_id=1, source_target_pairs={{0,2},{1,3},{2,0},{3,1},{4,6},{5,7},{6,4},{7,5},{8,10},{9,11},{10,... | collective-permute-start | bytes 786440 | tf_op jit(solution)/shard_map/ppermute | solution.py:27
  5.7 11.1 %collective-permute-start.2 = (bf16[2,4,128,128]{3,2,1,0:T(8,128)(2,1)S(1)}, bf16[2,4,128,128]{3,2,1,0:T(8,128)(2,1)S(1)}, u32[]{:S(2)}, u32[]{:S(2)}) collective-permute-start(bf16[2,4,128,128]{3,2,1,0:T(8,128)(2,1)S(1)} %get-tuple-element.30.ko), channel_id=1, source_target_pairs={{0,4},{1,5},{2,6},{3,7},{4,8},{5,9},{6,10},{7,11},{8,12},{9,13},{1... | collective-permute-start | bytes 786440 | tf_op jit(solution)/shard_map/ppermute | solution.py:33
  8.5 14.8 %collective-permute-start = (bf16[2,8,128,128]{3,2,1,0:T(8,128)(2,1)S(1)}, bf16[2,8,128,128]{3,2,1,0:T(8,128)(2,1)S(1)}, u32[]{:S(2)}, u32[]{:S(2)}) collective-permute-start(bf16[2,8,128,128]{3,2,1,0:T(8,128)(2,1)S(1)} %get-tuple-element.27), channel_id=1, source_target_pairs={{0,2},{1,3},{2,0},{3,1},{4,6},{5,7},{6,4},{7,5},{8,10},{9,11},{10,... | collective-permute-start | bytes 1572872 | tf_op jit(solution)/shard_map/ppermute | solution.py:27
  12.8 7.9 %collective-permute-start.5 = (bf16[2,4,128,128]{3,2,1,0:T(8,128)(2,1)S(1)}, bf16[2,4,128,128]{3,2,1,0:T(8,128)(2,1)S(1)}, u32[]{:S(2)}, u32[]{:S(2)}) collective-permute-start(bf16[2,4,128,128]{3,2,1,0:T(8,128)(2,1)S(1)} %collective-permute-done.1.xo), channel_id=1, source_target_pairs={{0,4},{1,5},{2,6},{3,7},{4,8},{5,9},{6,10},{7,11},{8,12},{9,13},{1... | collective-permute-start | bytes 786440 | tf_op jit(solution)/shard_map/ppermute | solution.py:33
  16.8 3.9 %collective-permute-start.4 = (bf16[2,4,128,128]{3,2,1,0:T(8,128)(2,1)S(1)}, bf16[2,4,128,128]{3,2,1,0:T(8,128)(2,1)S(1)}, u32[]{:S(2)}, u32[]{:S(2)}) collective-permute-start(bf16[2,4,128,128]{3,2,1,0:T(8,128)(2,1)S(1)} %collective-permute-done.1.xo), channel_id=1, source_target_pairs={{0,1},{1,0},{2,3},{3,2},{4,5},{5,4},{6,7},{7,6},{8,9},{9,8},{10,11... | collective-permute-start | bytes 786440 | tf_op jit(solution)/shard_map/ppermute | solution.py:27
  16.9 3.8 %collective-permute-start.3 = (bf16[2,4,128,128]{3,2,1,0:T(8,128)(2,1)S(1)}, bf16[2,4,128,128]{3,2,1,0:T(8,128)(2,1)S(1)}, u32[]{:S(2)}, u32[]{:S(2)}) collective-permute-start(bf16[2,4,128,128]{3,2,1,0:T(8,128)(2,1)S(1)} %get-tuple-element.30.ko), channel_id=1, source_target_pairs={{0,1},{1,0},{2,3},{3,2},{4,5},{5,4},{6,7},{7,6},{8,9},{9,8},{10,11... | collective-permute-start | bytes 786440 | tf_op jit(solution)/shard_map/ppermute | solution.py:27
  17.4 3.3 %collective-permute-start.6 = (bf16[2,4,128,128]{3,2,1,0:T(8,128)(2,1)S(1)}, bf16[2,4,128,128]{3,2,1,0:T(8,128)(2,1)S(1)}, u32[]{:S(2)}, u32[]{:S(2)}) collective-permute-start(bf16[2,4,128,128]{3,2,1,0:T(8,128)(2,1)S(1)} %collective-permute-done.2.k1), channel_id=1, source_target_pairs={{0,1},{1,0},{2,3},{3,2},{4,5},{5,4},{6,7},{7,6},{8,9},{9,8},{10,11... | collective-permute-start | bytes 786440 | tf_op jit(solution)/shard_map/ppermute | solution.py:27
  20.7 2.5 %collective-permute-start.7 = (bf16[2,4,128,128]{3,2,1,0:T(8,128)(2,1)S(1)}, bf16[2,4,128,128]{3,2,1,0:T(8,128)(2,1)S(1)}, u32[]{:S(2)}, u32[]{:S(2)}) collective-permute-start(bf16[2,4,128,128]{3,2,1,0:T(8,128)(2,1)S(1)} %collective-permute-done.5.k2), channel_id=1, source_target_pairs={{0,1},{1,0},{2,3},{3,2},{4,5},{5,4},{6,7},{7,6},{8,9},{9,8},{10,11... | collective-permute-start | bytes 786440 | tf_op jit(solution)/shard_map/ppermute | solution.py:27
  26.2 3.6 %collective-permute-start.8 = (bf16[2,2,2,128,128]{4,3,2,1,0:T(8,128)(2,1)S(1)}, bf16[2,2,2,128,128]{4,3,2,1,0:T(8,128)(2,1)S(1)}, u32[]{:S(2)}, u32[]{:S(2)}) collective-permute-start(bf16[2,2,2,128,128]{4,3,2,1,0:T(8,128)(2,1)S(1)} %get-tuple-element.36), channel_id=1, source_target_pairs={{0,1},{1,0},{2,3},{3,2},{4,5},{5,4},{6,7},{7,6},{8,9},{9,8},{10,11... | collective-permute-start | bytes 786440 | tf_op jit(solution)/shard_map/ppermute | solution.py:27
  29.2 5.5 %collective-permute-start.10 = (bf16[2,2,2,128,128]{4,3,2,1,0:T(8,128)(2,1)S(1)}, bf16[2,2,2,128,128]{4,3,2,1,0:T(8,128)(2,1)S(1)}, u32[]{:S(2)}, u32[]{:S(2)}) collective-permute-start(bf16[2,2,2,128,128]{4,3,2,1,0:T(8,128)(2,1)S(1)} %get-tuple-element.40), channel_id=1, source_target_pairs={{0,1},{1,0},{2,3},{3,2},{4,5},{5,4},{6,7},{7,6},{8,9},{9,8},{10,11... | collective-permute-start | bytes 786440 | tf_op jit(solution)/shard_map/ppermute | solution.py:27
  29.8 10.6 %collective-permute-start.13 = (bf16[2,2,2,128,128]{4,3,2,1,0:T(8,128)(2,1)S(1)}, bf16[2,2,2,128,128]{4,3,2,1,0:T(8,128)(2,1)S(1)}, u32[]{:S(2)}, u32[]{:S(2)}) collective-permute-start(bf16[2,2,2,128,128]{4,3,2,1,0:T(8,128)(2,1)S(1)} %add_convert_fusion.3), channel_id=1, source_target_pairs={{0,28},{1,29},{2,30},{3,31},{4,0},{5,1},{6,2},{7,3},{8,4},{9,5},{1... | collective-permute-start | bytes 786440 | tf_op jit(solution)/shard_map/ppermute | solution.py:33
  34.7 5.8 %collective-permute-start.12 = (bf16[2,2,2,128,128]{4,3,2,1,0:T(8,128)(2,1)S(1)}, bf16[2,2,2,128,128]{4,3,2,1,0:T(8,128)(2,1)S(1)}, u32[]{:S(2)}, u32[]{:S(2)}) collective-permute-start(bf16[2,2,2,128,128]{4,3,2,1,0:T(8,128)(2,1)S(1)} %get-tuple-element.43), channel_id=1, source_target_pairs={{0,1},{1,0},{2,3},{3,2},{4,5},{5,4},{6,7},{7,6},{8,9},{9,8},{10,11... | collective-permute-start | bytes 786440 | tf_op jit(solution)/shard_map/ppermute | solution.py:27
  34.8 10.6 %collective-permute-start.15 = (bf16[2,2,2,128,128]{4,3,2,1,0:T(8,128)(2,1)S(1)}, bf16[2,2,2,128,128]{4,3,2,1,0:T(8,128)(2,1)S(1)}, u32[]{:S(2)}, u32[]{:S(2)}) collective-permute-start(bf16[2,2,2,128,128]{4,3,2,1,0:T(8,128)(2,1)S(1)} %add_convert_fusion.2), channel_id=1, source_target_pairs={{4,0},{5,1},{6,2},{7,3},{8,4},{9,5},{10,6},{11,7},{12,8},{13,9},{1... | collective-permute-start | bytes 786440 | tf_op jit(solution)/shard_map/ppermute | solution.py:33
  36.1 11.0 %collective-permute-start.11 = (bf16[4,128,128]{2,1,0:T(8,128)(2,1)S(1)}, bf16[4,128,128]{2,1,0:T(8,128)(2,1)S(1)}, u32[]{:S(2)}, u32[]{:S(2)}) collective-permute-start(bf16[4,128,128]{2,1,0:T(8,128)(2,1)S(1)} %get-tuple-element.41), channel_id=1, source_target_pairs={{0,2},{1,3},{2,0},{3,1},{4,6},{5,7},{6,4},{7,5},{8,10},{9,11},{10,... | collective-permute-start | bytes 393224 | tf_op jit(solution)/shard_map/ppermute | solution.py:27
  37.6 9.4 %collective-permute-start.9 = (bf16[4,128,128]{2,1,0:T(8,128)(2,1)S(1)}, bf16[4,128,128]{2,1,0:T(8,128)(2,1)S(1)}, u32[]{:S(2)}, u32[]{:S(2)}) collective-permute-start(bf16[4,128,128]{2,1,0:T(8,128)(2,1)S(1)} %get-tuple-element.37), channel_id=1, source_target_pairs={{0,2},{1,3},{2,0},{3,1},{4,6},{5,7},{6,4},{7,5},{8,10},{9,11},{10,... | collective-permute-start | bytes 393224 | tf_op jit(solution)/shard_map/ppermute | solution.py:27
  40.5 4.9 %collective-permute-start.14 = (bf16[2,2,2,128,128]{4,3,2,1,0:T(8,128)(2,1)S(1)}, bf16[2,2,2,128,128]{4,3,2,1,0:T(8,128)(2,1)S(1)}, u32[]{:S(2)}, u32[]{:S(2)}) collective-permute-start(bf16[2,2,2,128,128]{4,3,2,1,0:T(8,128)(2,1)S(1)} %get-tuple-element.46), channel_id=1, source_target_pairs={{0,1},{1,0},{2,3},{3,2},{4,5},{5,4},{6,7},{7,6},{8,9},{9,8},{10,11... | collective-permute-start | bytes 786440 | tf_op jit(solution)/shard_map/ppermute | solution.py:27
  40.6 8.4 %collective-permute-start.16 = (bf16[2,2,128,128]{3,2,1,0:T(8,128)(2,1)S(1)}, bf16[2,2,128,128]{3,2,1,0:T(8,128)(2,1)S(1)}, u32[]{:S(2)}, u32[]{:S(2)}) collective-permute-start(bf16[2,2,128,128]{3,2,1,0:T(8,128)(2,1)S(1)} %get-tuple-element.51), channel_id=1, source_target_pairs={{0,2},{1,3},{2,0},{3,1},{4,6},{5,7},{6,4},{7,5},{8,10},{9,11},{10,... | collective-permute-start | bytes 393224 | tf_op jit(solution)/shard_map/ppermute | solution.py:27
  45.5 5.2 %collective-permute-start.17 = (bf16[2,2,128,128]{3,2,1,0:T(8,128)(2,1)S(1)}, bf16[2,2,128,128]{3,2,1,0:T(8,128)(2,1)S(1)}, u32[]{:S(2)}, u32[]{:S(2)}) collective-permute-start(bf16[2,2,128,128]{3,2,1,0:T(8,128)(2,1)S(1)} %get-tuple-element.49), channel_id=1, source_target_pairs={{0,2},{1,3},{2,0},{3,1},{4,6},{5,7},{6,4},{7,5},{8,10},{9,11},{10,... | collective-permute-start | bytes 393224 | tf_op jit(solution)/shard_map/ppermute | solution.py:27

commit v3 on v2

--- a/solution.py
+++ b/solution.py
@@ -37,36 +37,10 @@
     return lax.optimization_barrier((a, *others))[0]
 
 
-def split_heads_kernel(place, *refs):
-    wide = refs[-1]
-    ins = [refs[0].at[0], refs[0].at[1]] if len(refs[0].shape) == 4 else refs[:2]
-    keep_ref, *sends = refs[1:-1] if len(refs[0].shape) == 4 else refs[2:-1]
-    tok, heads, width = ins[0].shape
-    half = heads // 2
-    part = half // len(sends)
-    x = place[0]
-    for s, ref in enumerate(ins):
-        wide[s] = ref[...].astype(jnp.float32).reshape(tok * heads, width)
-        for j in range(half):
-            low = wide[s, pl.ds(j, tok, stride=heads), :]
-            high = wide[s, pl.ds(half + j, tok, stride=heads), :]
-            keep_ref[s, j] = jnp.where(x == 0, low, high).astype(jnp.bfloat16)
-            sends[j // part][s, j % part] = jnp.where(x == 0, high, low).astype(jnp.bfloat16)
-
-
-def split_heads(place, chunks, *arrays):
-    tok, heads, width = arrays[0].shape[-3:]
-    shapes = [jax.ShapeDtypeStruct((2, heads // 2 // k, tok, width), jnp.bfloat16) for k in [1] + [chunks] * chunks]
-    vmem = pl.BlockSpec(memory_space=pltpu.VMEM)
-    return pl.pallas_call(
-        split_heads_kernel,
-        out_shape=tuple(shapes),
-        in_specs=[pl.BlockSpec(memory_space=pltpu.SMEM)] + [vmem] * len(arrays),
-        out_specs=(vmem,) * len(shapes),
-        scratch_shapes=[pltpu.VMEM((2, tok * heads, width), jnp.float32)],
-        compiler_params=pltpu.CompilerParams(vmem_limit_bytes=VMEM_LIMIT),
-        name="split_heads",
-    )(place, *arrays)
+def split_heads(x, a, b):
+    both = jnp.stack([a, b]).transpose(0, 2, 1, 3)
+    half = a.shape[1] // 2
+    return [lax.dynamic_slice_in_dim(both, half * side, half, 1) for side in (x, 1 - x)]
 
 
 def grads_kernel(
@@ -244,8 +218,8 @@
     bf, f32 = jnp.bfloat16, jnp.float32
     chunks = 2
 
-    kv_keep, kv_send = split_heads(place, 1, jnp.stack([keys, values]))
-    q_keep, q_send = split_heads(place, 1, queries, d_out)
+    kv_keep, kv_send = split_heads(x, keys, values)
+    q_keep, q_send = split_heads(x, queries, d_out)
     kv_x = swap(kv_send, 2)
     kv_1 = shift(kv_keep, quad, wrap=True)
     q_x = swap(q_send, 2)

time: 52.5 us -> 51.7 us (0.985)
  Pallas kernels: 11.4 us -> 9.36 us
  local copies, waits for them, and re-layouts: 0.05 us -> 1.44 us
    pallas_call x2 -> x0, Pallas kernels: 2.02 us -> none  [split_heads(): pl.pallas_call(split_heads_kernel, out_shape=tuple(shapes), in_specs=[pl....]
    another operation x0 -> x2, local copies, waits for them, and re-layouts: none -> 1.39 us  [split_heads(): both = jnp.stack([a, b]).transpose(0, 2, 1, 3)]
    another operation x3 -> x2, other arithmetic: 1.32 us -> 0.2 us  [the longest x1 1.14 us: body(): kv_keep, kv_send = split_heads(place, 1, jnp.stack([keys, values]))]
    dynamic_slice x0 -> x2, other arithmetic: none -> 0.95 us  [split_heads(): lax.dynamic_slice_in_dim(both, half * side, half, 1)]
  transfers between devices with their start and end apart: 18 -> 18, of which waited for: 6 -> 6; matrix products, arithmetic and copies ran while one was open for 1% -> 3% of each run, Pallas kernels for 12% -> 9%
where the time goes in v3:
time: 51.7 us; the launch traced here: 51.5 us
  starting transfers between devices  21.7 us (42%)
  waiting for transfers between devices  16.8 us (32%)
  Pallas kernels  9.36 us (18%)
  local copies, waits for them, and re-layouts  1.44 us (3%)
  other arithmetic  1.34 us (3%)
  between operations  0.83 us (2%)
    ppermute x4, starting transfers between devices, shift(): return lax.ppermute(a, 'ctx', pairs)  11.7 us
    ppermute x14, starting transfers between devices, swap(): return lax.ppermute(a, 'ctx', [(i, i ^ by) for i in range(n)])  10 us
    ppermute x4, waiting for transfers between devices, shift(): return lax.ppermute(a, 'ctx', pairs)  8.73 us
    ppermute x14, waiting for transfers between devices, swap(): return lax.ppermute(a, 'ctx', [(i, i ^ by) for i in range(n)])  8.09 us
    pallas_call x2, Pallas kernels, grads(): pl.pallas_call(functools.partial(grads_kernel, start, groups), out_shape=...  5.87 us
    pallas_call x2, Pallas kernels, join_heads(): pl.pallas_call(functools.partial(join_heads_kernel, count), out_shape=(ja...  3.49 us
    another operation x2, local copies, waits for them, and re-layouts, split_heads(): both = jnp.stack([a, b]).transpose(0, 2, 1, 3)  1.39 us
  transfers between devices with their start and end apart: 18, of which 6 were waited for; matrix products, arithmetic and copies ran while one was open for 3% of the time, Pallas kernels for 9%

profile of v3, /device:TPU:0, one launch (start us, length us, event | category | flops | bytes accessed | tf_op | source)
XLA Modules:
  0.0 51.5 jit_solution(10769289497496673789)
XLA Ops:
  0.7 1.1 %copy_bitcast_fusion.2 = (bf16[1,128,8,128]{3,1,2,0:T(8,128)(2,1)S(1)}, bf16[1,128,8,128]{3,1,2,0:T(8,128)(2,1)S(1)}) fusion(bf16[128,8,128]{2,1,0:T(8,128)(2,1)} %param.6, bf16[128,8,128]{2,1,0:T(8,128)(2,1)} %param.5), kind=kLoop, calls=%fused_computation.22 | loop fusion | bytes 1048576 | tf_op jit(solution)/shard_map/stack | solution.py:41
  1.8 0.0 copy-start
  1.8 0.0 copy-start.1
  1.8 0.1 fusion.5
  1.9 3.0 %collective-permute-start.1 = (bf16[2,4,128,128]{3,2,1,0:T(8,128)(2,1)S(1)}, bf16[2,4,128,128]{3,2,1,0:T(8,128)(2,1)S(1)}, u32[]{:S(2)}, u32[]{:S(2)}) collective-permute-start(bf16[2,4,128,128]{3,2,1,0:T(8,128)(2,1)S(1)} %get-tuple-element.43), channel_id=1, source_target_pairs={{0,2},{1,3},{2,0},{3,1},{4,6},{5,7},{6,4},{7,5},{8,10},{9,11},{10,... | collective-permute-start | bytes 786440 | tf_op jit(solution)/shard_map/ppermute | solution.py:27
  4.9 1.5 %collective-permute-start.2 = (bf16[2,4,128,128]{3,2,1,0:T(8,128)(2,1)S(1)}, bf16[2,4,128,128]{3,2,1,0:T(8,128)(2,1)S(1)}, u32[]{:S(2)}, u32[]{:S(2)}) collective-permute-start(bf16[2,4,128,128]{3,2,1,0:T(8,128)(2,1)S(1)} %get-tuple-element.22.ko), channel_id=1, source_target_pairs={{0,4},{1,5},{2,6},{3,7},{4,8},{5,9},{6,10},{7,11},{8,12},{9,13},{1... | collective-permute-start | bytes 786440 | tf_op jit(solution)/shard_map/ppermute | solution.py:33
  6.4 0.3 copy_bitcast_fusion
  6.7 0.9 %fusion.1 = (bf16[2,8,128,128]{3,2,1,0:T(8,128)(2,1)}, bf16[2,8,128,128]{3,2,1,0:T(8,128)(2,1)S(1)}) fusion(s32[]{:T(128)S(6)} %select_n.31, bf16[1,128,16,128]{3,1,2,0:T(8,128)(2,1)S(1)} %get-tuple-element.50, bf16[1,128,16,128]{3,1,2,0:T(8,128)(2,1)S(1)} %get-tuple-element.49, s32[]{:T(128)S(6)} %select_n.30), kind=kLoop, calls=%fused_computation.9 | loop fusion | flops 524288 | bytes 2097160 | tf_op jit(solution)/shard_map/dynamic_slice | solution.py:43
  7.6 0.5 %collective-permute-start = (bf16[2,8,128,128]{3,2,1,0:T(8,128)(2,1)}, bf16[2,8,128,128]{3,2,1,0:T(8,128)(2,1)S(1)}, u32[]{:S(2)}, u32[]{:S(2)}) collective-permute-start(bf16[2,8,128,128]{3,2,1,0:T(8,128)(2,1)} %get-tuple-element.41), channel_id=1, source_target_pairs={{0,2},{1,3},{2,0},{3,1},{4,6},{5,7},{6,4},{7,5},{8,10},{9,11},{10,... | collective-permute-start | bytes 1572872 | tf_op jit(solution)/shard_map/ppermute | solution.py:27
  8.1 3.9 %collective-permute-done.1.xo = bf16[2,4,128,128]{3,2,1,0:T(8,128)(2,1)S(1)} collective-permute-done((bf16[2,4,128,128]{3,2,1,0:T(8,128)(2,1)S(1)}, bf16[2,4,128,128]{3,2,1,0:T(8,128)(2,1)S(1)}, u32[]{:S(2)}, u32[]{:S(2)}) %collective-permute-start.1) | collective-permute-done | bytes 262176 | tf_op jit(solution)/shard_map/ppermute | solution.py:27
  12.0 4.0 %collective-permute-start.5 = (bf16[2,4,128,128]{3,2,1,0:T(8,128)(2,1)S(1)}, bf16[2,4,128,128]{3,2,1,0:T(8,128)(2,1)S(1)}, u32[]{:S(2)}, u32[]{:S(2)}) collective-permute-start(bf16[2,4,128,128]{3,2,1,0:T(8,128)(2,1)S(1)} %collective-permute-done.1.xo), channel_id=1, source_target_pairs={{0,4},{1,5},{2,6},{3,7},{4,8},{5,9},{6,10},{7,11},{8,12},{9,13},{1... | collective-permute-start | bytes 786440 | tf_op jit(solution)/shard_map/ppermute | solution.py:33
  16.0 0.0 collective-permute-done.2.k1
  16.0 0.1 collective-permute-start.4
  16.1 0.5 collective-permute-start.3
  16.6 0.1 collective-permute-start.6
  16.7 3.2 %collective-permute-done.5.k2 = bf16[2,4,128,128]{3,2,1,0:T(8,128)(2,1)S(1)} collective-permute-done((bf16[2,4,128,128]{3,2,1,0:T(8,128)(2,1)S(1)}, bf16[2,4,128,128]{3,2,1,0:T(8,128)(2,1)S(1)}, u32[]{:S(2)}, u32[]{:S(2)}) %collective-permute-start.5) | collective-permute-done | bytes 262176 | tf_op jit(solution)/shard_map/ppermute | solution.py:33
  19.9 0.0 collective-permute-start.7
  19.9 0.1 pad_add_fusion.place
  20.0 0.0 collective-permute-done.4.mxo
  20.0 0.0 collective-permute-done.3.mko
  20.0 2.5 %collective-permute-done.sent_q = bf16[2,8,128,128]{3,2,1,0:T(8,128)(2,1)S(1)} collective-permute-done((bf16[2,8,128,128]{3,2,1,0:T(8,128)(2,1)}, bf16[2,8,128,128]{3,2,1,0:T(8,128)(2,1)S(1)}, u32[]{:S(2)}, u32[]{:S(2)}) %collective-permute-start) | collective-permute-done | bytes 524320 | tf_op jit(solution)/shard_map/ppermute | solution.py:27
  22.4 0.0 collective-permute-done.6.mk1
  22.4 0.0 collective-permute-done.7.mk2
  22.4 2.9 %window_grads.2 = (bf16[4,128,128]{2,1,0:T(8,128)(2,1)S(1)}, bf16[4,128,128]{2,1,0:T(8,128)(2,1)S(1)}, f32[2,2,2,128,128]{4,3,2,1,0:T(8,128)S(1)}, bf16[2,2,2,12...) custom-call(s32[3]{0:T(128)S(1)} %pad_add_fusion.place, ...), custom_call_target="tpu_custom_call" | custom-call | flops 1 | bytes 1 | tf_op jit(solution)/shard_map/window_grads/pallas_call | solution.py:167
  25.4 0.1 collective-permute-start.8
  25.5 2.9 %window_grads.3 = (bf16[4,128,128]{2,1,0:T(8,128)(2,1)S(1)}, bf16[4,128,128]{2,1,0:T(8,128)(2,1)S(1)}, f32[2,2,2,128,128]{4,3,2,1,0:T(8,128)S(1)}, bf16[2,2,2,12...) custom-call(s32[3]{0:T(128)S(1)} %pad_add_fusion.place, ...), custom_call_target="tpu_custom_call" | custom-call | flops 1 | bytes 1 | tf_op jit(solution)/shard_map/window_grads/pallas_call | solution.py:167
  28.4 0.6 %collective-permute-start.10 = (bf16[2,2,2,128,128]{4,3,2,1,0:T(8,128)(2,1)S(1)}, bf16[2,2,2,128,128]{4,3,2,1,0:T(8,128)(2,1)S(1)}, u32[]{:S(2)}, u32[]{:S(2)}) collective-permute-start(bf16[2,2,2,128,128]{4,3,2,1,0:T(8,128)(2,1)S(1)} %get-tuple-element.32), channel_id=1, source_target_pairs={{0,1},{1,0},{2,3},{3,2},{4,5},{5,4},{6,7},{7,6},{8,9},{9,8},{10,11... | collective-permute-start | bytes 786440 | tf_op jit(solution)/shard_map/ppermute | solution.py:27
  29.0 0.0 collective-permute-done.8
  29.0 0.1 add_convert_fusion.3
  29.0 4.9 %collective-permute-start.13 = (bf16[2,2,2,128,128]{4,3,2,1,0:T(8,128)(2,1)S(1)}, bf16[2,2,2,128,128]{4,3,2,1,0:T(8,128)(2,1)S(1)}, u32[]{:S(2)}, u32[]{:S(2)}) collective-permute-start(bf16[2,2,2,128,128]{4,3,2,1,0:T(8,128)(2,1)S(1)} %add_convert_fusion.3), channel_id=1, source_target_pairs={{0,28},{1,29},{2,30},{3,31},{4,0},{5,1},{6,2},{7,3},{8,4},{9,5},{1... | collective-permute-start | bytes 786440 | tf_op jit(solution)/shard_map/ppermute | solution.py:33
  33.9 0.0 collective-permute-start.12
  33.9 0.1 add_convert_fusion.2
  34.0 1.3 %collective-permute-start.15 = (bf16[2,2,2,128,128]{4,3,2,1,0:T(8,128)(2,1)S(1)}, bf16[2,2,2,128,128]{4,3,2,1,0:T(8,128)(2,1)S(1)}, u32[]{:S(2)}, u32[]{:S(2)}) collective-permute-start(bf16[2,2,2,128,128]{4,3,2,1,0:T(8,128)(2,1)S(1)} %add_convert_fusion.2), channel_id=1, source_target_pairs={{4,0},{5,1},{6,2},{7,3},{8,4},{9,5},{10,6},{11,7},{12,8},{13,9},{1... | collective-permute-start | bytes 786440 | tf_op jit(solution)/shard_map/ppermute | solution.py:33
  35.3 1.6 %collective-permute-start.11 = (bf16[4,128,128]{2,1,0:T(8,128)(2,1)S(1)}, bf16[4,128,128]{2,1,0:T(8,128)(2,1)S(1)}, u32[]{:S(2)}, u32[]{:S(2)}) collective-permute-start(bf16[4,128,128]{2,1,0:T(8,128)(2,1)S(1)} %get-tuple-element.33), channel_id=1, source_target_pairs={{0,2},{1,3},{2,0},{3,1},{4,6},{5,7},{6,4},{7,5},{8,10},{9,11},{10,... | collective-permute-start | bytes 393224 | tf_op jit(solution)/shard_map/ppermute | solution.py:27
  36.8 0.5 %collective-permute-start.9 = (bf16[4,128,128]{2,1,0:T(8,128)(2,1)S(1)}, bf16[4,128,128]{2,1,0:T(8,128)(2,1)S(1)}, u32[]{:S(2)}, u32[]{:S(2)}) collective-permute-start(bf16[4,128,128]{2,1,0:T(8,128)(2,1)S(1)} %get-tuple-element.29), channel_id=1, source_target_pairs={{0,2},{1,3},{2,0},{3,1},{4,6},{5,7},{6,4},{7,5},{8,10},{9,11},{10,... | collective-permute-start | bytes 393224 | tf_op jit(solution)/shard_map/ppermute | solution.py:27
  37.3 2.3 %collective-permute-done.13 = bf16[2,2,2,128,128]{4,3,2,1,0:T(8,128)(2,1)S(1)} collective-permute-done((bf16[2,2,2,128,128]{4,3,2,1,0:T(8,128)(2,1)S(1)}, bf16[2,2,2,128,128]{4,3,2,1,0:T(8,128)(2,1)S(1)}, u32[]{:S(2)}, u32[]{:S(2)}) %collective-permute-start.13) | collective-permute-done | bytes 262176 | tf_op jit(solution)/shard_map/ppermute | solution.py:33
  39.6 0.0 collective-permute-start.14
  39.6 0.1 add_convert_fusion.1
  39.8 1.6 %collective-permute-start.16 = (bf16[2,2,128,128]{3,2,1,0:T(8,128)(2,1)S(1)}, bf16[2,2,128,128]{3,2,1,0:T(8,128)(2,1)S(1)}, u32[]{:S(2)}, u32[]{:S(2)}) collective-permute-start(bf16[2,2,128,128]{3,2,1,0:T(8,128)(2,1)S(1)} %get-tuple-element.47), channel_id=1, source_target_pairs={{0,2},{1,3},{2,0},{3,1},{4,6},{5,7},{6,4},{7,5},{8,10},{9,11},{10,... | collective-permute-start | bytes 393224 | tf_op jit(solution)/shard_map/ppermute | solution.py:27
  41.3 3.2 %collective-permute-done.15 = bf16[2,2,2,128,128]{4,3,2,1,0:T(8,128)(2,1)S(1)} collective-permute-done((bf16[2,2,2,128,128]{4,3,2,1,0:T(8,128)(2,1)S(1)}, bf16[2,2,2,128,128]{4,3,2,1,0:T(8,128)(2,1)S(1)}, u32[]{:S(2)}, u32[]{:S(2)}) %collective-permute-start.15) | collective-permute-done | bytes 262176 | tf_op jit(solution)/shard_map/ppermute | solution.py:33
  44.6 0.0 collective-permute-done.14
  44.6 0.1 add_convert_fusion
  44.7 1.6 %collective-permute-start.17 = (bf16[2,2,128,128]{3,2,1,0:T(8,128)(2,1)S(1)}, bf16[2,2,128,128]{3,2,1,0:T(8,128)(2,1)S(1)}, u32[]{:S(2)}, u32[]{:S(2)}) collective-permute-start(bf16[2,2,128,128]{3,2,1,0:T(8,128)(2,1)S(1)} %get-tuple-element.45), channel_id=1, source_target_pairs={{0,2},{1,3},{2,0},{3,1},{4,6},{5,7},{6,4},{7,5},{8,10},{9,11},{10,... | collective-permute-start | bytes 393224 | tf_op jit(solution)/shard_map/ppermute | solution.py:27
  46.3 0.0 collective-permute-done.11
  46.3 0.0 collective-permute-done.9
  46.3 1.9 %join_heads.2 = bf16[128,16,128]{2,1,0:T(8,128)(2,1)} custom-call(s32[3]{0:T(128)S(1)} %pad_add_fusion.place, bf16[1,4,128,128]{3,2,1,0:T(8,128)(2,1)S(1)} %bitcast.31, bf16[1,4,128,128]{3,2,1,0:T(8,128)(2,1)S(1)} %bitcast.32, bf16[1,4,128,128]{3,2,1,0:T(8,128)(2,1)S(1)} %bitcast.34, bf16[1,4,128,128]{3,2,1,0:T(8,128)(2,1)S(1)} %bitcast.33), custom_call_target="tpu_custom_call" | custom-call | tf_op jit(solution)/shard_map/join_heads/pallas_call | solution.py:200
  48.2 1.7 %collective-permute-done.17.refs_3_ = bf16[2,2,128,128]{3,2,1,0:T(8,128)(2,1)S(1)} collective-permute-done((bf16[2,2,128,128]{3,2,1,0:T(8,128)(2,1)S(1)}, bf16[2,2,128,128]{3,2,1,0:T(8,128)(2,1)S(1)}, u32[]{:S(2)}, u32[]{:S(2)}) %collective-permute-start.17) | collective-permute-done | bytes 131104 | tf_op jit(solution)/shard_map/ppermute | solution.py:27
  49.9 1.6 %join_heads.3 = (bf16[128,8,128]{2,1,0:T(8,128)(2,1)}, bf16[128,8,128]{2,1,0:T(8,128)(2,1)}) custom-call(s32[3]{0:T(128)S(1)} %pad_add_fusion.place, bf16[2,2,128,128]{3,2,1,0:T(8,128)(2,1)S(1)} %get-tuple-element.48.refs_0_, bf16[2,2,128,128]{3,2,1,0:T(8,128)(2,1)S(1)} %get-tuple-element.46.refs_1_, ...), custom_call_target="tpu_custom_call" | custom-call | tf_op jit(solution)/shard_map/join_heads/pallas_call | solution.py:200
  (7 shorter events, 0.1 us)
Async XLA Ops:
  1.8 4.6 %copy-start = (bf16[128,16,128]{2,1,0:T(8,128)(2,1)S(1)}, bf16[128,16,128]{2,1,0:T(8,128)(2,1)}, u32[]{:S(2)}) copy-start(bf16[128,16,128]{2,1,0:T(8,128)(2,1)} %param.7) | copy-start | bytes 1572868
  1.8 4.6 %copy-start.1 = (bf16[128,16,128]{2,1,0:T(8,128)(2,1)S(1)}, bf16[128,16,128]{2,1,0:T(8,128)(2,1)}, u32[]{:S(2)}) copy-start(bf16[128,16,128]{2,1,0:T(8,128)(2,1)} %param.4) | copy-start | bytes 1572868
  1.9 10.1 %collective-permute-start.1 = (bf16[2,4,128,128]{3,2,1,0:T(8,128)(2,1)S(1)}, bf16[2,4,128,128]{3,2,1,0:T(8,128)(2,1)S(1)}, u32[]{:S(2)}, u32[]{:S(2)}) collective-permute-start(bf16[2,4,128,128]{3,2,1,0:T(8,128)(2,1)S(1)} %get-tuple-element.43), channel_id=1, source_target_pairs={{0,2},{1,3},{2,0},{3,1},{4,6},{5,7},{6,4},{7,5},{8,10},{9,11},{10,... | collective-permute-start | bytes 786440 | tf_op jit(solution)/shard_map/ppermute | solution.py:27
  4.9 11.1 %collective-permute-start.2 = (bf16[2,4,128,128]{3,2,1,0:T(8,128)(2,1)S(1)}, bf16[2,4,128,128]{3,2,1,0:T(8,128)(2,1)S(1)}, u32[]{:S(2)}, u32[]{:S(2)}) collective-permute-start(bf16[2,4,128,128]{3,2,1,0:T(8,128)(2,1)S(1)} %get-tuple-element.22.ko), channel_id=1, source_target_pairs={{0,4},{1,5},{2,6},{3,7},{4,8},{5,9},{6,10},{7,11},{8,12},{9,13},{1... | collective-permute-start | bytes 786440 | tf_op jit(solution)/shard_map/ppermute | solution.py:33
  7.6 14.8 %collective-permute-start = (bf16[2,8,128,128]{3,2,1,0:T(8,128)(2,1)}, bf16[2,8,128,128]{3,2,1,0:T(8,128)(2,1)S(1)}, u32[]{:S(2)}, u32[]{:S(2)}) collective-permute-start(bf16[2,8,128,128]{3,2,1,0:T(8,128)(2,1)} %get-tuple-element.41), channel_id=1, source_target_pairs={{0,2},{1,3},{2,0},{3,1},{4,6},{5,7},{6,4},{7,5},{8,10},{9,11},{10,... | collective-permute-start | bytes 1572872 | tf_op jit(solution)/shard_map/ppermute | solution.py:27
  12.0 7.9 %collective-permute-start.5 = (bf16[2,4,128,128]{3,2,1,0:T(8,128)(2,1)S(1)}, bf16[2,4,128,128]{3,2,1,0:T(8,128)(2,1)S(1)}, u32[]{:S(2)}, u32[]{:S(2)}) collective-permute-start(bf16[2,4,128,128]{3,2,1,0:T(8,128)(2,1)S(1)} %collective-permute-done.1.xo), channel_id=1, source_target_pairs={{0,4},{1,5},{2,6},{3,7},{4,8},{5,9},{6,10},{7,11},{8,12},{9,13},{1... | collective-permute-start | bytes 786440 | tf_op jit(solution)/shard_map/ppermute | solution.py:33
  16.0 3.9 %collective-permute-start.4 = (bf16[2,4,128,128]{3,2,1,0:T(8,128)(2,1)S(1)}, bf16[2,4,128,128]{3,2,1,0:T(8,128)(2,1)S(1)}, u32[]{:S(2)}, u32[]{:S(2)}) collective-permute-start(bf16[2,4,128,128]{3,2,1,0:T(8,128)(2,1)S(1)} %collective-permute-done.1.xo), channel_id=1, source_target_pairs={{0,1},{1,0},{2,3},{3,2},{4,5},{5,4},{6,7},{7,6},{8,9},{9,8},{10,11... | collective-permute-start | bytes 786440 | tf_op jit(solution)/shard_map/ppermute | solution.py:27
  16.1 3.9 %collective-permute-start.3 = (bf16[2,4,128,128]{3,2,1,0:T(8,128)(2,1)S(1)}, bf16[2,4,128,128]{3,2,1,0:T(8,128)(2,1)S(1)}, u32[]{:S(2)}, u32[]{:S(2)}) collective-permute-start(bf16[2,4,128,128]{3,2,1,0:T(8,128)(2,1)S(1)} %get-tuple-element.22.ko), channel_id=1, source_target_pairs={{0,1},{1,0},{2,3},{3,2},{4,5},{5,4},{6,7},{7,6},{8,9},{9,8},{10,11... | collective-permute-start | bytes 786440 | tf_op jit(solution)/shard_map/ppermute | solution.py:27
  16.6 5.8 %collective-permute-start.6 = (bf16[2,4,128,128]{3,2,1,0:T(8,128)(2,1)S(1)}, bf16[2,4,128,128]{3,2,1,0:T(8,128)(2,1)S(1)}, u32[]{:S(2)}, u32[]{:S(2)}) collective-permute-start(bf16[2,4,128,128]{3,2,1,0:T(8,128)(2,1)S(1)} %collective-permute-done.2.k1), channel_id=1, source_target_pairs={{0,1},{1,0},{2,3},{3,2},{4,5},{5,4},{6,7},{7,6},{8,9},{9,8},{10,11... | collective-permute-start | bytes 786440 | tf_op jit(solution)/shard_map/ppermute | solution.py:27
  19.9 2.6 %collective-permute-start.7 = (bf16[2,4,128,128]{3,2,1,0:T(8,128)(2,1)S(1)}, bf16[2,4,128,128]{3,2,1,0:T(8,128)(2,1)S(1)}, u32[]{:S(2)}, u32[]{:S(2)}) collective-permute-start(bf16[2,4,128,128]{3,2,1,0:T(8,128)(2,1)S(1)} %collective-permute-done.5.k2), channel_id=1, source_target_pairs={{0,1},{1,0},{2,3},{3,2},{4,5},{5,4},{6,7},{7,6},{8,9},{9,8},{10,11... | collective-permute-start | bytes 786440 | tf_op jit(solution)/shard_map/ppermute | solution.py:27
  25.4 3.6 %collective-permute-start.8 = (bf16[2,2,2,128,128]{4,3,2,1,0:T(8,128)(2,1)S(1)}, bf16[2,2,2,128,128]{4,3,2,1,0:T(8,128)(2,1)S(1)}, u32[]{:S(2)}, u32[]{:S(2)}) collective-permute-start(bf16[2,2,2,128,128]{4,3,2,1,0:T(8,128)(2,1)S(1)} %get-tuple-element.28), channel_id=1, source_target_pairs={{0,1},{1,0},{2,3},{3,2},{4,5},{5,4},{6,7},{7,6},{8,9},{9,8},{10,11... | collective-permute-start | bytes 786440 | tf_op jit(solution)/shard_map/ppermute | solution.py:27
  28.4 5.5 %collective-permute-start.10 = (bf16[2,2,2,128,128]{4,3,2,1,0:T(8,128)(2,1)S(1)}, bf16[2,2,2,128,128]{4,3,2,1,0:T(8,128)(2,1)S(1)}, u32[]{:S(2)}, u32[]{:S(2)}) collective-permute-start(bf16[2,2,2,128,128]{4,3,2,1,0:T(8,128)(2,1)S(1)} %get-tuple-element.32), channel_id=1, source_target_pairs={{0,1},{1,0},{2,3},{3,2},{4,5},{5,4},{6,7},{7,6},{8,9},{9,8},{10,11... | collective-permute-start | bytes 786440 | tf_op jit(solution)/shard_map/ppermute | solution.py:27
  29.0 10.6 %collective-permute-start.13 = (bf16[2,2,2,128,128]{4,3,2,1,0:T(8,128)(2,1)S(1)}, bf16[2,2,2,128,128]{4,3,2,1,0:T(8,128)(2,1)S(1)}, u32[]{:S(2)}, u32[]{:S(2)}) collective-permute-start(bf16[2,2,2,128,128]{4,3,2,1,0:T(8,128)(2,1)S(1)} %add_convert_fusion.3), channel_id=1, source_target_pairs={{0,28},{1,29},{2,30},{3,31},{4,0},{5,1},{6,2},{7,3},{8,4},{9,5},{1... | collective-permute-start | bytes 786440 | tf_op jit(solution)/shard_map/ppermute | solution.py:33
  33.9 5.8 %collective-permute-start.12 = (bf16[2,2,2,128,128]{4,3,2,1,0:T(8,128)(2,1)S(1)}, bf16[2,2,2,128,128]{4,3,2,1,0:T(8,128)(2,1)S(1)}, u32[]{:S(2)}, u32[]{:S(2)}) collective-permute-start(bf16[2,2,2,128,128]{4,3,2,1,0:T(8,128)(2,1)S(1)} %get-tuple-element.35), channel_id=1, source_target_pairs={{0,1},{1,0},{2,3},{3,2},{4,5},{5,4},{6,7},{7,6},{8,9},{9,8},{10,11... | collective-permute-start | bytes 786440 | tf_op jit(solution)/shard_map/ppermute | solution.py:27
  34.0 10.6 %collective-permute-start.15 = (bf16[2,2,2,128,128]{4,3,2,1,0:T(8,128)(2,1)S(1)}, bf16[2,2,2,128,128]{4,3,2,1,0:T(8,128)(2,1)S(1)}, u32[]{:S(2)}, u32[]{:S(2)}) collective-permute-start(bf16[2,2,2,128,128]{4,3,2,1,0:T(8,128)(2,1)S(1)} %add_convert_fusion.2), channel_id=1, source_target_pairs={{4,0},{5,1},{6,2},{7,3},{8,4},{9,5},{10,6},{11,7},{12,8},{13,9},{1... | collective-permute-start | bytes 786440 | tf_op jit(solution)/shard_map/ppermute | solution.py:33
  35.3 11.0 %collective-permute-start.11 = (bf16[4,128,128]{2,1,0:T(8,128)(2,1)S(1)}, bf16[4,128,128]{2,1,0:T(8,128)(2,1)S(1)}, u32[]{:S(2)}, u32[]{:S(2)}) collective-permute-start(bf16[4,128,128]{2,1,0:T(8,128)(2,1)S(1)} %get-tuple-element.33), channel_id=1, source_target_pairs={{0,2},{1,3},{2,0},{3,1},{4,6},{5,7},{6,4},{7,5},{8,10},{9,11},{10,... | collective-permute-start | bytes 393224 | tf_op jit(solution)/shard_map/ppermute | solution.py:27
  36.8 9.5 %collective-permute-start.9 = (bf16[4,128,128]{2,1,0:T(8,128)(2,1)S(1)}, bf16[4,128,128]{2,1,0:T(8,128)(2,1)S(1)}, u32[]{:S(2)}, u32[]{:S(2)}) collective-permute-start(bf16[4,128,128]{2,1,0:T(8,128)(2,1)S(1)} %get-tuple-element.29), channel_id=1, source_target_pairs={{0,2},{1,3},{2,0},{3,1},{4,6},{5,7},{6,4},{7,5},{8,10},{9,11},{10,... | collective-permute-start | bytes 393224 | tf_op jit(solution)/shard_map/ppermute | solution.py:27
  39.6 4.9 %collective-permute-start.14 = (bf16[2,2,2,128,128]{4,3,2,1,0:T(8,128)(2,1)S(1)}, bf16[2,2,2,128,128]{4,3,2,1,0:T(8,128)(2,1)S(1)}, u32[]{:S(2)}, u32[]{:S(2)}) collective-permute-start(bf16[2,2,2,128,128]{4,3,2,1,0:T(8,128)(2,1)S(1)} %get-tuple-element.38), channel_id=1, source_target_pairs={{0,1},{1,0},{2,3},{3,2},{4,5},{5,4},{6,7},{7,6},{8,9},{9,8},{10,11... | collective-permute-start | bytes 786440 | tf_op jit(solution)/shard_map/ppermute | solution.py:27
  39.8 8.4 %collective-permute-start.16 = (bf16[2,2,128,128]{3,2,1,0:T(8,128)(2,1)S(1)}, bf16[2,2,128,128]{3,2,1,0:T(8,128)(2,1)S(1)}, u32[]{:S(2)}, u32[]{:S(2)}) collective-permute-start(bf16[2,2,128,128]{3,2,1,0:T(8,128)(2,1)S(1)} %get-tuple-element.47), channel_id=1, source_target_pairs={{0,2},{1,3},{2,0},{3,1},{4,6},{5,7},{6,4},{7,5},{8,10},{9,11},{10,... | collective-permute-start | bytes 393224 | tf_op jit(solution)/shard_map/ppermute | solution.py:27
  44.7 5.2 %collective-permute-start.17 = (bf16[2,2,128,128]{3,2,1,0:T(8,128)(2,1)S(1)}, bf16[2,2,128,128]{3,2,1,0:T(8,128)(2,1)S(1)}, u32[]{:S(2)}, u32[]{:S(2)}) collective-permute-start(bf16[2,2,128,128]{3,2,1,0:T(8,128)(2,1)S(1)} %get-tuple-element.45), channel_id=1, source_target_pairs={{0,2},{1,3},{2,0},{3,1},{4,6},{5,7},{6,4},{7,5},{8,10},{9,11},{10,... | collective-permute-start | bytes 393224 | tf_op jit(solution)/shard_map/ppermute | solution.py:27

commit v4 on v3

--- a/solution.py
+++ b/solution.py
@@ -1,4 +1,5 @@
 import functools
+import itertools
 import math
 
 import jax
@@ -44,10 +45,9 @@
 
 
 def grads_kernel(
-    start, groups, place, keep_q, sent_q, ko, xo, mko, mxo, k1, k2, mk1, mk2,
-    dq_keep, dq_send, prev_here, prev_mate, own_here, own_mate,
-    kv,
+    start, groups, place, keep_q, sent_q, ko, xo, mko, mxo, k1, k2, mk1, mk2, *rest
 ):
+    *done, dq_keep, dq_send, prev_here, prev_mate, own_here, own_mate, kv = rest
     _, all_groups, tok, width = ko.shape
     heads = keep_q.shape[1] // all_groups
     x, c, first = place[0], place[1], place[2]
@@ -61,6 +61,9 @@
         (ko, blocks + mine), (xo, blocks + other), (mko, blocks + mate_mine), (mxo, blocks + mate_other),
     ):
         kv[:, :, pl.ds(pl.multiple_of(slot * tok, tok), tok), :] = ref[:, start : start + groups]
+    first_head = start * heads if done else 0
+    for ref, out in zip(done, (dq_keep, dq_send)):
+        out[:first_head] = ref[...]
     rows = pl.ds(pl.multiple_of(c * tok, tok), reach)
     key = lax.broadcasted_iota(jnp.int32, (tok, heads * tok), 0)
     query = lax.broadcasted_iota(jnp.int32, (tok, heads * tok), 1) % tok
@@ -114,7 +117,7 @@
         for xx in range(2):
             win = slice(xx * 2 * tok, xx * 2 * tok + span)
             dqs.append((dot(kt[:, win], sides[xx][1], NN) * SCORE_SCALE).T.astype(jnp.bfloat16).reshape(heads, tok, width))
-        hs = pl.ds(g * heads, heads)
+        hs = pl.ds(first_head + g * heads, heads)
         dq_keep[hs] = jnp.where(x == 0, dqs[0], dqs[1])
         dq_send[hs] = jnp.where(x == 0, dqs[1], dqs[0])
         cut = span - 2 * tok
@@ -157,55 +160,64 @@
         sides.setdefault(g, []).append(weights(states[g], xx, *now))
     outputs(groups - 1, states[groups - 1], sides[groups - 1])
 
-def grads(start, groups, place, keep_q, sent_q, *kvs):
+def grads(start, groups, done, place, keep_q, sent_q, *kvs):
     _, all_groups, tok, width = kvs[0].shape
     heads = keep_q.shape[1] // all_groups
     bf, f32 = jnp.bfloat16, jnp.float32
-    dq_shape = jax.ShapeDtypeStruct((groups * heads, tok, width), bf)
+    dq_shape = jax.ShapeDtypeStruct(((groups + (start if done else 0)) * heads, tok, width), bf)
     dkv_shape = functools.partial(jax.ShapeDtypeStruct, (2, 2, groups, tok, width))
     vmem = pl.BlockSpec(memory_space=pltpu.VMEM)
     return pl.pallas_call(
         functools.partial(grads_kernel, start, groups),
         out_shape=(dq_shape, dq_shape, dkv_shape(f32), dkv_shape(bf), dkv_shape(f32), dkv_shape(bf)),
-        in_specs=[pl.BlockSpec(memory_space=pltpu.SMEM)] + [vmem] * 10,
+        in_specs=[pl.BlockSpec(memory_space=pltpu.SMEM)] + [vmem] * (10 + len(done)),
         out_specs=(vmem,) * 6,
         scratch_shapes=[pltpu.VMEM((2, groups, 2 * WINDOW, width), bf)],
         compiler_params=pltpu.CompilerParams(vmem_limit_bytes=VMEM_LIMIT),
         cost_estimate=pl.CostEstimate(flops=1, bytes_accessed=1, transcendentals=0),
         name="window_grads",
-    )(place, keep_q, sent_q, *kvs)
-
-
-def join_heads_kernel(count, place, *refs):
+    )(place, keep_q, sent_q, *kvs, *done)
+
+
+def join_heads_kernel(keeps, sents, count, place, *refs):
     outs, wide = refs[-1 - count : -1], refs[-1]
-    ins = refs[: -1 - count]
+    refs = refs[: -1 - count][::-1]
     tok, heads, width = outs[0].shape
     half = heads // 2
-    chunks = len(ins) // 2
-    part = half // chunks
     x = place[0]
+
+    def total(chunks, s, j):
+        part = half // len(chunks)
+        terms = [refs[n] for n in chunks[j // part]]
+        return sum(r[(s,) * (len(r.shape) - 3) + (j % part,)].astype(jnp.float32) for r in terms)
+
     for s, out in enumerate(outs):
         for j in range(half):
-            keep = ins[j // part][s, j % part].astype(jnp.float32)
-            sent = ins[chunks + j // part][s, j % part].astype(jnp.float32)
+            keep, sent = total(keeps, s, j), total(sents, s, j)
             wide[s, pl.ds(j, tok, stride=heads), :] = jnp.where(x == 0, keep, sent)
             wide[s, pl.ds(half + j, tok, stride=heads), :] = jnp.where(x == 0, sent, keep)
         out[...] = wide[s].reshape(tok, heads, width).astype(out.dtype)
 
 
 def join_heads(place, keeps, sents):
-    count, part, tok, width = keeps[0].shape
+    *lead, part, tok, width = keeps[0][0].shape
+    count = 2 if lead else 1
     heads = 2 * part * len(keeps)
+    numbers = itertools.count()
+    number = lambda chunks: [[next(numbers) for _ in terms] for terms in chunks]
     vmem = pl.BlockSpec(memory_space=pltpu.VMEM)
-    return pl.pallas_call(
-        functools.partial(join_heads_kernel, count),
-        out_shape=(jax.ShapeDtypeStruct((tok, heads, width), jnp.bfloat16),) * count,
-        in_specs=[pl.BlockSpec(memory_space=pltpu.SMEM)] + [vmem] * (2 * len(keeps)),
+    outs = (jax.ShapeDtypeStruct((tok, heads, width), jnp.bfloat16),) * count
+    arrays = [a for terms in keeps + sents for a in terms][::-1]
+    got = pl.pallas_call(
+        functools.partial(join_heads_kernel, number(keeps), number(sents), count),
+        out_shape=outs,
+        in_specs=[pl.BlockSpec(memory_space=pltpu.SMEM)] + [vmem] * len(arrays),
         out_specs=(vmem,) * count,
         scratch_shapes=[pltpu.VMEM((count, tok * heads, width), jnp.float32)],
         compiler_params=pltpu.CompilerParams(vmem_limit_bytes=VMEM_LIMIT),
         name="join_heads",
-    )(place, *keeps, *sents)
+    )(place, *arrays)
+    return got if count > 1 else got[0]
 
 
 def body(queries, keys, values, d_out):
@@ -228,23 +240,28 @@
     mates += [swap(kv_1, 1), swap(kv_2, 1)]
     per = kv_keep.shape[1] // chunks
 
-    dq_keep, dq_x, mine, dkv_x = [], [], [], []
+    sums, parts = [], []
+    dq = ()
     for i in range(chunks):
-        keep, send, prev_here, prev_mate, own_here, own_mate = grads(
-            i * per, per, place, q_keep, q_x,
+        *dq, prev_here, prev_mate, own_here, own_mate = grads(
+            i * per, per, tuple(dq), place, q_keep, q_x,
             kv_keep, kv_x, mates[0], mates[1], kv_1, kv_2, mates[2], mates[3],
         )
-        if i:
-            own_mate = after(own_mate, back)
-        prev_sum = (prev_here + swap(prev_mate, 1).astype(f32)).astype(bf)
-        back = shift(prev_sum, -quad, wrap=i + 1 < chunks)
-        own_sum = own_here + swap(own_mate, 1).astype(f32) + back.astype(f32)
-        dkv_x.append(swap(own_sum[1].astype(bf), 2))
-        mine.append(own_sum[0].astype(bf))
-        dq_keep.append(keep[None])
-        dq_x.append(swap(after(send, prev_sum), 2)[None])
-    (dq,) = join_heads(place, dq_keep, dq_x)
-    dk, dv = join_heads(place, mine, dkv_x)
+        sums.append((prev_here + swap(prev_mate, 1).astype(f32)).astype(bf))
+        parts.append(own_here + swap(own_mate, 1).astype(f32))
+    dq_x = swap(dq[1], 2)
+    back_a = shift(sums[0], -quad, wrap=True)
+    back_b2 = shift(sums[1][1], -quad)
+    back_b1 = shift(sums[1][0], -quad)
+    sum_a = parts[0] + back_a.astype(f32)
+    send_a = sum_a[1].astype(bf)
+    send_b = (parts[1][1] + after(back_b2, send_a).astype(f32)).astype(bf)
+    other_a = swap(send_a, 2)
+    other_b = swap(after(send_b, send_a, dq_x), 2)
+    dq = join_heads(place, [[dq[0]]], [[after(dq_x, back_b1)]])
+    dk, dv = join_heads(
+        place, [[sum_a[0].astype(bf)], [parts[1][0], back_b1]], [[other_a], [other_b]]
+    )
     return dq, dk, dv
 
 

time: 51.7 us -> 50.7 us (0.981)
  starting transfers between devices: 21.7 us -> 21 us
    ppermute x14 -> x13, starting transfers between devices: 10 us -> 8.26 us  [swap(): return lax.ppermute(a, 'ctx', [(i, i ^ by) for i in range(n)])]
    ppermute x4 -> x5, starting transfers between devices: 11.7 us -> 12.7 us  [shift(): return lax.ppermute(a, 'ctx', pairs)]
    ppermute x14 -> x13, waiting for transfers between devices: 8.09 us -> 7.72 us  [swap(): return lax.ppermute(a, 'ctx', [(i, i ^ by) for i in range(n)])]
    ppermute x4 -> x5, waiting for transfers between devices: 8.73 us -> 8.77 us  [shift(): return lax.ppermute(a, 'ctx', pairs)]
  transfers between devices with their start and end apart: 18 -> 18, of which waited for: 6 -> 7; matrix products, arithmetic and copies ran while one was open for 3% -> 3% of each run, Pallas kernels for 9% -> 10%
where the time goes in v4:
time: 50.7 us; the launch traced here: 50.5 us
  starting transfers between devices  21 us (41%)
  waiting for transfers between devices  16.5 us (33%)
  Pallas kernels  9.37 us (18%)
  local copies, waits for them, and re-layouts  1.46 us (3%)
  other arithmetic  1.34 us (3%)
  between operations  0.86 us (2%)
    ppermute x5, starting transfers between devices, shift(): return lax.ppermute(a, 'ctx', pairs)  12.7 us
    ppermute x5, waiting for transfers between devices, shift(): return lax.ppermute(a, 'ctx', pairs)  8.77 us
    ppermute x13, starting transfers between devices, swap(): return lax.ppermute(a, 'ctx', [(i, i ^ by) for i in range(n)])  8.26 us
    ppermute x13, waiting for transfers between devices, swap(): return lax.ppermute(a, 'ctx', [(i, i ^ by) for i in range(n)])  7.72 us
    pallas_call x2, Pallas kernels, grads(): pl.pallas_call(functools.partial(grads_kernel, start, groups), out_shape=...  5.87 us
    pallas_call x2, Pallas kernels, join_heads(): pl.pallas_call(functools.partial(join_heads_kernel, number(keeps), number...  3.5 us
    another operation x2, local copies, waits for them, and re-layouts, split_heads(): both = jnp.stack([a, b]).transpose(0, 2, 1, 3)  1.39 us
  transfers between devices with their start and end apart: 18, of which 7 were waited for; matrix products, arithmetic and copies ran while one was open for 3% of the time, Pallas kernels for 10%

profile of v4, /device:TPU:0, one launch (start us, length us, event | category | flops | bytes accessed | tf_op | source)
XLA Modules:
  0.0 50.5 jit_solution(6317853068722542362)
XLA Ops:
  0.7 1.1 %copy_bitcast_fusion.2 = (bf16[1,128,8,128]{3,1,2,0:T(8,128)(2,1)S(1)}, bf16[1,128,8,128]{3,1,2,0:T(8,128)(2,1)S(1)}) fusion(bf16[128,8,128]{2,1,0:T(8,128)(2,1)} %param.6, bf16[128,8,128]{2,1,0:T(8,128)(2,1)} %param.5), kind=kLoop, calls=%fused_computation.26 | loop fusion | bytes 1048576 | tf_op jit(solution)/shard_map/stack | solution.py:42
  1.8 0.0 copy-start
  1.8 0.0 copy-start.1
  1.8 0.1 fusion.5
  1.9 3.0 %collective-permute-start.1 = (bf16[2,4,128,128]{3,2,1,0:T(8,128)(2,1)S(1)}, bf16[2,4,128,128]{3,2,1,0:T(8,128)(2,1)S(1)}, u32[]{:S(2)}, u32[]{:S(2)}) collective-permute-start(bf16[2,4,128,128]{3,2,1,0:T(8,128)(2,1)S(1)} %get-tuple-element.43), channel_id=1, source_target_pairs={{0,2},{1,3},{2,0},{3,1},{4,6},{5,7},{6,4},{7,5},{8,10},{9,11},{10,... | collective-permute-start | bytes 786440 | tf_op jit(solution)/shard_map/ppermute | solution.py:28
  4.9 1.5 %collective-permute-start.2 = (bf16[2,4,128,128]{3,2,1,0:T(8,128)(2,1)S(1)}, bf16[2,4,128,128]{3,2,1,0:T(8,128)(2,1)S(1)}, u32[]{:S(2)}, u32[]{:S(2)}) collective-permute-start(bf16[2,4,128,128]{3,2,1,0:T(8,128)(2,1)S(1)} %get-tuple-element.22.ko), channel_id=1, source_target_pairs={{0,4},{1,5},{2,6},{3,7},{4,8},{5,9},{6,10},{7,11},{8,12},{9,13},{1... | collective-permute-start | bytes 786440 | tf_op jit(solution)/shard_map/ppermute | solution.py:34
  6.4 0.3 copy_bitcast_fusion
  6.7 0.9 %fusion.1 = (bf16[2,8,128,128]{3,2,1,0:T(8,128)(2,1)}, bf16[2,8,128,128]{3,2,1,0:T(8,128)(2,1)S(1)}) fusion(s32[]{:T(128)S(6)} %select_n.31, bf16[1,128,16,128]{3,1,2,0:T(8,128)(2,1)S(1)} %get-tuple-element.50, bf16[1,128,16,128]{3,1,2,0:T(8,128)(2,1)S(1)} %get-tuple-element.49, s32[]{:T(128)S(6)} %select_n.30), kind=kLoop, calls=%fused_computation.9 | loop fusion | flops 524288 | bytes 2097160 | tf_op jit(solution)/shard_map/dynamic_slice | solution.py:44
  7.6 0.5 %collective-permute-start = (bf16[2,8,128,128]{3,2,1,0:T(8,128)(2,1)}, bf16[2,8,128,128]{3,2,1,0:T(8,128)(2,1)S(1)}, u32[]{:S(2)}, u32[]{:S(2)}) collective-permute-start(bf16[2,8,128,128]{3,2,1,0:T(8,128)(2,1)} %get-tuple-element.41), channel_id=1, source_target_pairs={{0,2},{1,3},{2,0},{3,1},{4,6},{5,7},{6,4},{7,5},{8,10},{9,11},{10,... | collective-permute-start | bytes 1572872 | tf_op jit(solution)/shard_map/ppermute | solution.py:28
  8.1 3.9 %collective-permute-done.1.xo = bf16[2,4,128,128]{3,2,1,0:T(8,128)(2,1)S(1)} collective-permute-done((bf16[2,4,128,128]{3,2,1,0:T(8,128)(2,1)S(1)}, bf16[2,4,128,128]{3,2,1,0:T(8,128)(2,1)S(1)}, u32[]{:S(2)}, u32[]{:S(2)}) %collective-permute-start.1) | collective-permute-done | bytes 262176 | tf_op jit(solution)/shard_map/ppermute | solution.py:28
  12.0 4.0 %collective-permute-start.5 = (bf16[2,4,128,128]{3,2,1,0:T(8,128)(2,1)S(1)}, bf16[2,4,128,128]{3,2,1,0:T(8,128)(2,1)S(1)}, u32[]{:S(2)}, u32[]{:S(2)}) collective-permute-start(bf16[2,4,128,128]{3,2,1,0:T(8,128)(2,1)S(1)} %collective-permute-done.1.xo), channel_id=1, source_target_pairs={{0,4},{1,5},{2,6},{3,7},{4,8},{5,9},{6,10},{7,11},{8,12},{9,13},{1... | collective-permute-start | bytes 786440 | tf_op jit(solution)/shard_map/ppermute | solution.py:34
  16.0 0.0 collective-permute-done.2.k1
  16.0 0.1 collective-permute-start.4
  16.1 0.5 collective-permute-start.3
  16.6 0.1 collective-permute-start.6
  16.7 3.2 %collective-permute-done.5.k2 = bf16[2,4,128,128]{3,2,1,0:T(8,128)(2,1)S(1)} collective-permute-done((bf16[2,4,128,128]{3,2,1,0:T(8,128)(2,1)S(1)}, bf16[2,4,128,128]{3,2,1,0:T(8,128)(2,1)S(1)}, u32[]{:S(2)}, u32[]{:S(2)}) %collective-permute-start.5) | collective-permute-done | bytes 262176 | tf_op jit(solution)/shard_map/ppermute | solution.py:34
  19.9 0.0 collective-permute-start.7
  19.9 0.1 pad_add_fusion.place
  20.0 0.0 collective-permute-done.4.mxo
  20.0 0.0 collective-permute-done.3.mko
  20.0 2.5 %collective-permute-done.sent_q = bf16[2,8,128,128]{3,2,1,0:T(8,128)(2,1)S(1)} collective-permute-done((bf16[2,8,128,128]{3,2,1,0:T(8,128)(2,1)}, bf16[2,8,128,128]{3,2,1,0:T(8,128)(2,1)S(1)}, u32[]{:S(2)}, u32[]{:S(2)}) %collective-permute-start) | collective-permute-done | bytes 524320 | tf_op jit(solution)/shard_map/ppermute | solution.py:28
  22.4 0.0 collective-permute-done.6.mk1
  22.4 0.0 collective-permute-done.7.mk2
  22.4 2.9 %window_grads.2 = (bf16[4,128,128]{2,1,0:T(8,128)(2,1)S(1)}, bf16[4,128,128]{2,1,0:T(8,128)(2,1)S(1)}, f32[2,2,2,128,128]{4,3,2,1,0:T(8,128)S(1)}, bf16[2,2,2,12...) custom-call(s32[3]{0:T(128)S(1)} %pad_add_fusion.place, ...), custom_call_target="tpu_custom_call" | custom-call | flops 1 | bytes 1 | tf_op jit(solution)/shard_map/window_grads/pallas_call | solution.py:170
  25.4 0.1 collective-permute-start.14
  25.5 2.9 %window_grads.3 = (bf16[8,128,128]{2,1,0:T(8,128)(2,1)S(1)}, bf16[8,128,128]{2,1,0:T(8,128)(2,1)S(1)}, f32[2,2,2,128,128]{4,3,2,1,0:T(8,128)S(1)}, bf16[2,2,2,12...) custom-call(s32[3]{0:T(128)S(1)} %pad_add_fusion.place, ...), custom_call_target="tpu_custom_call" | custom-call | flops 1 | bytes 1 | tf_op jit(solution)/shard_map/window_grads/pallas_call | solution.py:170
  28.4 0.6 %collective-permute-start.9 = (bf16[2,2,2,128,128]{4,3,2,1,0:T(8,128)(2,1)S(1)}, bf16[2,2,2,128,128]{4,3,2,1,0:T(8,128)(2,1)S(1)}, u32[]{:S(2)}, u32[]{:S(2)}) collective-permute-start(bf16[2,2,2,128,128]{4,3,2,1,0:T(8,128)(2,1)S(1)} %get-tuple-element.28), channel_id=1, source_target_pairs={{0,1},{1,0},{2,3},{3,2},{4,5},{5,4},{6,7},{7,6},{8,9},{9,8},{10,11... | collective-permute-start | bytes 786440 | tf_op jit(solution)/shard_map/ppermute | solution.py:28
  29.0 0.1 collective-permute-start.13
  29.0 0.4 collective-permute-start.11
  29.5 1.7 %collective-permute-start.8 = (bf16[8,128,128]{2,1,0:T(8,128)(2,1)S(1)}, bf16[8,128,128]{2,1,0:T(8,128)(2,1)S(1)}, u32[]{:S(2)}, u32[]{:S(2)}) collective-permute-start(bf16[8,128,128]{2,1,0:T(8,128)(2,1)S(1)} %get-tuple-element.26), channel_id=1, source_target_pairs={{0,2},{1,3},{2,0},{3,1},{4,6},{5,7},{6,4},{7,5},{8,10},{9,11},{10,... | collective-permute-start | bytes 786440 | tf_op jit(solution)/shard_map/ppermute | solution.py:28
  31.2 0.0 collective-permute-done.14
  31.2 0.1 add_convert_fusion.1
  31.3 4.6 %collective-permute-start.15 = (bf16[2,2,2,128,128]{4,3,2,1,0:T(8,128)(2,1)S(1)}, bf16[2,2,2,128,128]{4,3,2,1,0:T(8,128)(2,1)S(1)}, u32[]{:S(2)}, u32[]{:S(2)}) collective-permute-start(bf16[2,2,2,128,128]{4,3,2,1,0:T(8,128)(2,1)S(1)} %add_convert_fusion.1), channel_id=1, source_target_pairs={{0,28},{1,29},{2,30},{3,31},{4,0},{5,1},{6,2},{7,3},{8,4},{9,5},{1... | collective-permute-start | bytes 786440 | tf_op jit(solution)/shard_map/ppermute | solution.py:34
  35.9 0.1 add_convert_fusion.2
  36.0 1.3 %collective-permute-start.12 = (bf16[2,2,128,128]{3,2,1,0:T(8,128)(2,1)S(1)}, bf16[2,2,128,128]{3,2,1,0:T(8,128)(2,1)S(1)}, u32[]{:S(2)}, u32[]{:S(2)}) collective-permute-start(bf16[2,2,128,128]{3,2,1,0:T(8,128)(2,1)S(1)} %get-tuple-element.47), channel_id=1, source_target_pairs={{4,0},{5,1},{6,2},{7,3},{8,4},{9,5},{10,6},{11,7},{12,8},{13,9},{1... | collective-permute-start | bytes 393224 | tf_op jit(solution)/shard_map/ppermute | solution.py:34
  37.3 0.0 collective-permute-done.11
  37.3 1.3 %collective-permute-start.10 = (bf16[2,2,128,128]{3,2,1,0:T(8,128)(2,1)S(1)}, bf16[2,2,128,128]{3,2,1,0:T(8,128)(2,1)S(1)}, u32[]{:S(2)}, u32[]{:S(2)}) collective-permute-start(bf16[2,2,128,128]{3,2,1,0:T(8,128)(2,1)S(1)} %get-tuple-element.48), channel_id=1, source_target_pairs={{4,0},{5,1},{6,2},{7,3},{8,4},{9,5},{10,6},{11,7},{12,8},{13,9},{1... | collective-permute-start | bytes 393224 | tf_op jit(solution)/shard_map/ppermute | solution.py:34
  38.6 0.1 convert_add_fusion
  38.7 2.7 %collective-permute-done.15 = bf16[2,2,2,128,128]{4,3,2,1,0:T(8,128)(2,1)S(1)} collective-permute-done((bf16[2,2,2,128,128]{4,3,2,1,0:T(8,128)(2,1)S(1)}, bf16[2,2,2,128,128]{4,3,2,1,0:T(8,128)(2,1)S(1)}, u32[]{:S(2)}, u32[]{:S(2)}) %collective-permute-start.15) | collective-permute-done | bytes 262176 | tf_op jit(solution)/shard_map/ppermute | solution.py:34
  41.4 0.1 add_convert_fusion
  41.6 0.6 %collective-permute-start.17 = (bf16[2,2,128,128]{3,2,1,0:T(8,128)(2,1)S(1)}, bf16[2,2,128,128]{3,2,1,0:T(8,128)(2,1)S(1)}, u32[]{:S(2)}, u32[]{:S(2)}) collective-permute-start(bf16[2,2,128,128]{3,2,1,0:T(8,128)(2,1)S(1)} %get-tuple-element.46), channel_id=1, source_target_pairs={{0,2},{1,3},{2,0},{3,1},{4,6},{5,7},{6,4},{7,5},{8,10},{9,11},{10,... | collective-permute-start | bytes 393224 | tf_op jit(solution)/shard_map/ppermute | solution.py:28
  42.2 1.7 %collective-permute-done.12 = bf16[2,2,128,128]{3,2,1,0:T(8,128)(2,1)S(1)} collective-permute-done((bf16[2,2,128,128]{3,2,1,0:T(8,128)(2,1)S(1)}, bf16[2,2,128,128]{3,2,1,0:T(8,128)(2,1)S(1)}, u32[]{:S(2)}, u32[]{:S(2)}) %collective-permute-start.12) | collective-permute-done | bytes 131104 | tf_op jit(solution)/shard_map/ppermute | solution.py:34
  43.9 0.0 collective-permute-done.8.refs_0_
  43.9 0.6 %collective-permute-start.16 = (bf16[2,2,128,128]{3,2,1,0:T(8,128)(2,1)S(1)}, bf16[2,2,128,128]{3,2,1,0:T(8,128)(2,1)S(1)}, u32[]{:S(2)}, u32[]{:S(2)}) collective-permute-start(bf16[2,2,128,128]{3,2,1,0:T(8,128)(2,1)S(1)} %fusion.9), channel_id=1, source_target_pairs={{0,2},{1,3},{2,0},{3,1},{4,6},{5,7},{6,4},{7,5},{8,10},{9,11},{10,... | collective-permute-start | bytes 393224 | tf_op jit(solution)/shard_map/ppermute | solution.py:28
  44.5 1.1 %collective-permute-done.10.refs_2_ = bf16[2,2,128,128]{3,2,1,0:T(8,128)(2,1)S(1)} collective-permute-done((bf16[2,2,128,128]{3,2,1,0:T(8,128)(2,1)S(1)}, bf16[2,2,128,128]{3,2,1,0:T(8,128)(2,1)S(1)}, u32[]{:S(2)}, u32[]{:S(2)}) %collective-permute-start.10) | collective-permute-done | bytes 131104 | tf_op jit(solution)/shard_map/ppermute | solution.py:34
  45.7 1.9 %join_heads.2 = bf16[128,16,128]{2,1,0:T(8,128)(2,1)} custom-call(s32[3]{0:T(128)S(1)} %pad_add_fusion.place, bf16[8,128,128]{2,1,0:T(8,128)(2,1)S(1)} %collective-permute-done.8.refs_0_, bf16[8,128,128]{2,1,0:T(8,128)(2,1)S(1)} %get-tuple-element.30.refs_1_), custom_call_target="tpu_custom_call" | custom-call | tf_op jit(solution)/shard_map/join_heads/pallas_call | solution.py:211
  47.6 1.3 %collective-permute-done.16.refs_0_ = bf16[2,2,128,128]{3,2,1,0:T(8,128)(2,1)S(1)} collective-permute-done((bf16[2,2,128,128]{3,2,1,0:T(8,128)(2,1)S(1)}, bf16[2,2,128,128]{3,2,1,0:T(8,128)(2,1)S(1)}, u32[]{:S(2)}, u32[]{:S(2)}) %collective-permute-start.16) | collective-permute-done | bytes 131104 | tf_op jit(solution)/shard_map/ppermute | solution.py:28
  48.9 1.6 %join_heads.3 = (bf16[128,8,128]{2,1,0:T(8,128)(2,1)}, bf16[128,8,128]{2,1,0:T(8,128)(2,1)}) custom-call(s32[3]{0:T(128)S(1)} %pad_add_fusion.place, bf16[2,2,128,128]{3,2,1,0:T(8,128)(2,1)S(1)} %collective-permute-done.16.refs_0_, bf16[2,2,128,128]{3,2,1,0:T(8,128)(2,1)S(1)} %collective-permute-done.17.refs_1_, ...), custom_call_target="tpu_custom_call" | custom-call | tf_op jit(solution)/shard_map/join_heads/pallas_call | solution.py:211
  (9 shorter events, 0.1 us)
Async XLA Ops:
  1.8 4.6 %copy-start = (bf16[128,16,128]{2,1,0:T(8,128)(2,1)S(1)}, bf16[128,16,128]{2,1,0:T(8,128)(2,1)}, u32[]{:S(2)}) copy-start(bf16[128,16,128]{2,1,0:T(8,128)(2,1)} %param.7) | copy-start | bytes 1572868
  1.8 4.6 %copy-start.1 = (bf16[128,16,128]{2,1,0:T(8,128)(2,1)S(1)}, bf16[128,16,128]{2,1,0:T(8,128)(2,1)}, u32[]{:S(2)}) copy-start(bf16[128,16,128]{2,1,0:T(8,128)(2,1)} %param.4) | copy-start | bytes 1572868
  1.9 10.1 %collective-permute-start.1 = (bf16[2,4,128,128]{3,2,1,0:T(8,128)(2,1)S(1)}, bf16[2,4,128,128]{3,2,1,0:T(8,128)(2,1)S(1)}, u32[]{:S(2)}, u32[]{:S(2)}) collective-permute-start(bf16[2,4,128,128]{3,2,1,0:T(8,128)(2,1)S(1)} %get-tuple-element.43), channel_id=1, source_target_pairs={{0,2},{1,3},{2,0},{3,1},{4,6},{5,7},{6,4},{7,5},{8,10},{9,11},{10,... | collective-permute-start | bytes 786440 | tf_op jit(solution)/shard_map/ppermute | solution.py:28
  4.9 11.1 %collective-permute-start.2 = (bf16[2,4,128,128]{3,2,1,0:T(8,128)(2,1)S(1)}, bf16[2,4,128,128]{3,2,1,0:T(8,128)(2,1)S(1)}, u32[]{:S(2)}, u32[]{:S(2)}) collective-permute-start(bf16[2,4,128,128]{3,2,1,0:T(8,128)(2,1)S(1)} %get-tuple-element.22.ko), channel_id=1, source_target_pairs={{0,4},{1,5},{2,6},{3,7},{4,8},{5,9},{6,10},{7,11},{8,12},{9,13},{1... | collective-permute-start | bytes 786440 | tf_op jit(solution)/shard_map/ppermute | solution.py:34
  7.6 14.8 %collective-permute-start = (bf16[2,8,128,128]{3,2,1,0:T(8,128)(2,1)}, bf16[2,8,128,128]{3,2,1,0:T(8,128)(2,1)S(1)}, u32[]{:S(2)}, u32[]{:S(2)}) collective-permute-start(bf16[2,8,128,128]{3,2,1,0:T(8,128)(2,1)} %get-tuple-element.41), channel_id=1, source_target_pairs={{0,2},{1,3},{2,0},{3,1},{4,6},{5,7},{6,4},{7,5},{8,10},{9,11},{10,... | collective-permute-start | bytes 1572872 | tf_op jit(solution)/shard_map/ppermute | solution.py:28
  12.0 7.9 %collective-permute-start.5 = (bf16[2,4,128,128]{3,2,1,0:T(8,128)(2,1)S(1)}, bf16[2,4,128,128]{3,2,1,0:T(8,128)(2,1)S(1)}, u32[]{:S(2)}, u32[]{:S(2)}) collective-permute-start(bf16[2,4,128,128]{3,2,1,0:T(8,128)(2,1)S(1)} %collective-permute-done.1.xo), channel_id=1, source_target_pairs={{0,4},{1,5},{2,6},{3,7},{4,8},{5,9},{6,10},{7,11},{8,12},{9,13},{1... | collective-permute-start | bytes 786440 | tf_op jit(solution)/shard_map/ppermute | solution.py:34
  16.0 3.9 %collective-permute-start.4 = (bf16[2,4,128,128]{3,2,1,0:T(8,128)(2,1)S(1)}, bf16[2,4,128,128]{3,2,1,0:T(8,128)(2,1)S(1)}, u32[]{:S(2)}, u32[]{:S(2)}) collective-permute-start(bf16[2,4,128,128]{3,2,1,0:T(8,128)(2,1)S(1)} %collective-permute-done.1.xo), channel_id=1, source_target_pairs={{0,1},{1,0},{2,3},{3,2},{4,5},{5,4},{6,7},{7,6},{8,9},{9,8},{10,11... | collective-permute-start | bytes 786440 | tf_op jit(solution)/shard_map/ppermute | solution.py:28
  16.1 3.9 %collective-permute-start.3 = (bf16[2,4,128,128]{3,2,1,0:T(8,128)(2,1)S(1)}, bf16[2,4,128,128]{3,2,1,0:T(8,128)(2,1)S(1)}, u32[]{:S(2)}, u32[]{:S(2)}) collective-permute-start(bf16[2,4,128,128]{3,2,1,0:T(8,128)(2,1)S(1)} %get-tuple-element.22.ko), channel_id=1, source_target_pairs={{0,1},{1,0},{2,3},{3,2},{4,5},{5,4},{6,7},{7,6},{8,9},{9,8},{10,11... | collective-permute-start | bytes 786440 | tf_op jit(solution)/shard_map/ppermute | solution.py:28
  16.6 5.8 %collective-permute-start.6 = (bf16[2,4,128,128]{3,2,1,0:T(8,128)(2,1)S(1)}, bf16[2,4,128,128]{3,2,1,0:T(8,128)(2,1)S(1)}, u32[]{:S(2)}, u32[]{:S(2)}) collective-permute-start(bf16[2,4,128,128]{3,2,1,0:T(8,128)(2,1)S(1)} %collective-permute-done.2.k1), channel_id=1, source_target_pairs={{0,1},{1,0},{2,3},{3,2},{4,5},{5,4},{6,7},{7,6},{8,9},{9,8},{10,11... | collective-permute-start | bytes 786440 | tf_op jit(solution)/shard_map/ppermute | solution.py:28
  19.9 2.6 %collective-permute-start.7 = (bf16[2,4,128,128]{3,2,1,0:T(8,128)(2,1)S(1)}, bf16[2,4,128,128]{3,2,1,0:T(8,128)(2,1)S(1)}, u32[]{:S(2)}, u32[]{:S(2)}) collective-permute-start(bf16[2,4,128,128]{3,2,1,0:T(8,128)(2,1)S(1)} %collective-permute-done.5.k2), channel_id=1, source_target_pairs={{0,1},{1,0},{2,3},{3,2},{4,5},{5,4},{6,7},{7,6},{8,9},{9,8},{10,11... | collective-permute-start | bytes 786440 | tf_op jit(solution)/shard_map/ppermute | solution.py:28
  25.4 5.8 %collective-permute-start.14 = (bf16[2,2,2,128,128]{4,3,2,1,0:T(8,128)(2,1)S(1)}, bf16[2,2,2,128,128]{4,3,2,1,0:T(8,128)(2,1)S(1)}, u32[]{:S(2)}, u32[]{:S(2)}) collective-permute-start(bf16[2,2,2,128,128]{4,3,2,1,0:T(8,128)(2,1)S(1)} %get-tuple-element.36), channel_id=1, source_target_pairs={{0,1},{1,0},{2,3},{3,2},{4,5},{5,4},{6,7},{7,6},{8,9},{9,8},{10,11... | collective-permute-start | bytes 786440 | tf_op jit(solution)/shard_map/ppermute | solution.py:28
  28.4 7.5 %collective-permute-start.9 = (bf16[2,2,2,128,128]{4,3,2,1,0:T(8,128)(2,1)S(1)}, bf16[2,2,2,128,128]{4,3,2,1,0:T(8,128)(2,1)S(1)}, u32[]{:S(2)}, u32[]{:S(2)}) collective-permute-start(bf16[2,2,2,128,128]{4,3,2,1,0:T(8,128)(2,1)S(1)} %get-tuple-element.28), channel_id=1, source_target_pairs={{0,1},{1,0},{2,3},{3,2},{4,5},{5,4},{6,7},{7,6},{8,9},{9,8},{10,11... | collective-permute-start | bytes 786440 | tf_op jit(solution)/shard_map/ppermute | solution.py:28
  29.0 9.7 %collective-permute-start.13 = (bf16[2,2,2,128,128]{4,3,2,1,0:T(8,128)(2,1)S(1)}, bf16[2,2,2,128,128]{4,3,2,1,0:T(8,128)(2,1)S(1)}, u32[]{:S(2)}, u32[]{:S(2)}) collective-permute-start(bf16[2,2,2,128,128]{4,3,2,1,0:T(8,128)(2,1)S(1)} %get-tuple-element.34), channel_id=1, source_target_pairs={{0,1},{1,0},{2,3},{3,2},{4,5},{5,4},{6,7},{7,6},{8,9},{9,8},{10,11... | collective-permute-start | bytes 786440 | tf_op jit(solution)/shard_map/ppermute | solution.py:28
  29.0 8.3 %collective-permute-start.11 = (bf16[2,2,2,128,128]{4,3,2,1,0:T(8,128)(2,1)S(1)}, bf16[2,2,2,128,128]{4,3,2,1,0:T(8,128)(2,1)S(1)}, u32[]{:S(2)}, u32[]{:S(2)}) collective-permute-start(bf16[2,2,2,128,128]{4,3,2,1,0:T(8,128)(2,1)S(1)} %get-tuple-element.32), channel_id=1, source_target_pairs={{0,1},{1,0},{2,3},{3,2},{4,5},{5,4},{6,7},{7,6},{8,9},{9,8},{10,11... | collective-permute-start | bytes 786440 | tf_op jit(solution)/shard_map/ppermute | solution.py:28
  29.5 14.4 %collective-permute-start.8 = (bf16[8,128,128]{2,1,0:T(8,128)(2,1)S(1)}, bf16[8,128,128]{2,1,0:T(8,128)(2,1)S(1)}, u32[]{:S(2)}, u32[]{:S(2)}) collective-permute-start(bf16[8,128,128]{2,1,0:T(8,128)(2,1)S(1)} %get-tuple-element.26), channel_id=1, source_target_pairs={{0,2},{1,3},{2,0},{3,1},{4,6},{5,7},{6,4},{7,5},{8,10},{9,11},{10,... | collective-permute-start | bytes 786440 | tf_op jit(solution)/shard_map/ppermute | solution.py:28
  31.3 10.1 %collective-permute-start.15 = (bf16[2,2,2,128,128]{4,3,2,1,0:T(8,128)(2,1)S(1)}, bf16[2,2,2,128,128]{4,3,2,1,0:T(8,128)(2,1)S(1)}, u32[]{:S(2)}, u32[]{:S(2)}) collective-permute-start(bf16[2,2,2,128,128]{4,3,2,1,0:T(8,128)(2,1)S(1)} %add_convert_fusion.1), channel_id=1, source_target_pairs={{0,28},{1,29},{2,30},{3,31},{4,0},{5,1},{6,2},{7,3},{8,4},{9,5},{1... | collective-permute-start | bytes 786440 | tf_op jit(solution)/shard_map/ppermute | solution.py:34
  36.0 7.9 %collective-permute-start.12 = (bf16[2,2,128,128]{3,2,1,0:T(8,128)(2,1)S(1)}, bf16[2,2,128,128]{3,2,1,0:T(8,128)(2,1)S(1)}, u32[]{:S(2)}, u32[]{:S(2)}) collective-permute-start(bf16[2,2,128,128]{3,2,1,0:T(8,128)(2,1)S(1)} %get-tuple-element.47), channel_id=1, source_target_pairs={{4,0},{5,1},{6,2},{7,3},{8,4},{9,5},{10,6},{11,7},{12,8},{13,9},{1... | collective-permute-start | bytes 393224 | tf_op jit(solution)/shard_map/ppermute | solution.py:34
  37.3 8.4 %collective-permute-start.10 = (bf16[2,2,128,128]{3,2,1,0:T(8,128)(2,1)S(1)}, bf16[2,2,128,128]{3,2,1,0:T(8,128)(2,1)S(1)}, u32[]{:S(2)}, u32[]{:S(2)}) collective-permute-start(bf16[2,2,128,128]{3,2,1,0:T(8,128)(2,1)S(1)} %get-tuple-element.48), channel_id=1, source_target_pairs={{4,0},{5,1},{6,2},{7,3},{8,4},{9,5},{10,6},{11,7},{12,8},{13,9},{1... | collective-permute-start | bytes 393224 | tf_op jit(solution)/shard_map/ppermute | solution.py:34
  41.6 7.4 %collective-permute-start.17 = (bf16[2,2,128,128]{3,2,1,0:T(8,128)(2,1)S(1)}, bf16[2,2,128,128]{3,2,1,0:T(8,128)(2,1)S(1)}, u32[]{:S(2)}, u32[]{:S(2)}) collective-permute-start(bf16[2,2,128,128]{3,2,1,0:T(8,128)(2,1)S(1)} %get-tuple-element.46), channel_id=1, source_target_pairs={{0,2},{1,3},{2,0},{3,1},{4,6},{5,7},{6,4},{7,5},{8,10},{9,11},{10,... | collective-permute-start | bytes 393224 | tf_op jit(solution)/shard_map/ppermute | solution.py:28
  43.9 5.0 %collective-permute-start.16 = (bf16[2,2,128,128]{3,2,1,0:T(8,128)(2,1)S(1)}, bf16[2,2,128,128]{3,2,1,0:T(8,128)(2,1)S(1)}, u32[]{:S(2)}, u32[]{:S(2)}) collective-permute-start(bf16[2,2,128,128]{3,2,1,0:T(8,128)(2,1)S(1)} %fusion.9), channel_id=1, source_target_pairs={{0,2},{1,3},{2,0},{3,1},{4,6},{5,7},{6,4},{7,5},{8,10},{9,11},{10,... | collective-permute-start | bytes 393224 | tf_op jit(solution)/shard_map/ppermute | solution.py:28

commit v5 on v4

--- a/solution.py
+++ b/solution.py
@@ -248,16 +248,17 @@
             kv_keep, kv_x, mates[0], mates[1], kv_1, kv_2, mates[2], mates[3],
         )
         sums.append((prev_here + swap(prev_mate, 1).astype(f32)).astype(bf))
-        parts.append(own_here + swap(own_mate, 1).astype(f32))
-    dq_x = swap(dq[1], 2)
-    back_a = shift(sums[0], -quad, wrap=True)
+        parts.append((own_here, own_mate))
+    parts = [here + swap(after(mate, sums[0]), 1).astype(f32) for here, mate in parts]
+    dq_x = swap(after(dq[1], sums[0]), 2)
+    back_a = shift(sums[0], -quad)
     back_b2 = shift(sums[1][1], -quad)
     back_b1 = shift(sums[1][0], -quad)
     sum_a = parts[0] + back_a.astype(f32)
     send_a = sum_a[1].astype(bf)
     send_b = (parts[1][1] + after(back_b2, send_a).astype(f32)).astype(bf)
-    other_a = swap(send_a, 2)
-    other_b = swap(after(send_b, send_a, dq_x), 2)
+    other_a = swap(after(send_a, dq_x), 2)
+    other_b = swap(after(send_b, send_a), 2)
     dq = join_heads(place, [[dq[0]]], [[after(dq_x, back_b1)]])
     dk, dv = join_heads(
         place, [[sum_a[0].astype(bf)], [parts[1][0], back_b1]], [[other_a], [other_b]]

time: 50.7 us -> 49.9 us (0.984)
  starting transfers between devices: 21 us -> 19.9 us
    ppermute x5, starting transfers between devices: 12.7 us -> 9.38 us  [shift(): return lax.ppermute(a, 'ctx', pairs)]
    ppermute x13, starting transfers between devices: 8.26 us -> 10.5 us  [swap(): return lax.ppermute(a, 'ctx', [(i, i ^ by) for i in range(n)])]
  transfers between devices with their start and end apart: 18 -> 18, of which waited for: 7 -> 6; matrix products, arithmetic and copies ran while one was open for 3% -> 3% of each run, Pallas kernels for 10% -> 10%
where the time goes in v5:
time: 49.9 us; the launch traced here: 49.6 us
  starting transfers between devices  19.9 us (40%)
  waiting for transfers between devices  16.7 us (33%)
  Pallas kernels  9.37 us (19%)
  local copies, waits for them, and re-layouts  1.46 us (3%)
  other arithmetic  1.33 us (3%)
  between operations  0.87 us (2%)
    ppermute x13, starting transfers between devices, swap(): return lax.ppermute(a, 'ctx', [(i, i ^ by) for i in range(n)])  10.5 us
    ppermute x5, starting transfers between devices, shift(): return lax.ppermute(a, 'ctx', pairs)  9.38 us
    ppermute x5, waiting for transfers between devices, shift(): return lax.ppermute(a, 'ctx', pairs)  9.02 us
    ppermute x13, waiting for transfers between devices, swap(): return lax.ppermute(a, 'ctx', [(i, i ^ by) for i in range(n)])  7.67 us
    pallas_call x2, Pallas kernels, grads(): pl.pallas_call(functools.partial(grads_kernel, start, groups), out_shape=...  5.87 us
    pallas_call x2, Pallas kernels, join_heads(): pl.pallas_call(functools.partial(join_heads_kernel, number(keeps), number...  3.5 us
    another operation x2, local copies, waits for them, and re-layouts, split_heads(): both = jnp.stack([a, b]).transpose(0, 2, 1, 3)  1.39 us
  transfers between devices with their start and end apart: 18, of which 6 were waited for; matrix products, arithmetic and copies ran while one was open for 3% of the time, Pallas kernels for 10%

profile of v5, /device:TPU:0, one launch (start us, length us, event | category | flops | bytes accessed | tf_op | source)
XLA Modules:
  0.0 49.6 jit_solution(16042561479048239394)
XLA Ops:
  0.7 1.1 %copy_bitcast_fusion.2 = (bf16[1,128,8,128]{3,1,2,0:T(8,128)(2,1)S(1)}, bf16[1,128,8,128]{3,1,2,0:T(8,128)(2,1)S(1)}) fusion(bf16[128,8,128]{2,1,0:T(8,128)(2,1)} %param.6, bf16[128,8,128]{2,1,0:T(8,128)(2,1)} %param.5), kind=kLoop, calls=%fused_computation.26 | loop fusion | bytes 1048576 | tf_op jit(solution)/shard_map/stack | solution.py:42
  1.8 0.0 copy-start
  1.8 0.0 copy-start.1
  1.8 0.1 fusion.5
  1.9 3.0 %collective-permute-start.1 = (bf16[2,4,128,128]{3,2,1,0:T(8,128)(2,1)S(1)}, bf16[2,4,128,128]{3,2,1,0:T(8,128)(2,1)S(1)}, u32[]{:S(2)}, u32[]{:S(2)}) collective-permute-start(bf16[2,4,128,128]{3,2,1,0:T(8,128)(2,1)S(1)} %get-tuple-element.51), channel_id=1, source_target_pairs={{0,2},{1,3},{2,0},{3,1},{4,6},{5,7},{6,4},{7,5},{8,10},{9,11},{10,... | collective-permute-start | bytes 786440 | tf_op jit(solution)/shard_map/ppermute | solution.py:28
  4.9 1.5 %collective-permute-start.2 = (bf16[2,4,128,128]{3,2,1,0:T(8,128)(2,1)S(1)}, bf16[2,4,128,128]{3,2,1,0:T(8,128)(2,1)S(1)}, u32[]{:S(2)}, u32[]{:S(2)}) collective-permute-start(bf16[2,4,128,128]{3,2,1,0:T(8,128)(2,1)S(1)} %get-tuple-element.26.ko), channel_id=1, source_target_pairs={{0,4},{1,5},{2,6},{3,7},{4,8},{5,9},{6,10},{7,11},{8,12},{9,13},{1... | collective-permute-start | bytes 786440 | tf_op jit(solution)/shard_map/ppermute | solution.py:34
  6.4 0.3 copy_bitcast_fusion
  6.7 0.9 %fusion.1 = (bf16[2,8,128,128]{3,2,1,0:T(8,128)(2,1)}, bf16[2,8,128,128]{3,2,1,0:T(8,128)(2,1)S(1)}) fusion(s32[]{:T(128)S(6)} %select_n.31, bf16[1,128,16,128]{3,1,2,0:T(8,128)(2,1)S(1)} %get-tuple-element.58, bf16[1,128,16,128]{3,1,2,0:T(8,128)(2,1)S(1)} %get-tuple-element.57, s32[]{:T(128)S(6)} %select_n.30), kind=kLoop, calls=%fused_computation.9 | loop fusion | flops 524288 | bytes 2097160 | tf_op jit(solution)/shard_map/dynamic_slice | solution.py:44
  7.6 0.5 %collective-permute-start = (bf16[2,8,128,128]{3,2,1,0:T(8,128)(2,1)}, bf16[2,8,128,128]{3,2,1,0:T(8,128)(2,1)S(1)}, u32[]{:S(2)}, u32[]{:S(2)}) collective-permute-start(bf16[2,8,128,128]{3,2,1,0:T(8,128)(2,1)} %get-tuple-element.49), channel_id=1, source_target_pairs={{0,2},{1,3},{2,0},{3,1},{4,6},{5,7},{6,4},{7,5},{8,10},{9,11},{10,... | collective-permute-start | bytes 1572872 | tf_op jit(solution)/shard_map/ppermute | solution.py:28
  8.1 3.9 %collective-permute-done.1.xo = bf16[2,4,128,128]{3,2,1,0:T(8,128)(2,1)S(1)} collective-permute-done((bf16[2,4,128,128]{3,2,1,0:T(8,128)(2,1)S(1)}, bf16[2,4,128,128]{3,2,1,0:T(8,128)(2,1)S(1)}, u32[]{:S(2)}, u32[]{:S(2)}) %collective-permute-start.1) | collective-permute-done | bytes 262176 | tf_op jit(solution)/shard_map/ppermute | solution.py:28
  12.0 4.0 %collective-permute-start.5 = (bf16[2,4,128,128]{3,2,1,0:T(8,128)(2,1)S(1)}, bf16[2,4,128,128]{3,2,1,0:T(8,128)(2,1)S(1)}, u32[]{:S(2)}, u32[]{:S(2)}) collective-permute-start(bf16[2,4,128,128]{3,2,1,0:T(8,128)(2,1)S(1)} %collective-permute-done.1.xo), channel_id=1, source_target_pairs={{0,4},{1,5},{2,6},{3,7},{4,8},{5,9},{6,10},{7,11},{8,12},{9,13},{1... | collective-permute-start | bytes 786440 | tf_op jit(solution)/shard_map/ppermute | solution.py:34
  16.0 0.0 collective-permute-done.2.k1
  16.0 0.1 collective-permute-start.4
  16.1 0.5 %collective-permute-start.3 = (bf16[2,4,128,128]{3,2,1,0:T(8,128)(2,1)S(1)}, bf16[2,4,128,128]{3,2,1,0:T(8,128)(2,1)S(1)}, u32[]{:S(2)}, u32[]{:S(2)}) collective-permute-start(bf16[2,4,128,128]{3,2,1,0:T(8,128)(2,1)S(1)} %get-tuple-element.26.ko), channel_id=1, source_target_pairs={{0,1},{1,0},{2,3},{3,2},{4,5},{5,4},{6,7},{7,6},{8,9},{9,8},{10,11... | collective-permute-start | bytes 786440 | tf_op jit(solution)/shard_map/ppermute | solution.py:28
  16.6 0.1 collective-permute-start.6
  16.7 3.2 %collective-permute-done.5.k2 = bf16[2,4,128,128]{3,2,1,0:T(8,128)(2,1)S(1)} collective-permute-done((bf16[2,4,128,128]{3,2,1,0:T(8,128)(2,1)S(1)}, bf16[2,4,128,128]{3,2,1,0:T(8,128)(2,1)S(1)}, u32[]{:S(2)}, u32[]{:S(2)}) %collective-permute-start.5) | collective-permute-done | bytes 262176 | tf_op jit(solution)/shard_map/ppermute | solution.py:34
  19.9 0.0 collective-permute-start.7
  19.9 0.1 pad_add_fusion.place
  20.0 0.0 collective-permute-done.4.mxo
  20.0 0.0 collective-permute-done.3.mko
  20.0 2.5 %collective-permute-done.sent_q = bf16[2,8,128,128]{3,2,1,0:T(8,128)(2,1)S(1)} collective-permute-done((bf16[2,8,128,128]{3,2,1,0:T(8,128)(2,1)}, bf16[2,8,128,128]{3,2,1,0:T(8,128)(2,1)S(1)}, u32[]{:S(2)}, u32[]{:S(2)}) %collective-permute-start) | collective-permute-done | bytes 524320 | tf_op jit(solution)/shard_map/ppermute | solution.py:28
  22.4 0.0 collective-permute-done.6.mk1
  22.4 0.0 collective-permute-done.7.mk2
  22.4 2.9 %window_grads.2 = (bf16[4,128,128]{2,1,0:T(8,128)(2,1)S(1)}, bf16[4,128,128]{2,1,0:T(8,128)(2,1)S(1)}, f32[2,2,2,128,128]{4,3,2,1,0:T(8,128)S(1)}, bf16[2,2,2,12...) custom-call(s32[3]{0:T(128)S(1)} %pad_add_fusion.place, ...), custom_call_target="tpu_custom_call" | custom-call | flops 1 | bytes 1 | tf_op jit(solution)/shard_map/window_grads/pallas_call | solution.py:170
  25.4 0.1 collective-permute-start.8
  25.5 2.9 %window_grads.3 = (bf16[8,128,128]{2,1,0:T(8,128)(2,1)S(1)}, bf16[8,128,128]{2,1,0:T(8,128)(2,1)S(1)}, f32[2,2,2,128,128]{4,3,2,1,0:T(8,128)S(1)}, bf16[2,2,2,12...) custom-call(s32[3]{0:T(128)S(1)} %pad_add_fusion.place, ...), custom_call_target="tpu_custom_call" | custom-call | flops 1 | bytes 1 | tf_op jit(solution)/shard_map/window_grads/pallas_call | solution.py:170
  28.4 0.6 %collective-permute-start.10 = (bf16[2,2,2,128,128]{4,3,2,1,0:T(8,128)(2,1)S(1)}, bf16[2,2,2,128,128]{4,3,2,1,0:T(8,128)(2,1)S(1)}, u32[]{:S(2)}, u32[]{:S(2)}) collective-permute-start(bf16[2,2,2,128,128]{4,3,2,1,0:T(8,128)(2,1)S(1)} %get-tuple-element.35), channel_id=1, source_target_pairs={{0,1},{1,0},{2,3},{3,2},{4,5},{5,4},{6,7},{7,6},{8,9},{9,8},{10,11... | collective-permute-start | bytes 786440 | tf_op jit(solution)/shard_map/ppermute | solution.py:28
  29.0 0.0 collective-permute-done.8
  29.0 0.1 add_convert_fusion.2
  29.0 1.3 %collective-permute-start.15 = (bf16[2,2,2,128,128]{4,3,2,1,0:T(8,128)(2,1)S(1)}, bf16[2,2,2,128,128]{4,3,2,1,0:T(8,128)(2,1)S(1)}, u32[]{:S(2)}, u32[]{:S(2)}) collective-permute-start(bf16[2,2,2,128,128]{4,3,2,1,0:T(8,128)(2,1)S(1)} %add_convert_fusion.2), channel_id=1, source_target_pairs={{4,0},{5,1},{6,2},{7,3},{8,4},{9,5},{10,6},{11,7},{12,8},{13,9},{1... | collective-permute-start | bytes 786440 | tf_op jit(solution)/shard_map/ppermute | solution.py:34
  30.3 0.1 collective-permute-start.14
  30.4 1.8 %collective-permute-start.9 = (bf16[8,128,128]{2,1,0:T(8,128)(2,1)S(1)}, bf16[8,128,128]{2,1,0:T(8,128)(2,1)S(1)}, u32[]{:S(2)}, u32[]{:S(2)}) collective-permute-start(bf16[8,128,128]{2,1,0:T(8,128)(2,1)S(1)} %get-tuple-element.33), channel_id=1, source_target_pairs={{0,2},{1,3},{2,0},{3,1},{4,6},{5,7},{6,4},{7,5},{8,10},{9,11},{10,... | collective-permute-start | bytes 786440 | tf_op jit(solution)/shard_map/ppermute | solution.py:28
  32.2 0.0 collective-permute-done.10
  32.2 0.1 add_convert_fusion.1
  32.3 1.3 %collective-permute-start.13 = (bf16[2,2,128,128]{3,2,1,0:T(8,128)(2,1)S(1)}, bf16[2,2,128,128]{3,2,1,0:T(8,128)(2,1)S(1)}, u32[]{:S(2)}, u32[]{:S(2)}) collective-permute-start(bf16[2,2,128,128]{3,2,1,0:T(8,128)(2,1)S(1)} %get-tuple-element.55), channel_id=1, source_target_pairs={{4,0},{5,1},{6,2},{7,3},{8,4},{9,5},{10,6},{11,7},{12,8},{13,9},{1... | collective-permute-start | bytes 393224 | tf_op jit(solution)/shard_map/ppermute | solution.py:34
  33.6 0.2 collective-permute-start.12
  33.9 0.0 collective-permute-done.14
  33.9 1.3 %collective-permute-start.11 = (bf16[2,2,128,128]{3,2,1,0:T(8,128)(2,1)S(1)}, bf16[2,2,128,128]{3,2,1,0:T(8,128)(2,1)S(1)}, u32[]{:S(2)}, u32[]{:S(2)}) collective-permute-start(bf16[2,2,128,128]{3,2,1,0:T(8,128)(2,1)S(1)} %get-tuple-element.56), channel_id=1, source_target_pairs={{4,0},{5,1},{6,2},{7,3},{8,4},{9,5},{10,6},{11,7},{12,8},{13,9},{1... | collective-permute-start | bytes 393224 | tf_op jit(solution)/shard_map/ppermute | solution.py:34
  35.1 4.9 %collective-permute-done.15 = bf16[2,2,2,128,128]{4,3,2,1,0:T(8,128)(2,1)S(1)} collective-permute-done((bf16[2,2,2,128,128]{4,3,2,1,0:T(8,128)(2,1)S(1)}, bf16[2,2,2,128,128]{4,3,2,1,0:T(8,128)(2,1)S(1)}, u32[]{:S(2)}, u32[]{:S(2)}) %collective-permute-start.15) | collective-permute-done | bytes 262176 | tf_op jit(solution)/shard_map/ppermute | solution.py:34
  40.1 0.1 add_convert_fusion
  40.2 0.0 collective-permute-done.9.refs_0_
  40.2 1.8 %collective-permute-start.17 = (bf16[2,2,128,128]{3,2,1,0:T(8,128)(2,1)S(1)}, bf16[2,2,128,128]{3,2,1,0:T(8,128)(2,1)S(1)}, u32[]{:S(2)}, u32[]{:S(2)}) collective-permute-start(bf16[2,2,128,128]{3,2,1,0:T(8,128)(2,1)S(1)} %get-tuple-element.46), channel_id=1, source_target_pairs={{0,2},{1,3},{2,0},{3,1},{4,6},{5,7},{6,4},{7,5},{8,10},{9,11},{10,... | collective-permute-start | bytes 393224 | tf_op jit(solution)/shard_map/ppermute | solution.py:28
  42.0 0.9 %collective-permute-done.13 = bf16[2,2,128,128]{3,2,1,0:T(8,128)(2,1)S(1)} collective-permute-done((bf16[2,2,128,128]{3,2,1,0:T(8,128)(2,1)S(1)}, bf16[2,2,128,128]{3,2,1,0:T(8,128)(2,1)S(1)}, u32[]{:S(2)}, u32[]{:S(2)}) %collective-permute-start.13) | collective-permute-done | bytes 131104 | tf_op jit(solution)/shard_map/ppermute | solution.py:34
  43.0 1.8 %collective-permute-start.16 = (bf16[2,2,128,128]{3,2,1,0:T(8,128)(2,1)S(1)}, bf16[2,2,128,128]{3,2,1,0:T(8,128)(2,1)S(1)}, u32[]{:S(2)}, u32[]{:S(2)}) collective-permute-start(bf16[2,2,128,128]{3,2,1,0:T(8,128)(2,1)S(1)} %fusion.9), channel_id=1, source_target_pairs={{0,2},{1,3},{2,0},{3,1},{4,6},{5,7},{6,4},{7,5},{8,10},{9,11},{10,... | collective-permute-start | bytes 393224 | tf_op jit(solution)/shard_map/ppermute | solution.py:28
  44.8 0.0 collective-permute-done.11.refs_2_
  44.8 1.9 %join_heads.2 = bf16[128,16,128]{2,1,0:T(8,128)(2,1)} custom-call(s32[3]{0:T(128)S(1)} %pad_add_fusion.place, bf16[8,128,128]{2,1,0:T(8,128)(2,1)S(1)} %collective-permute-done.9.refs_0_, bf16[8,128,128]{2,1,0:T(8,128)(2,1)S(1)} %get-tuple-element.37.refs_1_), custom_call_target="tpu_custom_call" | custom-call | tf_op jit(solution)/shard_map/join_heads/pallas_call | solution.py:211
  46.8 1.3 %collective-permute-done.16.refs_0_ = bf16[2,2,128,128]{3,2,1,0:T(8,128)(2,1)S(1)} collective-permute-done((bf16[2,2,128,128]{3,2,1,0:T(8,128)(2,1)S(1)}, bf16[2,2,128,128]{3,2,1,0:T(8,128)(2,1)S(1)}, u32[]{:S(2)}, u32[]{:S(2)}) %collective-permute-start.16) | collective-permute-done | bytes 131104 | tf_op jit(solution)/shard_map/ppermute | solution.py:28
  48.1 1.6 %join_heads.3 = (bf16[128,8,128]{2,1,0:T(8,128)(2,1)}, bf16[128,8,128]{2,1,0:T(8,128)(2,1)}) custom-call(s32[3]{0:T(128)S(1)} %pad_add_fusion.place, bf16[2,2,128,128]{3,2,1,0:T(8,128)(2,1)S(1)} %collective-permute-done.16.refs_0_, bf16[2,2,128,128]{3,2,1,0:T(8,128)(2,1)S(1)} %collective-permute-done.17.refs_1_, ...), custom_call_target="tpu_custom_call" | custom-call | tf_op jit(solution)/shard_map/join_heads/pallas_call | solution.py:211
  (9 shorter events, 0.1 us)
Async XLA Ops:
  1.8 4.6 %copy-start = (bf16[128,16,128]{2,1,0:T(8,128)(2,1)S(1)}, bf16[128,16,128]{2,1,0:T(8,128)(2,1)}, u32[]{:S(2)}) copy-start(bf16[128,16,128]{2,1,0:T(8,128)(2,1)} %param.7) | copy-start | bytes 1572868
  1.8 4.6 %copy-start.1 = (bf16[128,16,128]{2,1,0:T(8,128)(2,1)S(1)}, bf16[128,16,128]{2,1,0:T(8,128)(2,1)}, u32[]{:S(2)}) copy-start(bf16[128,16,128]{2,1,0:T(8,128)(2,1)} %param.4) | copy-start | bytes 1572868
  1.9 10.1 %collective-permute-start.1 = (bf16[2,4,128,128]{3,2,1,0:T(8,128)(2,1)S(1)}, bf16[2,4,128,128]{3,2,1,0:T(8,128)(2,1)S(1)}, u32[]{:S(2)}, u32[]{:S(2)}) collective-permute-start(bf16[2,4,128,128]{3,2,1,0:T(8,128)(2,1)S(1)} %get-tuple-element.51), channel_id=1, source_target_pairs={{0,2},{1,3},{2,0},{3,1},{4,6},{5,7},{6,4},{7,5},{8,10},{9,11},{10,... | collective-permute-start | bytes 786440 | tf_op jit(solution)/shard_map/ppermute | solution.py:28
  4.9 11.1 %collective-permute-start.2 = (bf16[2,4,128,128]{3,2,1,0:T(8,128)(2,1)S(1)}, bf16[2,4,128,128]{3,2,1,0:T(8,128)(2,1)S(1)}, u32[]{:S(2)}, u32[]{:S(2)}) collective-permute-start(bf16[2,4,128,128]{3,2,1,0:T(8,128)(2,1)S(1)} %get-tuple-element.26.ko), channel_id=1, source_target_pairs={{0,4},{1,5},{2,6},{3,7},{4,8},{5,9},{6,10},{7,11},{8,12},{9,13},{1... | collective-permute-start | bytes 786440 | tf_op jit(solution)/shard_map/ppermute | solution.py:34
  7.6 14.8 %collective-permute-start = (bf16[2,8,128,128]{3,2,1,0:T(8,128)(2,1)}, bf16[2,8,128,128]{3,2,1,0:T(8,128)(2,1)S(1)}, u32[]{:S(2)}, u32[]{:S(2)}) collective-permute-start(bf16[2,8,128,128]{3,2,1,0:T(8,128)(2,1)} %get-tuple-element.49), channel_id=1, source_target_pairs={{0,2},{1,3},{2,0},{3,1},{4,6},{5,7},{6,4},{7,5},{8,10},{9,11},{10,... | collective-permute-start | bytes 1572872 | tf_op jit(solution)/shard_map/ppermute | solution.py:28
  12.0 7.9 %collective-permute-start.5 = (bf16[2,4,128,128]{3,2,1,0:T(8,128)(2,1)S(1)}, bf16[2,4,128,128]{3,2,1,0:T(8,128)(2,1)S(1)}, u32[]{:S(2)}, u32[]{:S(2)}) collective-permute-start(bf16[2,4,128,128]{3,2,1,0:T(8,128)(2,1)S(1)} %collective-permute-done.1.xo), channel_id=1, source_target_pairs={{0,4},{1,5},{2,6},{3,7},{4,8},{5,9},{6,10},{7,11},{8,12},{9,13},{1... | collective-permute-start | bytes 786440 | tf_op jit(solution)/shard_map/ppermute | solution.py:34
  16.0 3.9 %collective-permute-start.4 = (bf16[2,4,128,128]{3,2,1,0:T(8,128)(2,1)S(1)}, bf16[2,4,128,128]{3,2,1,0:T(8,128)(2,1)S(1)}, u32[]{:S(2)}, u32[]{:S(2)}) collective-permute-start(bf16[2,4,128,128]{3,2,1,0:T(8,128)(2,1)S(1)} %collective-permute-done.1.xo), channel_id=1, source_target_pairs={{0,1},{1,0},{2,3},{3,2},{4,5},{5,4},{6,7},{7,6},{8,9},{9,8},{10,11... | collective-permute-start | bytes 786440 | tf_op jit(solution)/shard_map/ppermute | solution.py:28
  16.1 3.9 %collective-permute-start.3 = (bf16[2,4,128,128]{3,2,1,0:T(8,128)(2,1)S(1)}, bf16[2,4,128,128]{3,2,1,0:T(8,128)(2,1)S(1)}, u32[]{:S(2)}, u32[]{:S(2)}) collective-permute-start(bf16[2,4,128,128]{3,2,1,0:T(8,128)(2,1)S(1)} %get-tuple-element.26.ko), channel_id=1, source_target_pairs={{0,1},{1,0},{2,3},{3,2},{4,5},{5,4},{6,7},{7,6},{8,9},{9,8},{10,11... | collective-permute-start | bytes 786440 | tf_op jit(solution)/shard_map/ppermute | solution.py:28
  16.6 5.8 %collective-permute-start.6 = (bf16[2,4,128,128]{3,2,1,0:T(8,128)(2,1)S(1)}, bf16[2,4,128,128]{3,2,1,0:T(8,128)(2,1)S(1)}, u32[]{:S(2)}, u32[]{:S(2)}) collective-permute-start(bf16[2,4,128,128]{3,2,1,0:T(8,128)(2,1)S(1)} %collective-permute-done.2.k1), channel_id=1, source_target_pairs={{0,1},{1,0},{2,3},{3,2},{4,5},{5,4},{6,7},{7,6},{8,9},{9,8},{10,11... | collective-permute-start | bytes 786440 | tf_op jit(solution)/shard_map/ppermute | solution.py:28
  19.9 2.6 %collective-permute-start.7 = (bf16[2,4,128,128]{3,2,1,0:T(8,128)(2,1)S(1)}, bf16[2,4,128,128]{3,2,1,0:T(8,128)(2,1)S(1)}, u32[]{:S(2)}, u32[]{:S(2)}) collective-permute-start(bf16[2,4,128,128]{3,2,1,0:T(8,128)(2,1)S(1)} %collective-permute-done.5.k2), channel_id=1, source_target_pairs={{0,1},{1,0},{2,3},{3,2},{4,5},{5,4},{6,7},{7,6},{8,9},{9,8},{10,11... | collective-permute-start | bytes 786440 | tf_op jit(solution)/shard_map/ppermute | solution.py:28
  25.4 3.6 %collective-permute-start.8 = (bf16[2,2,2,128,128]{4,3,2,1,0:T(8,128)(2,1)S(1)}, bf16[2,2,2,128,128]{4,3,2,1,0:T(8,128)(2,1)S(1)}, u32[]{:S(2)}, u32[]{:S(2)}) collective-permute-start(bf16[2,2,2,128,128]{4,3,2,1,0:T(8,128)(2,1)S(1)} %get-tuple-element.32), channel_id=1, source_target_pairs={{0,1},{1,0},{2,3},{3,2},{4,5},{5,4},{6,7},{7,6},{8,9},{9,8},{10,11... | collective-permute-start | bytes 786440 | tf_op jit(solution)/shard_map/ppermute | solution.py:28
  28.4 3.8 %collective-permute-start.10 = (bf16[2,2,2,128,128]{4,3,2,1,0:T(8,128)(2,1)S(1)}, bf16[2,2,2,128,128]{4,3,2,1,0:T(8,128)(2,1)S(1)}, u32[]{:S(2)}, u32[]{:S(2)}) collective-permute-start(bf16[2,2,2,128,128]{4,3,2,1,0:T(8,128)(2,1)S(1)} %get-tuple-element.35), channel_id=1, source_target_pairs={{0,1},{1,0},{2,3},{3,2},{4,5},{5,4},{6,7},{7,6},{8,9},{9,8},{10,11... | collective-permute-start | bytes 786440 | tf_op jit(solution)/shard_map/ppermute | solution.py:28
  29.0 11.1 %collective-permute-start.15 = (bf16[2,2,2,128,128]{4,3,2,1,0:T(8,128)(2,1)S(1)}, bf16[2,2,2,128,128]{4,3,2,1,0:T(8,128)(2,1)S(1)}, u32[]{:S(2)}, u32[]{:S(2)}) collective-permute-start(bf16[2,2,2,128,128]{4,3,2,1,0:T(8,128)(2,1)S(1)} %add_convert_fusion.2), channel_id=1, source_target_pairs={{4,0},{5,1},{6,2},{7,3},{8,4},{9,5},{10,6},{11,7},{12,8},{13,9},{1... | collective-permute-start | bytes 786440 | tf_op jit(solution)/shard_map/ppermute | solution.py:34
  30.3 3.5 %collective-permute-start.14 = (bf16[2,2,2,128,128]{4,3,2,1,0:T(8,128)(2,1)S(1)}, bf16[2,2,2,128,128]{4,3,2,1,0:T(8,128)(2,1)S(1)}, u32[]{:S(2)}, u32[]{:S(2)}) collective-permute-start(bf16[2,2,2,128,128]{4,3,2,1,0:T(8,128)(2,1)S(1)} %get-tuple-element.43), channel_id=1, source_target_pairs={{0,1},{1,0},{2,3},{3,2},{4,5},{5,4},{6,7},{7,6},{8,9},{9,8},{10,11... | collective-permute-start | bytes 786440 | tf_op jit(solution)/shard_map/ppermute | solution.py:28
  30.4 9.8 %collective-permute-start.9 = (bf16[8,128,128]{2,1,0:T(8,128)(2,1)S(1)}, bf16[8,128,128]{2,1,0:T(8,128)(2,1)S(1)}, u32[]{:S(2)}, u32[]{:S(2)}) collective-permute-start(bf16[8,128,128]{2,1,0:T(8,128)(2,1)S(1)} %get-tuple-element.33), channel_id=1, source_target_pairs={{0,2},{1,3},{2,0},{3,1},{4,6},{5,7},{6,4},{7,5},{8,10},{9,11},{10,... | collective-permute-start | bytes 786440 | tf_op jit(solution)/shard_map/ppermute | solution.py:28
  32.3 10.6 %collective-permute-start.13 = (bf16[2,2,128,128]{3,2,1,0:T(8,128)(2,1)S(1)}, bf16[2,2,128,128]{3,2,1,0:T(8,128)(2,1)S(1)}, u32[]{:S(2)}, u32[]{:S(2)}) collective-permute-start(bf16[2,2,128,128]{3,2,1,0:T(8,128)(2,1)S(1)} %get-tuple-element.55), channel_id=1, source_target_pairs={{4,0},{5,1},{6,2},{7,3},{8,4},{9,5},{10,6},{11,7},{12,8},{13,9},{1... | collective-permute-start | bytes 393224 | tf_op jit(solution)/shard_map/ppermute | solution.py:34
  33.6 9.3 %collective-permute-start.12 = (bf16[2,2,2,128,128]{4,3,2,1,0:T(8,128)(2,1)S(1)}, bf16[2,2,2,128,128]{4,3,2,1,0:T(8,128)(2,1)S(1)}, u32[]{:S(2)}, u32[]{:S(2)}) collective-permute-start(bf16[2,2,2,128,128]{4,3,2,1,0:T(8,128)(2,1)S(1)} %get-tuple-element.40), channel_id=1, source_target_pairs={{0,1},{1,0},{2,3},{3,2},{4,5},{5,4},{6,7},{7,6},{8,9},{9,8},{10,11... | collective-permute-start | bytes 786440 | tf_op jit(solution)/shard_map/ppermute | solution.py:28
  33.9 11.0 %collective-permute-start.11 = (bf16[2,2,128,128]{3,2,1,0:T(8,128)(2,1)S(1)}, bf16[2,2,128,128]{3,2,1,0:T(8,128)(2,1)S(1)}, u32[]{:S(2)}, u32[]{:S(2)}) collective-permute-start(bf16[2,2,128,128]{3,2,1,0:T(8,128)(2,1)S(1)} %get-tuple-element.56), channel_id=1, source_target_pairs={{4,0},{5,1},{6,2},{7,3},{8,4},{9,5},{10,6},{11,7},{12,8},{13,9},{1... | collective-permute-start | bytes 393224 | tf_op jit(solution)/shard_map/ppermute | solution.py:34
  40.2 6.5 %collective-permute-start.17 = (bf16[2,2,128,128]{3,2,1,0:T(8,128)(2,1)S(1)}, bf16[2,2,128,128]{3,2,1,0:T(8,128)(2,1)S(1)}, u32[]{:S(2)}, u32[]{:S(2)}) collective-permute-start(bf16[2,2,128,128]{3,2,1,0:T(8,128)(2,1)S(1)} %get-tuple-element.46), channel_id=1, source_target_pairs={{0,2},{1,3},{2,0},{3,1},{4,6},{5,7},{6,4},{7,5},{8,10},{9,11},{10,... | collective-permute-start | bytes 393224 | tf_op jit(solution)/shard_map/ppermute | solution.py:28
  43.0 5.1 %collective-permute-start.16 = (bf16[2,2,128,128]{3,2,1,0:T(8,128)(2,1)S(1)}, bf16[2,2,128,128]{3,2,1,0:T(8,128)(2,1)S(1)}, u32[]{:S(2)}, u32[]{:S(2)}) collective-permute-start(bf16[2,2,128,128]{3,2,1,0:T(8,128)(2,1)S(1)} %fusion.9), channel_id=1, source_target_pairs={{0,2},{1,3},{2,0},{3,1},{4,6},{5,7},{6,4},{7,5},{8,10},{9,11},{10,... | collective-permute-start | bytes 393224 | tf_op jit(solution)/shard_map/ppermute | solution.py:28

commit v6 on v5

--- a/solution.py
+++ b/solution.py
@@ -14,6 +14,7 @@
 LOG2E = math.log2(math.e)
 NEG = -1e30
 VMEM_LIMIT = 48 * 1024 * 1024
+PIECES = 2
 
 NT = (((1,), (1,)), ((), ()))
 NN = (((1,), (0,)), ((), ()))
@@ -180,23 +181,32 @@
 
 
 def join_heads_kernel(keeps, sents, count, place, *refs):
-    outs, wide = refs[-1 - count : -1], refs[-1]
-    refs = refs[: -1 - count][::-1]
+    *refs, wide, ready, sems = refs
+    outs, refs = refs[-count:], refs[:-count][::-1]
     tok, heads, width = outs[0].shape
     half = heads // 2
+    rows = tok // PIECES
     x = place[0]
 
-    def total(chunks, s, j):
+    def total(chunks, s, j, at):
         part = half // len(chunks)
         terms = [refs[n] for n in chunks[j // part]]
-        return sum(r[(s,) * (len(r.shape) - 3) + (j % part,)].astype(jnp.float32) for r in terms)
-
+        return sum(r[(s,) * (len(r.shape) - 3) + (j % part, at)].astype(jnp.float32) for r in terms)
+
+    copies = []
     for s, out in enumerate(outs):
-        for j in range(half):
-            keep, sent = total(keeps, s, j), total(sents, s, j)
-            wide[s, pl.ds(j, tok, stride=heads), :] = jnp.where(x == 0, keep, sent)
-            wide[s, pl.ds(half + j, tok, stride=heads), :] = jnp.where(x == 0, sent, keep)
-        out[...] = wide[s].reshape(tok, heads, width).astype(out.dtype)
+        for piece in range(PIECES):
+            at = pl.ds(piece * rows, rows)
+            n = s * PIECES + piece
+            for j in range(half):
+                keep, sent = total(keeps, s, j, at), total(sents, s, j, at)
+                wide[n, pl.ds(j, rows, stride=heads), :] = jnp.where(x == 0, keep, sent)
+                wide[n, pl.ds(half + j, rows, stride=heads), :] = jnp.where(x == 0, sent, keep)
+            ready[n] = wide[n].reshape(rows, heads, width).astype(out.dtype)
+            copies.append(pltpu.make_async_copy(ready.at[n], out.at[at], sems.at[n]))
+            copies[-1].start()
+    for copy in copies:
+        copy.wait()
 
 
 def join_heads(place, keeps, sents):
@@ -212,8 +222,12 @@
         functools.partial(join_heads_kernel, number(keeps), number(sents), count),
         out_shape=outs,
         in_specs=[pl.BlockSpec(memory_space=pltpu.SMEM)] + [vmem] * len(arrays),
-        out_specs=(vmem,) * count,
-        scratch_shapes=[pltpu.VMEM((count, tok * heads, width), jnp.float32)],
+        out_specs=(pl.BlockSpec(memory_space=pl.ANY),) * count,
+        scratch_shapes=[
+            pltpu.VMEM((count * PIECES, tok // PIECES * heads, width), jnp.float32),
+            pltpu.VMEM((count * PIECES, tok // PIECES, heads, width), jnp.bfloat16),
+            pltpu.SemaphoreType.DMA((count * PIECES,)),
+        ],
         compiler_params=pltpu.CompilerParams(vmem_limit_bytes=VMEM_LIMIT),
         name="join_heads",
     )(place, *arrays)

time: 49.9 us -> 49.8 us (level)
  no operation moved by 1% of the time
where the time goes in v6:
time: 49.8 us; the launch traced here: 49.6 us
  starting transfers between devices  19.9 us (40%)
  waiting for transfers between devices  16.8 us (34%)
  Pallas kernels  9.23 us (19%)
  local copies, waits for them, and re-layouts  1.46 us (3%)
  other arithmetic  1.33 us (3%)
  between operations  0.88 us (2%)
    ppermute x13, starting transfers between devices, swap(): return lax.ppermute(a, 'ctx', [(i, i ^ by) for i in range(n)])  10.5 us
    ppermute x5, starting transfers between devices, shift(): return lax.ppermute(a, 'ctx', pairs)  9.38 us
    ppermute x5, waiting for transfers between devices, shift(): return lax.ppermute(a, 'ctx', pairs)  9.02 us
    ppermute x13, waiting for transfers between devices, swap(): return lax.ppermute(a, 'ctx', [(i, i ^ by) for i in range(n)])  7.76 us
    pallas_call x2, Pallas kernels, grads(): pl.pallas_call(functools.partial(grads_kernel, start, groups), out_shape=...  5.87 us
    pallas_call x2, Pallas kernels, join_heads(): pl.pallas_call(functools.partial(join_heads_kernel, number(keeps), number...  3.36 us
    another operation x2, local copies, waits for them, and re-layouts, split_heads(): both = jnp.stack([a, b]).transpose(0, 2, 1, 3)  1.39 us
  transfers between devices with their start and end apart: 18, of which 6 were waited for; matrix products, arithmetic and copies ran while one was open for 3% of the time, Pallas kernels for 10%

profile of v6, /device:TPU:0, one launch (start us, length us, event | category | flops | bytes accessed | tf_op | source)
XLA Modules:
  0.0 49.6 jit_solution(3836450982328213546)
XLA Ops:
  0.7 1.1 %copy_bitcast_fusion.2 = (bf16[1,128,8,128]{3,1,2,0:T(8,128)(2,1)S(1)}, bf16[1,128,8,128]{3,1,2,0:T(8,128)(2,1)S(1)}) fusion(bf16[128,8,128]{2,1,0:T(8,128)(2,1)} %param.6, bf16[128,8,128]{2,1,0:T(8,128)(2,1)} %param.5), kind=kLoop, calls=%fused_computation.26 | loop fusion | bytes 1048576 | tf_op jit(solution)/shard_map/stack | solution.py:43
  1.8 0.0 copy-start
  1.8 0.0 copy-start.1
  1.8 0.1 fusion.5
  1.9 3.0 %collective-permute-start.1 = (bf16[2,4,128,128]{3,2,1,0:T(8,128)(2,1)S(1)}, bf16[2,4,128,128]{3,2,1,0:T(8,128)(2,1)S(1)}, u32[]{:S(2)}, u32[]{:S(2)}) collective-permute-start(bf16[2,4,128,128]{3,2,1,0:T(8,128)(2,1)S(1)} %get-tuple-element.51), channel_id=1, source_target_pairs={{0,2},{1,3},{2,0},{3,1},{4,6},{5,7},{6,4},{7,5},{8,10},{9,11},{10,... | collective-permute-start | bytes 786440 | tf_op jit(solution)/shard_map/ppermute | solution.py:29
  4.9 1.5 %collective-permute-start.2 = (bf16[2,4,128,128]{3,2,1,0:T(8,128)(2,1)S(1)}, bf16[2,4,128,128]{3,2,1,0:T(8,128)(2,1)S(1)}, u32[]{:S(2)}, u32[]{:S(2)}) collective-permute-start(bf16[2,4,128,128]{3,2,1,0:T(8,128)(2,1)S(1)} %get-tuple-element.26.ko), channel_id=1, source_target_pairs={{0,4},{1,5},{2,6},{3,7},{4,8},{5,9},{6,10},{7,11},{8,12},{9,13},{1... | collective-permute-start | bytes 786440 | tf_op jit(solution)/shard_map/ppermute | solution.py:35
  6.4 0.3 copy_bitcast_fusion
  6.7 0.9 %fusion.1 = (bf16[2,8,128,128]{3,2,1,0:T(8,128)(2,1)}, bf16[2,8,128,128]{3,2,1,0:T(8,128)(2,1)S(1)}) fusion(s32[]{:T(128)S(6)} %select_n.31, bf16[1,128,16,128]{3,1,2,0:T(8,128)(2,1)S(1)} %get-tuple-element.58, bf16[1,128,16,128]{3,1,2,0:T(8,128)(2,1)S(1)} %get-tuple-element.57, s32[]{:T(128)S(6)} %select_n.30), kind=kLoop, calls=%fused_computation.9 | loop fusion | flops 524288 | bytes 2097160 | tf_op jit(solution)/shard_map/dynamic_slice | solution.py:45
  7.6 0.5 %collective-permute-start = (bf16[2,8,128,128]{3,2,1,0:T(8,128)(2,1)}, bf16[2,8,128,128]{3,2,1,0:T(8,128)(2,1)S(1)}, u32[]{:S(2)}, u32[]{:S(2)}) collective-permute-start(bf16[2,8,128,128]{3,2,1,0:T(8,128)(2,1)} %get-tuple-element.49), channel_id=1, source_target_pairs={{0,2},{1,3},{2,0},{3,1},{4,6},{5,7},{6,4},{7,5},{8,10},{9,11},{10,... | collective-permute-start | bytes 1572872 | tf_op jit(solution)/shard_map/ppermute | solution.py:29
  8.1 3.9 %collective-permute-done.1.xo = bf16[2,4,128,128]{3,2,1,0:T(8,128)(2,1)S(1)} collective-permute-done((bf16[2,4,128,128]{3,2,1,0:T(8,128)(2,1)S(1)}, bf16[2,4,128,128]{3,2,1,0:T(8,128)(2,1)S(1)}, u32[]{:S(2)}, u32[]{:S(2)}) %collective-permute-start.1) | collective-permute-done | bytes 262176 | tf_op jit(solution)/shard_map/ppermute | solution.py:29
  12.0 4.0 %collective-permute-start.5 = (bf16[2,4,128,128]{3,2,1,0:T(8,128)(2,1)S(1)}, bf16[2,4,128,128]{3,2,1,0:T(8,128)(2,1)S(1)}, u32[]{:S(2)}, u32[]{:S(2)}) collective-permute-start(bf16[2,4,128,128]{3,2,1,0:T(8,128)(2,1)S(1)} %collective-permute-done.1.xo), channel_id=1, source_target_pairs={{0,4},{1,5},{2,6},{3,7},{4,8},{5,9},{6,10},{7,11},{8,12},{9,13},{1... | collective-permute-start | bytes 786440 | tf_op jit(solution)/shard_map/ppermute | solution.py:35
  16.0 0.0 collective-permute-done.2.k1
  16.0 0.1 collective-permute-start.4
  16.1 0.5 %collective-permute-start.3 = (bf16[2,4,128,128]{3,2,1,0:T(8,128)(2,1)S(1)}, bf16[2,4,128,128]{3,2,1,0:T(8,128)(2,1)S(1)}, u32[]{:S(2)}, u32[]{:S(2)}) collective-permute-start(bf16[2,4,128,128]{3,2,1,0:T(8,128)(2,1)S(1)} %get-tuple-element.26.ko), channel_id=1, source_target_pairs={{0,1},{1,0},{2,3},{3,2},{4,5},{5,4},{6,7},{7,6},{8,9},{9,8},{10,11... | collective-permute-start | bytes 786440 | tf_op jit(solution)/shard_map/ppermute | solution.py:29
  16.6 0.1 collective-permute-start.6
  16.7 3.2 %collective-permute-done.5.k2 = bf16[2,4,128,128]{3,2,1,0:T(8,128)(2,1)S(1)} collective-permute-done((bf16[2,4,128,128]{3,2,1,0:T(8,128)(2,1)S(1)}, bf16[2,4,128,128]{3,2,1,0:T(8,128)(2,1)S(1)}, u32[]{:S(2)}, u32[]{:S(2)}) %collective-permute-start.5) | collective-permute-done | bytes 262176 | tf_op jit(solution)/shard_map/ppermute | solution.py:35
  19.9 0.0 collective-permute-start.7
  19.9 0.1 pad_add_fusion.place
  20.0 0.0 collective-permute-done.4.mxo
  20.0 0.0 collective-permute-done.3.mko
  20.0 2.5 %collective-permute-done.sent_q = bf16[2,8,128,128]{3,2,1,0:T(8,128)(2,1)S(1)} collective-permute-done((bf16[2,8,128,128]{3,2,1,0:T(8,128)(2,1)}, bf16[2,8,128,128]{3,2,1,0:T(8,128)(2,1)S(1)}, u32[]{:S(2)}, u32[]{:S(2)}) %collective-permute-start) | collective-permute-done | bytes 524320 | tf_op jit(solution)/shard_map/ppermute | solution.py:29
  22.4 0.0 collective-permute-done.6.mk1
  22.4 0.0 collective-permute-done.7.mk2
  22.4 2.9 %window_grads.2 = (bf16[4,128,128]{2,1,0:T(8,128)(2,1)S(1)}, bf16[4,128,128]{2,1,0:T(8,128)(2,1)S(1)}, f32[2,2,2,128,128]{4,3,2,1,0:T(8,128)S(1)}, bf16[2,2,2,12...) custom-call(s32[3]{0:T(128)S(1)} %pad_add_fusion.place, ...), custom_call_target="tpu_custom_call" | custom-call | flops 1 | bytes 1 | tf_op jit(solution)/shard_map/window_grads/pallas_call | solution.py:171
  25.4 0.1 collective-permute-start.8
  25.5 2.9 %window_grads.3 = (bf16[8,128,128]{2,1,0:T(8,128)(2,1)S(1)}, bf16[8,128,128]{2,1,0:T(8,128)(2,1)S(1)}, f32[2,2,2,128,128]{4,3,2,1,0:T(8,128)S(1)}, bf16[2,2,2,12...) custom-call(s32[3]{0:T(128)S(1)} %pad_add_fusion.place, ...), custom_call_target="tpu_custom_call" | custom-call | flops 1 | bytes 1 | tf_op jit(solution)/shard_map/window_grads/pallas_call | solution.py:171
  28.4 0.6 %collective-permute-start.10 = (bf16[2,2,2,128,128]{4,3,2,1,0:T(8,128)(2,1)S(1)}, bf16[2,2,2,128,128]{4,3,2,1,0:T(8,128)(2,1)S(1)}, u32[]{:S(2)}, u32[]{:S(2)}) collective-permute-start(bf16[2,2,2,128,128]{4,3,2,1,0:T(8,128)(2,1)S(1)} %get-tuple-element.35), channel_id=1, source_target_pairs={{0,1},{1,0},{2,3},{3,2},{4,5},{5,4},{6,7},{7,6},{8,9},{9,8},{10,11... | collective-permute-start | bytes 786440 | tf_op jit(solution)/shard_map/ppermute | solution.py:29
  29.0 0.0 collective-permute-done.8
  29.0 0.1 add_convert_fusion.2
  29.0 1.3 %collective-permute-start.15 = (bf16[2,2,2,128,128]{4,3,2,1,0:T(8,128)(2,1)S(1)}, bf16[2,2,2,128,128]{4,3,2,1,0:T(8,128)(2,1)S(1)}, u32[]{:S(2)}, u32[]{:S(2)}) collective-permute-start(bf16[2,2,2,128,128]{4,3,2,1,0:T(8,128)(2,1)S(1)} %add_convert_fusion.2), channel_id=1, source_target_pairs={{4,0},{5,1},{6,2},{7,3},{8,4},{9,5},{10,6},{11,7},{12,8},{13,9},{1... | collective-permute-start | bytes 786440 | tf_op jit(solution)/shard_map/ppermute | solution.py:35
  30.3 0.1 collective-permute-start.14
  30.4 1.8 %collective-permute-start.9 = (bf16[8,128,128]{2,1,0:T(8,128)(2,1)S(1)}, bf16[8,128,128]{2,1,0:T(8,128)(2,1)S(1)}, u32[]{:S(2)}, u32[]{:S(2)}) collective-permute-start(bf16[8,128,128]{2,1,0:T(8,128)(2,1)S(1)} %get-tuple-element.33), channel_id=1, source_target_pairs={{0,2},{1,3},{2,0},{3,1},{4,6},{5,7},{6,4},{7,5},{8,10},{9,11},{10,... | collective-permute-start | bytes 786440 | tf_op jit(solution)/shard_map/ppermute | solution.py:29
  32.2 0.0 collective-permute-done.10
  32.2 0.1 add_convert_fusion.1
  32.3 1.3 %collective-permute-start.13 = (bf16[2,2,128,128]{3,2,1,0:T(8,128)(2,1)S(1)}, bf16[2,2,128,128]{3,2,1,0:T(8,128)(2,1)S(1)}, u32[]{:S(2)}, u32[]{:S(2)}) collective-permute-start(bf16[2,2,128,128]{3,2,1,0:T(8,128)(2,1)S(1)} %get-tuple-element.55), channel_id=1, source_target_pairs={{4,0},{5,1},{6,2},{7,3},{8,4},{9,5},{10,6},{11,7},{12,8},{13,9},{1... | collective-permute-start | bytes 393224 | tf_op jit(solution)/shard_map/ppermute | solution.py:35
  33.6 0.2 collective-permute-start.12
  33.9 1.3 %collective-permute-start.11 = (bf16[2,2,128,128]{3,2,1,0:T(8,128)(2,1)S(1)}, bf16[2,2,128,128]{3,2,1,0:T(8,128)(2,1)S(1)}, u32[]{:S(2)}, u32[]{:S(2)}) collective-permute-start(bf16[2,2,128,128]{3,2,1,0:T(8,128)(2,1)S(1)} %get-tuple-element.56), channel_id=1, source_target_pairs={{4,0},{5,1},{6,2},{7,3},{8,4},{9,5},{10,6},{11,7},{12,8},{13,9},{1... | collective-permute-start | bytes 393224 | tf_op jit(solution)/shard_map/ppermute | solution.py:35
  35.1 4.9 %collective-permute-done.15 = bf16[2,2,2,128,128]{4,3,2,1,0:T(8,128)(2,1)S(1)} collective-permute-done((bf16[2,2,2,128,128]{4,3,2,1,0:T(8,128)(2,1)S(1)}, bf16[2,2,2,128,128]{4,3,2,1,0:T(8,128)(2,1)S(1)}, u32[]{:S(2)}, u32[]{:S(2)}) %collective-permute-start.15) | collective-permute-done | bytes 262176 | tf_op jit(solution)/shard_map/ppermute | solution.py:35
  40.1 0.1 add_convert_fusion
  40.2 1.8 %collective-permute-start.17 = (bf16[2,2,128,128]{3,2,1,0:T(8,128)(2,1)S(1)}, bf16[2,2,128,128]{3,2,1,0:T(8,128)(2,1)S(1)}, u32[]{:S(2)}, u32[]{:S(2)}) collective-permute-start(bf16[2,2,128,128]{3,2,1,0:T(8,128)(2,1)S(1)} %get-tuple-element.46), channel_id=1, source_target_pairs={{0,2},{1,3},{2,0},{3,1},{4,6},{5,7},{6,4},{7,5},{8,10},{9,11},{10,... | collective-permute-start | bytes 393224 | tf_op jit(solution)/shard_map/ppermute | solution.py:29
  42.0 0.9 %collective-permute-done.13 = bf16[2,2,128,128]{3,2,1,0:T(8,128)(2,1)S(1)} collective-permute-done((bf16[2,2,128,128]{3,2,1,0:T(8,128)(2,1)S(1)}, bf16[2,2,128,128]{3,2,1,0:T(8,128)(2,1)S(1)}, u32[]{:S(2)}, u32[]{:S(2)}) %collective-permute-start.13) | collective-permute-done | bytes 131104 | tf_op jit(solution)/shard_map/ppermute | solution.py:35
  42.9 0.0 collective-permute-done.12
  43.0 1.8 %collective-permute-start.16 = (bf16[2,2,128,128]{3,2,1,0:T(8,128)(2,1)S(1)}, bf16[2,2,128,128]{3,2,1,0:T(8,128)(2,1)S(1)}, u32[]{:S(2)}, u32[]{:S(2)}) collective-permute-start(bf16[2,2,128,128]{3,2,1,0:T(8,128)(2,1)S(1)} %fusion.9), channel_id=1, source_target_pairs={{0,2},{1,3},{2,0},{3,1},{4,6},{5,7},{6,4},{7,5},{8,10},{9,11},{10,... | collective-permute-start | bytes 393224 | tf_op jit(solution)/shard_map/ppermute | solution.py:29
  44.8 0.0 collective-permute-done.11.refs_2_
  44.8 1.8 %join_heads.2 = bf16[128,16,128]{2,1,0:T(8,128)(2,1)} custom-call(s32[3]{0:T(128)S(1)} %pad_add_fusion.place, bf16[8,128,128]{2,1,0:T(8,128)(2,1)S(1)} %collective-permute-done.9.refs_0_, bf16[8,128,128]{2,1,0:T(8,128)(2,1)S(1)} %get-tuple-element.37.refs_1_), custom_call_target="tpu_custom_call" | custom-call | tf_op jit(solution)/shard_map/join_heads/pallas_call | solution.py:221
  46.7 0.0 collective-permute-done.17.refs_1_
  46.7 1.4 %collective-permute-done.16.refs_0_ = bf16[2,2,128,128]{3,2,1,0:T(8,128)(2,1)S(1)} collective-permute-done((bf16[2,2,128,128]{3,2,1,0:T(8,128)(2,1)S(1)}, bf16[2,2,128,128]{3,2,1,0:T(8,128)(2,1)S(1)}, u32[]{:S(2)}, u32[]{:S(2)}) %collective-permute-start.16) | collective-permute-done | bytes 131104 | tf_op jit(solution)/shard_map/ppermute | solution.py:29
  48.1 1.5 %join_heads.3 = (bf16[128,8,128]{2,1,0:T(8,128)(2,1)}, bf16[128,8,128]{2,1,0:T(8,128)(2,1)}) custom-call(s32[3]{0:T(128)S(1)} %pad_add_fusion.place, bf16[2,2,128,128]{3,2,1,0:T(8,128)(2,1)S(1)} %collective-permute-done.16.refs_0_, bf16[2,2,128,128]{3,2,1,0:T(8,128)(2,1)S(1)} %collective-permute-done.17.refs_1_, ...), custom_call_target="tpu_custom_call" | custom-call | tf_op jit(solution)/shard_map/join_heads/pallas_call | solution.py:221
  (9 shorter events, 0.1 us)
Async XLA Ops:
  1.8 4.6 %copy-start = (bf16[128,16,128]{2,1,0:T(8,128)(2,1)S(1)}, bf16[128,16,128]{2,1,0:T(8,128)(2,1)}, u32[]{:S(2)}) copy-start(bf16[128,16,128]{2,1,0:T(8,128)(2,1)} %param.7) | copy-start | bytes 1572868
  1.8 4.6 %copy-start.1 = (bf16[128,16,128]{2,1,0:T(8,128)(2,1)S(1)}, bf16[128,16,128]{2,1,0:T(8,128)(2,1)}, u32[]{:S(2)}) copy-start(bf16[128,16,128]{2,1,0:T(8,128)(2,1)} %param.4) | copy-start | bytes 1572868
  1.9 10.1 %collective-permute-start.1 = (bf16[2,4,128,128]{3,2,1,0:T(8,128)(2,1)S(1)}, bf16[2,4,128,128]{3,2,1,0:T(8,128)(2,1)S(1)}, u32[]{:S(2)}, u32[]{:S(2)}) collective-permute-start(bf16[2,4,128,128]{3,2,1,0:T(8,128)(2,1)S(1)} %get-tuple-element.51), channel_id=1, source_target_pairs={{0,2},{1,3},{2,0},{3,1},{4,6},{5,7},{6,4},{7,5},{8,10},{9,11},{10,... | collective-permute-start | bytes 786440 | tf_op jit(solution)/shard_map/ppermute | solution.py:29
  4.9 11.1 %collective-permute-start.2 = (bf16[2,4,128,128]{3,2,1,0:T(8,128)(2,1)S(1)}, bf16[2,4,128,128]{3,2,1,0:T(8,128)(2,1)S(1)}, u32[]{:S(2)}, u32[]{:S(2)}) collective-permute-start(bf16[2,4,128,128]{3,2,1,0:T(8,128)(2,1)S(1)} %get-tuple-element.26.ko), channel_id=1, source_target_pairs={{0,4},{1,5},{2,6},{3,7},{4,8},{5,9},{6,10},{7,11},{8,12},{9,13},{1... | collective-permute-start | bytes 786440 | tf_op jit(solution)/shard_map/ppermute | solution.py:35
  7.6 14.8 %collective-permute-start = (bf16[2,8,128,128]{3,2,1,0:T(8,128)(2,1)}, bf16[2,8,128,128]{3,2,1,0:T(8,128)(2,1)S(1)}, u32[]{:S(2)}, u32[]{:S(2)}) collective-permute-start(bf16[2,8,128,128]{3,2,1,0:T(8,128)(2,1)} %get-tuple-element.49), channel_id=1, source_target_pairs={{0,2},{1,3},{2,0},{3,1},{4,6},{5,7},{6,4},{7,5},{8,10},{9,11},{10,... | collective-permute-start | bytes 1572872 | tf_op jit(solution)/shard_map/ppermute | solution.py:29
  12.0 7.9 %collective-permute-start.5 = (bf16[2,4,128,128]{3,2,1,0:T(8,128)(2,1)S(1)}, bf16[2,4,128,128]{3,2,1,0:T(8,128)(2,1)S(1)}, u32[]{:S(2)}, u32[]{:S(2)}) collective-permute-start(bf16[2,4,128,128]{3,2,1,0:T(8,128)(2,1)S(1)} %collective-permute-done.1.xo), channel_id=1, source_target_pairs={{0,4},{1,5},{2,6},{3,7},{4,8},{5,9},{6,10},{7,11},{8,12},{9,13},{1... | collective-permute-start | bytes 786440 | tf_op jit(solution)/shard_map/ppermute | solution.py:35
  16.0 3.9 %collective-permute-start.4 = (bf16[2,4,128,128]{3,2,1,0:T(8,128)(2,1)S(1)}, bf16[2,4,128,128]{3,2,1,0:T(8,128)(2,1)S(1)}, u32[]{:S(2)}, u32[]{:S(2)}) collective-permute-start(bf16[2,4,128,128]{3,2,1,0:T(8,128)(2,1)S(1)} %collective-permute-done.1.xo), channel_id=1, source_target_pairs={{0,1},{1,0},{2,3},{3,2},{4,5},{5,4},{6,7},{7,6},{8,9},{9,8},{10,11... | collective-permute-start | bytes 786440 | tf_op jit(solution)/shard_map/ppermute | solution.py:29
  16.1 3.9 %collective-permute-start.3 = (bf16[2,4,128,128]{3,2,1,0:T(8,128)(2,1)S(1)}, bf16[2,4,128,128]{3,2,1,0:T(8,128)(2,1)S(1)}, u32[]{:S(2)}, u32[]{:S(2)}) collective-permute-start(bf16[2,4,128,128]{3,2,1,0:T(8,128)(2,1)S(1)} %get-tuple-element.26.ko), channel_id=1, source_target_pairs={{0,1},{1,0},{2,3},{3,2},{4,5},{5,4},{6,7},{7,6},{8,9},{9,8},{10,11... | collective-permute-start | bytes 786440 | tf_op jit(solution)/shard_map/ppermute | solution.py:29
  16.6 5.8 %collective-permute-start.6 = (bf16[2,4,128,128]{3,2,1,0:T(8,128)(2,1)S(1)}, bf16[2,4,128,128]{3,2,1,0:T(8,128)(2,1)S(1)}, u32[]{:S(2)}, u32[]{:S(2)}) collective-permute-start(bf16[2,4,128,128]{3,2,1,0:T(8,128)(2,1)S(1)} %collective-permute-done.2.k1), channel_id=1, source_target_pairs={{0,1},{1,0},{2,3},{3,2},{4,5},{5,4},{6,7},{7,6},{8,9},{9,8},{10,11... | collective-permute-start | bytes 786440 | tf_op jit(solution)/shard_map/ppermute | solution.py:29
  19.9 2.6 %collective-permute-start.7 = (bf16[2,4,128,128]{3,2,1,0:T(8,128)(2,1)S(1)}, bf16[2,4,128,128]{3,2,1,0:T(8,128)(2,1)S(1)}, u32[]{:S(2)}, u32[]{:S(2)}) collective-permute-start(bf16[2,4,128,128]{3,2,1,0:T(8,128)(2,1)S(1)} %collective-permute-done.5.k2), channel_id=1, source_target_pairs={{0,1},{1,0},{2,3},{3,2},{4,5},{5,4},{6,7},{7,6},{8,9},{9,8},{10,11... | collective-permute-start | bytes 786440 | tf_op jit(solution)/shard_map/ppermute | solution.py:29
  25.4 3.6 %collective-permute-start.8 = (bf16[2,2,2,128,128]{4,3,2,1,0:T(8,128)(2,1)S(1)}, bf16[2,2,2,128,128]{4,3,2,1,0:T(8,128)(2,1)S(1)}, u32[]{:S(2)}, u32[]{:S(2)}) collective-permute-start(bf16[2,2,2,128,128]{4,3,2,1,0:T(8,128)(2,1)S(1)} %get-tuple-element.32), channel_id=1, source_target_pairs={{0,1},{1,0},{2,3},{3,2},{4,5},{5,4},{6,7},{7,6},{8,9},{9,8},{10,11... | collective-permute-start | bytes 786440 | tf_op jit(solution)/shard_map/ppermute | solution.py:29
  28.4 3.8 %collective-permute-start.10 = (bf16[2,2,2,128,128]{4,3,2,1,0:T(8,128)(2,1)S(1)}, bf16[2,2,2,128,128]{4,3,2,1,0:T(8,128)(2,1)S(1)}, u32[]{:S(2)}, u32[]{:S(2)}) collective-permute-start(bf16[2,2,2,128,128]{4,3,2,1,0:T(8,128)(2,1)S(1)} %get-tuple-element.35), channel_id=1, source_target_pairs={{0,1},{1,0},{2,3},{3,2},{4,5},{5,4},{6,7},{7,6},{8,9},{9,8},{10,11... | collective-permute-start | bytes 786440 | tf_op jit(solution)/shard_map/ppermute | solution.py:29
  29.0 11.1 %collective-permute-start.15 = (bf16[2,2,2,128,128]{4,3,2,1,0:T(8,128)(2,1)S(1)}, bf16[2,2,2,128,128]{4,3,2,1,0:T(8,128)(2,1)S(1)}, u32[]{:S(2)}, u32[]{:S(2)}) collective-permute-start(bf16[2,2,2,128,128]{4,3,2,1,0:T(8,128)(2,1)S(1)} %add_convert_fusion.2), channel_id=1, source_target_pairs={{4,0},{5,1},{6,2},{7,3},{8,4},{9,5},{10,6},{11,7},{12,8},{13,9},{1... | collective-permute-start | bytes 786440 | tf_op jit(solution)/shard_map/ppermute | solution.py:35
  30.3 3.5 %collective-permute-start.14 = (bf16[2,2,2,128,128]{4,3,2,1,0:T(8,128)(2,1)S(1)}, bf16[2,2,2,128,128]{4,3,2,1,0:T(8,128)(2,1)S(1)}, u32[]{:S(2)}, u32[]{:S(2)}) collective-permute-start(bf16[2,2,2,128,128]{4,3,2,1,0:T(8,128)(2,1)S(1)} %get-tuple-element.43), channel_id=1, source_target_pairs={{0,1},{1,0},{2,3},{3,2},{4,5},{5,4},{6,7},{7,6},{8,9},{9,8},{10,11... | collective-permute-start | bytes 786440 | tf_op jit(solution)/shard_map/ppermute | solution.py:29
  30.4 9.8 %collective-permute-start.9 = (bf16[8,128,128]{2,1,0:T(8,128)(2,1)S(1)}, bf16[8,128,128]{2,1,0:T(8,128)(2,1)S(1)}, u32[]{:S(2)}, u32[]{:S(2)}) collective-permute-start(bf16[8,128,128]{2,1,0:T(8,128)(2,1)S(1)} %get-tuple-element.33), channel_id=1, source_target_pairs={{0,2},{1,3},{2,0},{3,1},{4,6},{5,7},{6,4},{7,5},{8,10},{9,11},{10,... | collective-permute-start | bytes 786440 | tf_op jit(solution)/shard_map/ppermute | solution.py:29
  32.3 10.6 %collective-permute-start.13 = (bf16[2,2,128,128]{3,2,1,0:T(8,128)(2,1)S(1)}, bf16[2,2,128,128]{3,2,1,0:T(8,128)(2,1)S(1)}, u32[]{:S(2)}, u32[]{:S(2)}) collective-permute-start(bf16[2,2,128,128]{3,2,1,0:T(8,128)(2,1)S(1)} %get-tuple-element.55), channel_id=1, source_target_pairs={{4,0},{5,1},{6,2},{7,3},{8,4},{9,5},{10,6},{11,7},{12,8},{13,9},{1... | collective-permute-start | bytes 393224 | tf_op jit(solution)/shard_map/ppermute | solution.py:35
  33.6 9.3 %collective-permute-start.12 = (bf16[2,2,2,128,128]{4,3,2,1,0:T(8,128)(2,1)S(1)}, bf16[2,2,2,128,128]{4,3,2,1,0:T(8,128)(2,1)S(1)}, u32[]{:S(2)}, u32[]{:S(2)}) collective-permute-start(bf16[2,2,2,128,128]{4,3,2,1,0:T(8,128)(2,1)S(1)} %get-tuple-element.40), channel_id=1, source_target_pairs={{0,1},{1,0},{2,3},{3,2},{4,5},{5,4},{6,7},{7,6},{8,9},{9,8},{10,11... | collective-permute-start | bytes 786440 | tf_op jit(solution)/shard_map/ppermute | solution.py:29
  33.9 11.0 %collective-permute-start.11 = (bf16[2,2,128,128]{3,2,1,0:T(8,128)(2,1)S(1)}, bf16[2,2,128,128]{3,2,1,0:T(8,128)(2,1)S(1)}, u32[]{:S(2)}, u32[]{:S(2)}) collective-permute-start(bf16[2,2,128,128]{3,2,1,0:T(8,128)(2,1)S(1)} %get-tuple-element.56), channel_id=1, source_target_pairs={{4,0},{5,1},{6,2},{7,3},{8,4},{9,5},{10,6},{11,7},{12,8},{13,9},{1... | collective-permute-start | bytes 393224 | tf_op jit(solution)/shard_map/ppermute | solution.py:35
  40.2 6.5 %collective-permute-start.17 = (bf16[2,2,128,128]{3,2,1,0:T(8,128)(2,1)S(1)}, bf16[2,2,128,128]{3,2,1,0:T(8,128)(2,1)S(1)}, u32[]{:S(2)}, u32[]{:S(2)}) collective-permute-start(bf16[2,2,128,128]{3,2,1,0:T(8,128)(2,1)S(1)} %get-tuple-element.46), channel_id=1, source_target_pairs={{0,2},{1,3},{2,0},{3,1},{4,6},{5,7},{6,4},{7,5},{8,10},{9,11},{10,... | collective-permute-start | bytes 393224 | tf_op jit(solution)/shard_map/ppermute | solution.py:29
  43.0 5.1 %collective-permute-start.16 = (bf16[2,2,128,128]{3,2,1,0:T(8,128)(2,1)S(1)}, bf16[2,2,128,128]{3,2,1,0:T(8,128)(2,1)S(1)}, u32[]{:S(2)}, u32[]{:S(2)}) collective-permute-start(bf16[2,2,128,128]{3,2,1,0:T(8,128)(2,1)S(1)} %fusion.9), channel_id=1, source_target_pairs={{0,2},{1,3},{2,0},{3,1},{4,6},{5,7},{6,4},{7,5},{8,10},{9,11},{10,... | collective-permute-start | bytes 393224 | tf_op jit(solution)/shard_map/ppermute | solution.py:29

commit v7 on v5

--- a/solution.py
+++ b/solution.py
@@ -233,7 +233,7 @@
     kv_keep, kv_send = split_heads(x, keys, values)
     q_keep, q_send = split_heads(x, queries, d_out)
     kv_x = swap(kv_send, 2)
-    kv_1 = shift(kv_keep, quad, wrap=True)
+    kv_1 = shift(kv_keep, quad)
     q_x = swap(q_send, 2)
     kv_2 = shift(kv_x, quad)
     mates = [swap(after(a, kv_1), 1) for a in (kv_keep, kv_x)]

time: 49.9 us -> 50.3 us (level)
    ppermute x5, waiting for transfers between devices: 9.02 us -> 11.1 us  [shift(): return lax.ppermute(a, 'ctx', pairs)]
    ppermute x13, waiting for transfers between devices: 7.67 us -> 5.71 us  [swap(): return lax.ppermute(a, 'ctx', [(i, i ^ by) for i in range(n)])]
    ppermute x5, starting transfers between devices: 9.38 us -> 11 us  [shift(): return lax.ppermute(a, 'ctx', pairs)]
    ppermute x13, starting transfers between devices: 10.5 us -> 9.27 us  [swap(): return lax.ppermute(a, 'ctx', [(i, i ^ by) for i in range(n)])]
  transfers between devices with their start and end apart: 18 -> 18, of which waited for: 6 -> 7; matrix products, arithmetic and copies ran while one was open for 3% -> 3% of each run, Pallas kernels for 10% -> 10%
where the time goes in v7:
time: 50.3 us; the launch traced here: 50.1 us
  starting transfers between devices  20.2 us (40%)
  waiting for transfers between devices  16.8 us (33%)
  Pallas kernels  9.38 us (19%)
  local copies, waits for them, and re-layouts  1.46 us (3%)
  other arithmetic  1.33 us (3%)
  between operations  0.89 us (2%)
    ppermute x5, waiting for transfers between devices, shift(): return lax.ppermute(a, 'ctx', pairs)  11.1 us
    ppermute x5, starting transfers between devices, shift(): return lax.ppermute(a, 'ctx', pairs)  11 us
    ppermute x13, starting transfers between devices, swap(): return lax.ppermute(a, 'ctx', [(i, i ^ by) for i in range(n)])  9.27 us
    pallas_call x2, Pallas kernels, grads(): pl.pallas_call(functools.partial(grads_kernel, start, groups), out_shape=...  5.88 us
    ppermute x13, waiting for transfers between devices, swap(): return lax.ppermute(a, 'ctx', [(i, i ^ by) for i in range(n)])  5.71 us
    pallas_call x2, Pallas kernels, join_heads(): pl.pallas_call(functools.partial(join_heads_kernel, number(keeps), number...  3.5 us
    another operation x2, local copies, waits for them, and re-layouts, split_heads(): both = jnp.stack([a, b]).transpose(0, 2, 1, 3)  1.39 us
  transfers between devices with their start and end apart: 18, of which 7 were waited for; matrix products, arithmetic and copies ran while one was open for 3% of the time, Pallas kernels for 10%

profile of v7, /device:TPU:0, one launch (start us, length us, event | category | flops | bytes accessed | tf_op | source)
XLA Modules:
  0.0 50.1 jit_solution(4737750621538291163)
XLA Ops:
  0.7 1.1 %copy_bitcast_fusion.2 = (bf16[1,128,8,128]{3,1,2,0:T(8,128)(2,1)S(1)}, bf16[1,128,8,128]{3,1,2,0:T(8,128)(2,1)S(1)}) fusion(bf16[128,8,128]{2,1,0:T(8,128)(2,1)} %param.6, bf16[128,8,128]{2,1,0:T(8,128)(2,1)} %param.5), kind=kLoop, calls=%fused_computation.26 | loop fusion | bytes 1048576 | tf_op jit(solution)/shard_map/stack | solution.py:42
  1.8 0.0 copy-start
  1.8 0.0 copy-start.1
  1.8 0.1 fusion.5
  1.9 3.0 %collective-permute-start.1 = (bf16[2,4,128,128]{3,2,1,0:T(8,128)(2,1)S(1)}, bf16[2,4,128,128]{3,2,1,0:T(8,128)(2,1)S(1)}, u32[]{:S(2)}, u32[]{:S(2)}) collective-permute-start(bf16[2,4,128,128]{3,2,1,0:T(8,128)(2,1)S(1)} %get-tuple-element.51), channel_id=1, source_target_pairs={{0,2},{1,3},{2,0},{3,1},{4,6},{5,7},{6,4},{7,5},{8,10},{9,11},{10,... | collective-permute-start | bytes 786440 | tf_op jit(solution)/shard_map/ppermute | solution.py:28
  4.9 3.4 %collective-permute-start.2 = (bf16[2,4,128,128]{3,2,1,0:T(8,128)(2,1)S(1)}, bf16[2,4,128,128]{3,2,1,0:T(8,128)(2,1)S(1)}, u32[]{:S(2)}, u32[]{:S(2)}) collective-permute-start(bf16[2,4,128,128]{3,2,1,0:T(8,128)(2,1)S(1)} %get-tuple-element.26.ko), channel_id=1, source_target_pairs={{0,4},{1,5},{2,6},{3,7},{4,8},{5,9},{6,10},{7,11},{8,12},{9,13},{1... | collective-permute-start | bytes 786440 | tf_op jit(solution)/shard_map/ppermute | solution.py:34
  8.3 0.3 copy_bitcast_fusion
  8.6 0.9 %fusion.1 = (bf16[2,8,128,128]{3,2,1,0:T(8,128)(2,1)}, bf16[2,8,128,128]{3,2,1,0:T(8,128)(2,1)S(1)}) fusion(s32[]{:T(128)S(6)} %select_n.31, bf16[1,128,16,128]{3,1,2,0:T(8,128)(2,1)S(1)} %get-tuple-element.58, bf16[1,128,16,128]{3,1,2,0:T(8,128)(2,1)S(1)} %get-tuple-element.57, s32[]{:T(128)S(6)} %select_n.30), kind=kLoop, calls=%fused_computation.9 | loop fusion | flops 524288 | bytes 2097160 | tf_op jit(solution)/shard_map/dynamic_slice | solution.py:44
  9.5 0.5 %collective-permute-start = (bf16[2,8,128,128]{3,2,1,0:T(8,128)(2,1)}, bf16[2,8,128,128]{3,2,1,0:T(8,128)(2,1)S(1)}, u32[]{:S(2)}, u32[]{:S(2)}) collective-permute-start(bf16[2,8,128,128]{3,2,1,0:T(8,128)(2,1)} %get-tuple-element.49), channel_id=1, source_target_pairs={{0,2},{1,3},{2,0},{3,1},{4,6},{5,7},{6,4},{7,5},{8,10},{9,11},{10,... | collective-permute-start | bytes 1572872 | tf_op jit(solution)/shard_map/ppermute | solution.py:28
  10.1 1.1 %collective-permute-done.1.xo = bf16[2,4,128,128]{3,2,1,0:T(8,128)(2,1)S(1)} collective-permute-done((bf16[2,4,128,128]{3,2,1,0:T(8,128)(2,1)S(1)}, bf16[2,4,128,128]{3,2,1,0:T(8,128)(2,1)S(1)}, u32[]{:S(2)}, u32[]{:S(2)}) %collective-permute-start.1) | collective-permute-done | bytes 262176 | tf_op jit(solution)/shard_map/ppermute | solution.py:28
  11.2 3.7 %collective-permute-start.5 = (bf16[2,4,128,128]{3,2,1,0:T(8,128)(2,1)S(1)}, bf16[2,4,128,128]{3,2,1,0:T(8,128)(2,1)S(1)}, u32[]{:S(2)}, u32[]{:S(2)}) collective-permute-start(bf16[2,4,128,128]{3,2,1,0:T(8,128)(2,1)S(1)} %collective-permute-done.1.xo), channel_id=1, source_target_pairs={{0,4},{1,5},{2,6},{3,7},{4,8},{5,9},{6,10},{7,11},{8,12},{9,13},{1... | collective-permute-start | bytes 786440 | tf_op jit(solution)/shard_map/ppermute | solution.py:34
  14.9 0.0 collective-permute-done.2.k1
  14.9 0.1 collective-permute-start.4
  15.0 0.5 collective-permute-start.3
  15.5 0.1 collective-permute-start.6
  15.5 4.0 %collective-permute-done.5.k2 = bf16[2,4,128,128]{3,2,1,0:T(8,128)(2,1)S(1)} collective-permute-done((bf16[2,4,128,128]{3,2,1,0:T(8,128)(2,1)S(1)}, bf16[2,4,128,128]{3,2,1,0:T(8,128)(2,1)S(1)}, u32[]{:S(2)}, u32[]{:S(2)}) %collective-permute-start.5) | collective-permute-done | bytes 262176 | tf_op jit(solution)/shard_map/ppermute | solution.py:34
  19.5 0.0 collective-permute-start.7
  19.5 0.1 pad_add_fusion.place
  19.6 0.0 collective-permute-done.4.mxo
  19.6 0.0 collective-permute-done.3.mko
  19.6 3.2 %collective-permute-done.sent_q = bf16[2,8,128,128]{3,2,1,0:T(8,128)(2,1)S(1)} collective-permute-done((bf16[2,8,128,128]{3,2,1,0:T(8,128)(2,1)}, bf16[2,8,128,128]{3,2,1,0:T(8,128)(2,1)S(1)}, u32[]{:S(2)}, u32[]{:S(2)}) %collective-permute-start) | collective-permute-done | bytes 524320 | tf_op jit(solution)/shard_map/ppermute | solution.py:28
  22.8 0.0 collective-permute-done.7.mk2
  22.9 2.9 %window_grads.2 = (bf16[4,128,128]{2,1,0:T(8,128)(2,1)S(1)}, bf16[4,128,128]{2,1,0:T(8,128)(2,1)S(1)}, f32[2,2,2,128,128]{4,3,2,1,0:T(8,128)S(1)}, bf16[2,2,2,12...) custom-call(s32[3]{0:T(128)S(1)} %pad_add_fusion.place, ...), custom_call_target="tpu_custom_call" | custom-call | flops 1 | bytes 1 | tf_op jit(solution)/shard_map/window_grads/pallas_call | solution.py:170
  25.8 0.1 collective-permute-start.8
  25.9 2.9 %window_grads.3 = (bf16[8,128,128]{2,1,0:T(8,128)(2,1)S(1)}, bf16[8,128,128]{2,1,0:T(8,128)(2,1)S(1)}, f32[2,2,2,128,128]{4,3,2,1,0:T(8,128)S(1)}, bf16[2,2,2,12...) custom-call(s32[3]{0:T(128)S(1)} %pad_add_fusion.place, ...), custom_call_target="tpu_custom_call" | custom-call | flops 1 | bytes 1 | tf_op jit(solution)/shard_map/window_grads/pallas_call | solution.py:170
  28.8 0.6 %collective-permute-start.10 = (bf16[2,2,2,128,128]{4,3,2,1,0:T(8,128)(2,1)S(1)}, bf16[2,2,2,128,128]{4,3,2,1,0:T(8,128)(2,1)S(1)}, u32[]{:S(2)}, u32[]{:S(2)}) collective-permute-start(bf16[2,2,2,128,128]{4,3,2,1,0:T(8,128)(2,1)S(1)} %get-tuple-element.35), channel_id=1, source_target_pairs={{0,1},{1,0},{2,3},{3,2},{4,5},{5,4},{6,7},{7,6},{8,9},{9,8},{10,11... | collective-permute-start | bytes 786440 | tf_op jit(solution)/shard_map/ppermute | solution.py:28
  29.4 0.0 collective-permute-done.8
  29.4 0.1 add_convert_fusion.2
  29.5 1.3 %collective-permute-start.15 = (bf16[2,2,2,128,128]{4,3,2,1,0:T(8,128)(2,1)S(1)}, bf16[2,2,2,128,128]{4,3,2,1,0:T(8,128)(2,1)S(1)}, u32[]{:S(2)}, u32[]{:S(2)}) collective-permute-start(bf16[2,2,2,128,128]{4,3,2,1,0:T(8,128)(2,1)S(1)} %add_convert_fusion.2), channel_id=1, source_target_pairs={{4,0},{5,1},{6,2},{7,3},{8,4},{9,5},{10,6},{11,7},{12,8},{13,9},{1... | collective-permute-start | bytes 786440 | tf_op jit(solution)/shard_map/ppermute | solution.py:34
  30.8 0.1 collective-permute-start.14
  30.8 1.4 %collective-permute-start.9 = (bf16[8,128,128]{2,1,0:T(8,128)(2,1)S(1)}, bf16[8,128,128]{2,1,0:T(8,128)(2,1)S(1)}, u32[]{:S(2)}, u32[]{:S(2)}) collective-permute-start(bf16[8,128,128]{2,1,0:T(8,128)(2,1)S(1)} %get-tuple-element.33), channel_id=1, source_target_pairs={{0,2},{1,3},{2,0},{3,1},{4,6},{5,7},{6,4},{7,5},{8,10},{9,11},{10,... | collective-permute-start | bytes 786440 | tf_op jit(solution)/shard_map/ppermute | solution.py:28
  32.2 0.0 collective-permute-done.10
  32.2 0.1 add_convert_fusion.1
  32.3 1.3 %collective-permute-start.13 = (bf16[2,2,128,128]{3,2,1,0:T(8,128)(2,1)S(1)}, bf16[2,2,128,128]{3,2,1,0:T(8,128)(2,1)S(1)}, u32[]{:S(2)}, u32[]{:S(2)}) collective-permute-start(bf16[2,2,128,128]{3,2,1,0:T(8,128)(2,1)S(1)} %get-tuple-element.55), channel_id=1, source_target_pairs={{4,0},{5,1},{6,2},{7,3},{8,4},{9,5},{10,6},{11,7},{12,8},{13,9},{1... | collective-permute-start | bytes 393224 | tf_op jit(solution)/shard_map/ppermute | solution.py:34
  33.6 0.2 collective-permute-start.12
  33.9 0.0 collective-permute-done.14
  33.9 1.3 %collective-permute-start.11 = (bf16[2,2,128,128]{3,2,1,0:T(8,128)(2,1)S(1)}, bf16[2,2,128,128]{3,2,1,0:T(8,128)(2,1)S(1)}, u32[]{:S(2)}, u32[]{:S(2)}) collective-permute-start(bf16[2,2,128,128]{3,2,1,0:T(8,128)(2,1)S(1)} %get-tuple-element.56), channel_id=1, source_target_pairs={{4,0},{5,1},{6,2},{7,3},{8,4},{9,5},{10,6},{11,7},{12,8},{13,9},{1... | collective-permute-start | bytes 393224 | tf_op jit(solution)/shard_map/ppermute | solution.py:34
  35.1 5.4 %collective-permute-done.15 = bf16[2,2,2,128,128]{4,3,2,1,0:T(8,128)(2,1)S(1)} collective-permute-done((bf16[2,2,2,128,128]{4,3,2,1,0:T(8,128)(2,1)S(1)}, bf16[2,2,2,128,128]{4,3,2,1,0:T(8,128)(2,1)S(1)}, u32[]{:S(2)}, u32[]{:S(2)}) %collective-permute-start.15) | collective-permute-done | bytes 262176 | tf_op jit(solution)/shard_map/ppermute | solution.py:34
  40.5 0.1 add_convert_fusion
  40.6 1.4 %collective-permute-start.17 = (bf16[2,2,128,128]{3,2,1,0:T(8,128)(2,1)S(1)}, bf16[2,2,128,128]{3,2,1,0:T(8,128)(2,1)S(1)}, u32[]{:S(2)}, u32[]{:S(2)}) collective-permute-start(bf16[2,2,128,128]{3,2,1,0:T(8,128)(2,1)S(1)} %get-tuple-element.46), channel_id=1, source_target_pairs={{0,2},{1,3},{2,0},{3,1},{4,6},{5,7},{6,4},{7,5},{8,10},{9,11},{10,... | collective-permute-start | bytes 393224 | tf_op jit(solution)/shard_map/ppermute | solution.py:28
  42.0 1.3 %collective-permute-done.13 = bf16[2,2,128,128]{3,2,1,0:T(8,128)(2,1)S(1)} collective-permute-done((bf16[2,2,128,128]{3,2,1,0:T(8,128)(2,1)S(1)}, bf16[2,2,128,128]{3,2,1,0:T(8,128)(2,1)S(1)}, u32[]{:S(2)}, u32[]{:S(2)}) %collective-permute-start.13) | collective-permute-done | bytes 131104 | tf_op jit(solution)/shard_map/ppermute | solution.py:34
  43.3 0.0 collective-permute-done.12
  43.4 1.4 %collective-permute-start.16 = (bf16[2,2,128,128]{3,2,1,0:T(8,128)(2,1)S(1)}, bf16[2,2,128,128]{3,2,1,0:T(8,128)(2,1)S(1)}, u32[]{:S(2)}, u32[]{:S(2)}) collective-permute-start(bf16[2,2,128,128]{3,2,1,0:T(8,128)(2,1)S(1)} %fusion.9), channel_id=1, source_target_pairs={{0,2},{1,3},{2,0},{3,1},{4,6},{5,7},{6,4},{7,5},{8,10},{9,11},{10,... | collective-permute-start | bytes 393224 | tf_op jit(solution)/shard_map/ppermute | solution.py:28
  44.8 0.4 collective-permute-done.11.refs_2_
  45.2 1.9 %join_heads.2 = bf16[128,16,128]{2,1,0:T(8,128)(2,1)} custom-call(s32[3]{0:T(128)S(1)} %pad_add_fusion.place, bf16[8,128,128]{2,1,0:T(8,128)(2,1)S(1)} %collective-permute-done.9.refs_0_, bf16[8,128,128]{2,1,0:T(8,128)(2,1)S(1)} %get-tuple-element.37.refs_1_), custom_call_target="tpu_custom_call" | custom-call | tf_op jit(solution)/shard_map/join_heads/pallas_call | solution.py:211
  47.1 0.0 collective-permute-done.17.refs_1_
  47.2 1.3 %collective-permute-done.16.refs_0_ = bf16[2,2,128,128]{3,2,1,0:T(8,128)(2,1)S(1)} collective-permute-done((bf16[2,2,128,128]{3,2,1,0:T(8,128)(2,1)S(1)}, bf16[2,2,128,128]{3,2,1,0:T(8,128)(2,1)S(1)}, u32[]{:S(2)}, u32[]{:S(2)}) %collective-permute-start.16) | collective-permute-done | bytes 131104 | tf_op jit(solution)/shard_map/ppermute | solution.py:28
  48.5 1.6 %join_heads.3 = (bf16[128,8,128]{2,1,0:T(8,128)(2,1)}, bf16[128,8,128]{2,1,0:T(8,128)(2,1)}) custom-call(s32[3]{0:T(128)S(1)} %pad_add_fusion.place, bf16[2,2,128,128]{3,2,1,0:T(8,128)(2,1)S(1)} %collective-permute-done.16.refs_0_, bf16[2,2,128,128]{3,2,1,0:T(8,128)(2,1)S(1)} %collective-permute-done.17.refs_1_, ...), custom_call_target="tpu_custom_call" | custom-call | tf_op jit(solution)/shard_map/join_heads/pallas_call | solution.py:211
  (9 shorter events, 0.1 us)
Async XLA Ops:
  1.8 6.5 %copy-start = (bf16[128,16,128]{2,1,0:T(8,128)(2,1)S(1)}, bf16[128,16,128]{2,1,0:T(8,128)(2,1)}, u32[]{:S(2)}) copy-start(bf16[128,16,128]{2,1,0:T(8,128)(2,1)} %param.7) | copy-start | bytes 1572868
  1.8 6.5 %copy-start.1 = (bf16[128,16,128]{2,1,0:T(8,128)(2,1)S(1)}, bf16[128,16,128]{2,1,0:T(8,128)(2,1)}, u32[]{:S(2)}) copy-start(bf16[128,16,128]{2,1,0:T(8,128)(2,1)} %param.4) | copy-start | bytes 1572868
  1.9 9.3 %collective-permute-start.1 = (bf16[2,4,128,128]{3,2,1,0:T(8,128)(2,1)S(1)}, bf16[2,4,128,128]{3,2,1,0:T(8,128)(2,1)S(1)}, u32[]{:S(2)}, u32[]{:S(2)}) collective-permute-start(bf16[2,4,128,128]{3,2,1,0:T(8,128)(2,1)S(1)} %get-tuple-element.51), channel_id=1, source_target_pairs={{0,2},{1,3},{2,0},{3,1},{4,6},{5,7},{6,4},{7,5},{8,10},{9,11},{10,... | collective-permute-start | bytes 786440 | tf_op jit(solution)/shard_map/ppermute | solution.py:28
  4.9 10.0 %collective-permute-start.2 = (bf16[2,4,128,128]{3,2,1,0:T(8,128)(2,1)S(1)}, bf16[2,4,128,128]{3,2,1,0:T(8,128)(2,1)S(1)}, u32[]{:S(2)}, u32[]{:S(2)}) collective-permute-start(bf16[2,4,128,128]{3,2,1,0:T(8,128)(2,1)S(1)} %get-tuple-element.26.ko), channel_id=1, source_target_pairs={{0,4},{1,5},{2,6},{3,7},{4,8},{5,9},{6,10},{7,11},{8,12},{9,13},{1... | collective-permute-start | bytes 786440 | tf_op jit(solution)/shard_map/ppermute | solution.py:34
  9.5 13.3 %collective-permute-start = (bf16[2,8,128,128]{3,2,1,0:T(8,128)(2,1)}, bf16[2,8,128,128]{3,2,1,0:T(8,128)(2,1)S(1)}, u32[]{:S(2)}, u32[]{:S(2)}) collective-permute-start(bf16[2,8,128,128]{3,2,1,0:T(8,128)(2,1)} %get-tuple-element.49), channel_id=1, source_target_pairs={{0,2},{1,3},{2,0},{3,1},{4,6},{5,7},{6,4},{7,5},{8,10},{9,11},{10,... | collective-permute-start | bytes 1572872 | tf_op jit(solution)/shard_map/ppermute | solution.py:28
  11.2 8.3 %collective-permute-start.5 = (bf16[2,4,128,128]{3,2,1,0:T(8,128)(2,1)S(1)}, bf16[2,4,128,128]{3,2,1,0:T(8,128)(2,1)S(1)}, u32[]{:S(2)}, u32[]{:S(2)}) collective-permute-start(bf16[2,4,128,128]{3,2,1,0:T(8,128)(2,1)S(1)} %collective-permute-done.1.xo), channel_id=1, source_target_pairs={{0,4},{1,5},{2,6},{3,7},{4,8},{5,9},{6,10},{7,11},{8,12},{9,13},{1... | collective-permute-start | bytes 786440 | tf_op jit(solution)/shard_map/ppermute | solution.py:34
  14.9 4.7 %collective-permute-start.4 = (bf16[2,4,128,128]{3,2,1,0:T(8,128)(2,1)S(1)}, bf16[2,4,128,128]{3,2,1,0:T(8,128)(2,1)S(1)}, u32[]{:S(2)}, u32[]{:S(2)}) collective-permute-start(bf16[2,4,128,128]{3,2,1,0:T(8,128)(2,1)S(1)} %collective-permute-done.1.xo), channel_id=1, source_target_pairs={{0,1},{1,0},{2,3},{3,2},{4,5},{5,4},{6,7},{7,6},{8,9},{9,8},{10,11... | collective-permute-start | bytes 786440 | tf_op jit(solution)/shard_map/ppermute | solution.py:28
  15.0 4.7 %collective-permute-start.3 = (bf16[2,4,128,128]{3,2,1,0:T(8,128)(2,1)S(1)}, bf16[2,4,128,128]{3,2,1,0:T(8,128)(2,1)S(1)}, u32[]{:S(2)}, u32[]{:S(2)}) collective-permute-start(bf16[2,4,128,128]{3,2,1,0:T(8,128)(2,1)S(1)} %get-tuple-element.26.ko), channel_id=1, source_target_pairs={{0,1},{1,0},{2,3},{3,2},{4,5},{5,4},{6,7},{7,6},{8,9},{9,8},{10,11... | collective-permute-start | bytes 786440 | tf_op jit(solution)/shard_map/ppermute | solution.py:28
  15.5 7.4 %collective-permute-start.6 = (bf16[2,4,128,128]{3,2,1,0:T(8,128)(2,1)S(1)}, bf16[2,4,128,128]{3,2,1,0:T(8,128)(2,1)S(1)}, u32[]{:S(2)}, u32[]{:S(2)}) collective-permute-start(bf16[2,4,128,128]{3,2,1,0:T(8,128)(2,1)S(1)} %collective-permute-done.2.k1), channel_id=1, source_target_pairs={{0,1},{1,0},{2,3},{3,2},{4,5},{5,4},{6,7},{7,6},{8,9},{9,8},{10,11... | collective-permute-start | bytes 786440 | tf_op jit(solution)/shard_map/ppermute | solution.py:28
  19.5 3.3 %collective-permute-start.7 = (bf16[2,4,128,128]{3,2,1,0:T(8,128)(2,1)S(1)}, bf16[2,4,128,128]{3,2,1,0:T(8,128)(2,1)S(1)}, u32[]{:S(2)}, u32[]{:S(2)}) collective-permute-start(bf16[2,4,128,128]{3,2,1,0:T(8,128)(2,1)S(1)} %collective-permute-done.5.k2), channel_id=1, source_target_pairs={{0,1},{1,0},{2,3},{3,2},{4,5},{5,4},{6,7},{7,6},{8,9},{9,8},{10,11... | collective-permute-start | bytes 786440 | tf_op jit(solution)/shard_map/ppermute | solution.py:28
  25.8 3.6 %collective-permute-start.8 = (bf16[2,2,2,128,128]{4,3,2,1,0:T(8,128)(2,1)S(1)}, bf16[2,2,2,128,128]{4,3,2,1,0:T(8,128)(2,1)S(1)}, u32[]{:S(2)}, u32[]{:S(2)}) collective-permute-start(bf16[2,2,2,128,128]{4,3,2,1,0:T(8,128)(2,1)S(1)} %get-tuple-element.32), channel_id=1, source_target_pairs={{0,1},{1,0},{2,3},{3,2},{4,5},{5,4},{6,7},{7,6},{8,9},{9,8},{10,11... | collective-permute-start | bytes 786440 | tf_op jit(solution)/shard_map/ppermute | solution.py:28
  28.8 3.4 %collective-permute-start.10 = (bf16[2,2,2,128,128]{4,3,2,1,0:T(8,128)(2,1)S(1)}, bf16[2,2,2,128,128]{4,3,2,1,0:T(8,128)(2,1)S(1)}, u32[]{:S(2)}, u32[]{:S(2)}) collective-permute-start(bf16[2,2,2,128,128]{4,3,2,1,0:T(8,128)(2,1)S(1)} %get-tuple-element.35), channel_id=1, source_target_pairs={{0,1},{1,0},{2,3},{3,2},{4,5},{5,4},{6,7},{7,6},{8,9},{9,8},{10,11... | collective-permute-start | bytes 786440 | tf_op jit(solution)/shard_map/ppermute | solution.py:28
  29.5 11.1 %collective-permute-start.15 = (bf16[2,2,2,128,128]{4,3,2,1,0:T(8,128)(2,1)S(1)}, bf16[2,2,2,128,128]{4,3,2,1,0:T(8,128)(2,1)S(1)}, u32[]{:S(2)}, u32[]{:S(2)}) collective-permute-start(bf16[2,2,2,128,128]{4,3,2,1,0:T(8,128)(2,1)S(1)} %add_convert_fusion.2), channel_id=1, source_target_pairs={{4,0},{5,1},{6,2},{7,3},{8,4},{9,5},{10,6},{11,7},{12,8},{13,9},{1... | collective-permute-start | bytes 786440 | tf_op jit(solution)/shard_map/ppermute | solution.py:34
  30.8 3.1 %collective-permute-start.14 = (bf16[2,2,2,128,128]{4,3,2,1,0:T(8,128)(2,1)S(1)}, bf16[2,2,2,128,128]{4,3,2,1,0:T(8,128)(2,1)S(1)}, u32[]{:S(2)}, u32[]{:S(2)}) collective-permute-start(bf16[2,2,2,128,128]{4,3,2,1,0:T(8,128)(2,1)S(1)} %get-tuple-element.43), channel_id=1, source_target_pairs={{0,1},{1,0},{2,3},{3,2},{4,5},{5,4},{6,7},{7,6},{8,9},{9,8},{10,11... | collective-permute-start | bytes 786440 | tf_op jit(solution)/shard_map/ppermute | solution.py:28
  30.8 9.8 %collective-permute-start.9 = (bf16[8,128,128]{2,1,0:T(8,128)(2,1)S(1)}, bf16[8,128,128]{2,1,0:T(8,128)(2,1)S(1)}, u32[]{:S(2)}, u32[]{:S(2)}) collective-permute-start(bf16[8,128,128]{2,1,0:T(8,128)(2,1)S(1)} %get-tuple-element.33), channel_id=1, source_target_pairs={{0,2},{1,3},{2,0},{3,1},{4,6},{5,7},{6,4},{7,5},{8,10},{9,11},{10,... | collective-permute-start | bytes 786440 | tf_op jit(solution)/shard_map/ppermute | solution.py:28
  32.3 11.0 %collective-permute-start.13 = (bf16[2,2,128,128]{3,2,1,0:T(8,128)(2,1)S(1)}, bf16[2,2,128,128]{3,2,1,0:T(8,128)(2,1)S(1)}, u32[]{:S(2)}, u32[]{:S(2)}) collective-permute-start(bf16[2,2,128,128]{3,2,1,0:T(8,128)(2,1)S(1)} %get-tuple-element.55), channel_id=1, source_target_pairs={{4,0},{5,1},{6,2},{7,3},{8,4},{9,5},{10,6},{11,7},{12,8},{13,9},{1... | collective-permute-start | bytes 393224 | tf_op jit(solution)/shard_map/ppermute | solution.py:34
  33.6 9.7 %collective-permute-start.12 = (bf16[2,2,2,128,128]{4,3,2,1,0:T(8,128)(2,1)S(1)}, bf16[2,2,2,128,128]{4,3,2,1,0:T(8,128)(2,1)S(1)}, u32[]{:S(2)}, u32[]{:S(2)}) collective-permute-start(bf16[2,2,2,128,128]{4,3,2,1,0:T(8,128)(2,1)S(1)} %get-tuple-element.40), channel_id=1, source_target_pairs={{0,1},{1,0},{2,3},{3,2},{4,5},{5,4},{6,7},{7,6},{8,9},{9,8},{10,11... | collective-permute-start | bytes 786440 | tf_op jit(solution)/shard_map/ppermute | solution.py:28
  33.9 11.3 %collective-permute-start.11 = (bf16[2,2,128,128]{3,2,1,0:T(8,128)(2,1)S(1)}, bf16[2,2,128,128]{3,2,1,0:T(8,128)(2,1)S(1)}, u32[]{:S(2)}, u32[]{:S(2)}) collective-permute-start(bf16[2,2,128,128]{3,2,1,0:T(8,128)(2,1)S(1)} %get-tuple-element.56), channel_id=1, source_target_pairs={{4,0},{5,1},{6,2},{7,3},{8,4},{9,5},{10,6},{11,7},{12,8},{13,9},{1... | collective-permute-start | bytes 393224 | tf_op jit(solution)/shard_map/ppermute | solution.py:34
  40.6 6.5 %collective-permute-start.17 = (bf16[2,2,128,128]{3,2,1,0:T(8,128)(2,1)S(1)}, bf16[2,2,128,128]{3,2,1,0:T(8,128)(2,1)S(1)}, u32[]{:S(2)}, u32[]{:S(2)}) collective-permute-start(bf16[2,2,128,128]{3,2,1,0:T(8,128)(2,1)S(1)} %get-tuple-element.46), channel_id=1, source_target_pairs={{0,2},{1,3},{2,0},{3,1},{4,6},{5,7},{6,4},{7,5},{8,10},{9,11},{10,... | collective-permute-start | bytes 393224 | tf_op jit(solution)/shard_map/ppermute | solution.py:28
  43.4 5.1 %collective-permute-start.16 = (bf16[2,2,128,128]{3,2,1,0:T(8,128)(2,1)S(1)}, bf16[2,2,128,128]{3,2,1,0:T(8,128)(2,1)S(1)}, u32[]{:S(2)}, u32[]{:S(2)}) collective-permute-start(bf16[2,2,128,128]{3,2,1,0:T(8,128)(2,1)S(1)} %fusion.9), channel_id=1, source_target_pairs={{0,2},{1,3},{2,0},{3,1},{4,6},{5,7},{6,4},{7,5},{8,10},{9,11},{10,... | collective-permute-start | bytes 393224 | tf_op jit(solution)/shard_map/ppermute | solution.py:28
